TPU v7x, 256 devices: a whole 4x4x8 slice. The times are simulated.
256 devices in a mesh: dp: 128 (over z, y, x), frame: 2 (over core).
Axes of the slice: x: 4, y: 4, z: 8, core: 2. Of those that a mesh axis runs over, the one named last changes fastest.
Arguments:
- queries: bfloat16 [131072, 1536], P(('dp', 'frame')), may hold values from -7 to 7
- keys: bfloat16 [131072, 1536], P(('dp', 'frame')), may hold values from -7 to 7
- values: bfloat16 [131072, 1536], P(('dp', 'frame')), may hold values from -6 to 6
- grad_out: bfloat16 [131072, 3072], P(('dp', 'frame')), may hold values from -6 to 6
- out_weight: bfloat16 [1536, 3072], P(('dp', 'frame')), may hold values from -0.109375 to 0.109375
- frame_clip: int32 [128, 8], P('dp'), may hold values from 0 to 3, as said below
- frame_rows: int32 [128, 8], P('dp'), may hold values from 3 to 8
- frame_cols: int32 [128, 8], P('dp'), may hold values from 6 to 16
Outputs:
- grad_queries: bfloat16 [131072, 1536], P(('dp', 'frame'))
- grad_keys: bfloat16 [131072, 1536], P(('dp', 'frame'))
- grad_values: bfloat16 [131072, 1536], P(('dp', 'frame'))
Inputs may be any that keep to these rules, and one draw needn't show every extreme that they name: `frame_clip`: within a group clip numbers never fall. Half of the groups hold a long clip split by frames: frames a to 7 form one clip, with a at most 1, and the frames before a another. The other groups hold short clips, each whole on the frames of one device: the clip number changes between frames 4 - 1 and 4, and once inside each device's frames.
All inputs are finite; a program needn't handle non-finite values.
Results may differ from a plain program's by a relative error of at most 0.015.
Values may be sent and summed in bfloat16 or wider, within the bound.
No kernel may reach another device: no remote copies, remote signals or barrier semaphores. Data moves between devices by JAX's collectives and lax.ppermute only.
A program may use at most 192 MiB of HBM per device.

v0:
```python
import jax
import jax.numpy as jnp
from jax import lax
from jax.sharding import PartitionSpec as P

HEAD_DIM = 128
TILE_H = 8
TILE_W = 16
RADIUS = 3


def lookup(column_table, indices, frame_slots):
    hits = indices[..., None] == frame_slots
    return jnp.sum(jnp.where(hits, column_table, 0), axis=-1)


def window_masks(query_frames, clip_row, rows_row, cols_row):
    frame_total = clip_row.shape[0]
    frame_slots = jnp.arange(frame_total, dtype=jnp.int32)
    offsets = jnp.arange(2 * RADIUS + 1, dtype=jnp.int32) - RADIUS
    key_frames = query_frames[:, None] + offsets[None, :]
    inside = (key_frames >= 0) & (key_frames < frame_total)
    key_clip = lookup(clip_row, key_frames, frame_slots)
    query_clip = lookup(clip_row, query_frames, frame_slots)
    same_clip = inside & (key_clip == query_clip[:, None])
    cells = jnp.arange(TILE_H * TILE_W, dtype=jnp.int32)
    row_of = cells // TILE_W
    col_of = cells % TILE_W
    nearby = (jnp.abs(row_of[:, None] - row_of[None, :]) <= RADIUS) & (
        jnp.abs(col_of[:, None] - col_of[None, :]) <= RADIUS
    )
    key_rows = lookup(rows_row, key_frames, frame_slots)
    key_cols = lookup(cols_row, key_frames, frame_slots)
    key_valid = (
        inside[:, :, None]
        & (row_of[None, None, :] < key_rows[:, :, None])
        & (col_of[None, None, :] < key_cols[:, :, None])
    )
    allowed = same_clip[:, None, :, None] & nearby[None, :, None, :] & key_valid[:, None, :, :]
    selfpair = (offsets == 0)[None, None, :, None] & (cells[:, None] == cells[None, :])[
        None, :, None, :
    ]
    allowed = allowed | selfpair
    query_rows = lookup(rows_row, query_frames, frame_slots)
    query_cols = lookup(cols_row, query_frames, frame_slots)
    query_valid = (row_of[None, :] < query_rows[:, None]) & (col_of[None, :] < query_cols[:, None])
    return (allowed, query_valid)


def one_head(query_head, grad_head, pair_head, allowed):
    frame_count = query_head.shape[0]
    reach_len = 2 * RADIUS + 1
    key_window = jnp.stack(
        [pair_head[0, offset : offset + frame_count] for offset in range(reach_len)], axis=1
    )
    value_window = jnp.stack(
        [pair_head[1, offset : offset + frame_count] for offset in range(reach_len)], axis=1
    )
    scale = 1.0 / HEAD_DIM**0.5
    scores = (
        jnp.einsum("fid,fojd->fioj", query_head, key_window, preferred_element_type=jnp.float32)
        * scale
    )
    scores = jnp.where(allowed, scores, -jnp.inf)
    row_top = jnp.max(scores, axis=(2, 3), keepdims=True)
    probs = jnp.exp(scores - row_top)
    probs = probs / jnp.sum(probs, axis=(2, 3), keepdims=True)
    probs_low = probs.astype(jnp.bfloat16)
    grad_probs = jnp.einsum(
        "fid,fojd->fioj", grad_head, value_window, preferred_element_type=jnp.float32
    )
    delta = jnp.sum(probs * grad_probs, axis=(2, 3), keepdims=True)
    grad_scores = (scale * probs * (grad_probs - delta)).astype(jnp.bfloat16)
    grad_query = jnp.einsum(
        "fioj,fojd->fid", grad_scores, key_window, preferred_element_type=jnp.float32
    )
    key_terms = jnp.einsum(
        "fioj,fid->fojd", grad_scores, query_head, preferred_element_type=jnp.float32
    )
    value_terms = jnp.einsum(
        "fioj,fid->fojd", probs_low, grad_head, preferred_element_type=jnp.float32
    )
    key_grad = jnp.zeros((frame_count + 2 * RADIUS,) + key_terms.shape[2:], jnp.float32)
    value_grad = jnp.zeros((frame_count + 2 * RADIUS,) + key_terms.shape[2:], jnp.float32)
    for offset in range(reach_len):
        key_grad = key_grad.at[offset : offset + frame_count].add(key_terms[:, offset])
        value_grad = value_grad.at[offset : offset + frame_count].add(value_terms[:, offset])
    return (grad_query, jnp.stack([key_grad, value_grad]))


def on_device(queries, keys, values, grad_out, out_weight, frame_clip, frame_rows, frame_cols):
    tile = TILE_H * TILE_W
    width = queries.shape[1]
    frame_count = queries.shape[0] // tile
    position = lax.axis_index("frame")
    grad_attn = lax.dot_general(
        grad_out,
        lax.all_gather(out_weight, ("dp", "frame"), axis=0, tiled=True),
        (((1,), (1,)), ((), ())),
        preferred_element_type=jnp.float32,
    )
    query_frames = position * frame_count + jnp.arange(frame_count, dtype=jnp.int32)
    allowed, query_valid = window_masks(query_frames, frame_clip[0], frame_rows[0], frame_cols[0])
    grad_attn = grad_attn.astype(jnp.bfloat16) * query_valid.reshape(-1, 1).astype(jnp.bfloat16)
    stacked = jnp.stack([keys, values]).reshape(2, frame_count, tile, width)
    whole = lax.all_gather(stacked, "frame", axis=1, tiled=True)
    whole = jnp.pad(whole, ((0, 0), (RADIUS, RADIUS), (0, 0), (0, 0)))
    padded = lax.dynamic_slice_in_dim(whole, position * frame_count, frame_count + 2 * RADIUS, 1)
    query_tiles = queries.reshape(frame_count, tile, width)
    grad_tiles = grad_attn.reshape(frame_count, tile, width)

    def head_loop(head, carry):
        query_total, pair_total = carry
        start = head * HEAD_DIM
        query_head = lax.dynamic_slice_in_dim(query_tiles, start, HEAD_DIM, 2)
        grad_head = lax.dynamic_slice_in_dim(grad_tiles, start, HEAD_DIM, 2)
        pair_head = lax.dynamic_slice_in_dim(padded, start, HEAD_DIM, 3)
        query_part, pair_part = one_head(query_head, grad_head, pair_head, allowed)
        query_total = lax.dynamic_update_slice_in_dim(query_total, query_part, start, 2)
        pair_total = lax.dynamic_update_slice_in_dim(pair_total, pair_part, start, 3)
        return (query_total, pair_total)

    query_init = jnp.zeros((frame_count, tile, width), jnp.float32)
    pair_init = jnp.zeros((2, frame_count + 2 * RADIUS, tile, width), jnp.float32)
    grad_query, pair_grad = lax.fori_loop(0, width // HEAD_DIM, head_loop, (query_init, pair_init))
    grad_query = grad_query.reshape(frame_count * tile, width)
    group_frames = frame_count * lax.axis_size("frame")
    placed = jnp.zeros((2, group_frames + 2 * RADIUS, tile, width), jnp.float32)
    placed = lax.dynamic_update_slice_in_dim(placed, pair_grad, position * frame_count, 1)
    own_grad = lax.psum_scatter(
        placed[:, RADIUS : RADIUS + group_frames].astype(jnp.bfloat16),
        "frame",
        scatter_dimension=1,
        tiled=True,
    ).astype(jnp.float32)
    own_grad = own_grad.reshape(2, frame_count * tile, width)
    return (
        grad_query.astype(jnp.bfloat16),
        own_grad[0].astype(jnp.bfloat16),
        own_grad[1].astype(jnp.bfloat16),
    )


def solution(mesh):
    in_specs = (
        P(("dp", "frame"), None),
        P(("dp", "frame"), None),
        P(("dp", "frame"), None),
        P(("dp", "frame"), None),
        P(("dp", "frame"), None),
        P("dp", None),
        P("dp", None),
        P("dp", None),
    )
    out_specs = (P(("dp", "frame"), None), P(("dp", "frame"), None), P(("dp", "frame"), None))
    return jax.shard_map(
        on_device, mesh=mesh, in_specs=in_specs, out_specs=out_specs, check_vma=False
    )
```

profile of v0, /device:TPU:1, one launch (start us, length us, event | category | flops | bytes accessed | tf_op | source)
XLA Modules:
  0.0 538.9 jit_solution(3591482957605486706)
XLA Ops:
  7.2 4.0 pad_maximum_fusion
  13.8 24.2 %all-gather.4.cloned.1.call-done = bf16[2,8,128,1536]{3,2,1,0:T(8,128)(2,1)} async-done(((bf16[2,4,128,1536]{3,2,1,0:T(8,128)(2,1)}), bf16[2,8,128,1536]{3,2,1,0:T(8,128)(2,1)}) %all-gather.4.cloned.1.call-update) | async-done | bytes 6291472 | tf_op jit(solution)/shard_map/all_gather | solution.py:106
  38.0 6.9 %pad_dynamic-slice_fusion = bf16[2,10,128,1536]{3,2,1,0:T(8,128)(2,1)} fusion(s32[]{:T(128)S(6)} %select_n.95, bf16[2,8,128,1536]{3,2,1,0:T(8,128)(2,1)} %all-gather.4.cloned.1.call-done), kind=kLoop, calls=%fused_computation.97 | loop fusion | bytes 14155780 | tf_op jit(solution)/shard_map/dynamic_slice | solution.py:108
  44.9 118.5 %all-gather.6.cloned.1.call-done = bf16[256,6,3072]{2,1,0:T(8,128)(2,1)} async-done(((bf16[1,6,3072]{2,1,0:T(8,128)(2,1)}), bf16[256,6,3072]{2,1,0:T(8,128)(2,1)}) %all-gather.6.cloned.1.call-update) | async-done | bytes 9437200 | tf_op jit(solution)/shard_map/all_gather | solution.py:98
  163.5 14.2 %reshape.1206 = bf16[1536,3072]{1,0:T(8,128)(2,1)} reshape(bf16[256,6,3072]{2,1,0:T(8,128)(2,1)} %all-gather.6.cloned.1.call-done) | data formatting | bytes 18874368
  177.6 9.8 %fusion.63 = bf16[512,1536]{1,0:T(8,128)(2,1)} fusion(bf16[512,3072]{1,0:T(8,128)(2,1)S(1)} %copy-done, bf16[1536,3072]{1,0:T(8,128)(2,1)} %reshape.1206, bf16[512]{0:T(512)(128)(2,1)S(1)} %fusion.65), kind=kOutput, calls=%fused_computation.100 | convolution fusion | flops 4833411072 | bytes 14156800 | tf_op jit(solution)/shard_map/dot_general | solution.py:96
  187.5 4.0 broadcast_in_dim.98
  192.7 277.0 %while.33 = (s32[]{:T(128)}, bf16[4,128,1536]{2,1,0:T(8,128)(2,1)}, bf16[2,10,128,1536]{3,2,1,0:T(8,128)(2,1)}, bf16[4,128,1536]{2,1,0:T(8,128)(2,1)}, bf16[2,10...) while((s32[]{:T(128)}, bf16[4,128,1536]{2,1,0:T(8,128)(2,1)}, ...), condition=%wide.region_10.11_spmd.clone, body=%wide.region_6.10_spmd.clone.sunk | while | flops 598014464 | bytes 50878500 | solution.py:125
  199.2 1.7 fusion.125
  207.8 1.5 fusion.134
  211.5 1.3 fusion.136
  222.3 1.7 fusion.125
  230.9 1.5 fusion.134
  234.6 1.3 fusion.136
  245.4 1.8 fusion.125
  254.0 1.5 fusion.134
  257.7 1.3 fusion.136
  268.5 1.8 fusion.125
  277.1 1.5 fusion.134
  280.8 1.3 fusion.136
  291.6 1.7 fusion.125
  300.1 1.5 fusion.134
  303.9 1.3 fusion.136
  314.7 1.7 fusion.125
  323.2 1.5 fusion.134
  327.0 1.3 fusion.136
  337.8 1.8 fusion.125
  346.3 1.5 fusion.134
  350.1 1.3 fusion.136
  360.8 1.8 fusion.125
  369.4 1.5 fusion.134
  373.1 1.3 fusion.136
  383.9 1.7 fusion.125
  392.5 1.5 fusion.134
  396.2 1.3 fusion.136
  407.0 1.7 fusion.125
  415.6 1.5 fusion.134
  419.3 1.3 fusion.136
  430.1 1.8 fusion.125
  438.7 1.5 fusion.134
  442.4 1.3 fusion.136
  453.2 1.8 fusion.125
  461.8 1.5 fusion.134
  469.7 5.4 broadcast_in_dim.107
  475.1 7.1 %constant_dynamic-update-slice_fusion = bf16[2,14,128,1536]{3,2,1,0:T(8,128)(2,1)} fusion(bf16[2,14,128,1536]{3,2,1,0:T(8,128)(2,1)} %broadcast_in_dim.107, bf16[2,10,128,1536]{3,2,1,0:T(8,128)(2,1)} %get-tuple-element.534, s32[]{:T(128)S(6)} %select_n.95), kind=kLoop, calls=%fused_computation.129 | loop fusion | bytes 15728644 | tf_op jit(solution)/shard_map/dynamic_update_slice | solution.py:129
  482.3 5.9 %slice.1087 = bf16[2,8,128,1536]{3,2,1,0:T(8,128)(2,1)} slice(bf16[2,14,128,1536]{3,2,1,0:T(8,128)(2,1)} %constant_dynamic-update-slice_fusion), slice={[0:2], [3:11], [0:128], [0:1536]} | slice | bytes 12582912 | tf_op jit(solution)/shard_map/slice | solution.py:131
  490.3 38.3 %all-reduce.6.cloned.1.call-done = bf16[2,8,128,1536]{3,2,1,0:T(8,128)(2,1)} async-done(((bf16[2,8,128,1536]{3,2,1,0:T(8,128)(2,1)}), bf16[2,8,128,1536]{3,2,1,0:T(8,128)(2,1)}) %all-reduce.6.cloned.1.call-update) | async-done | bytes 6291472
  528.6 3.7 constant_dynamic-slice_fusion.1
  (518 shorter events, 226.9 us)
Async XLA Ops:
  7.2 170.5 %copy-start = (bf16[512,3072]{1,0:T(8,128)(2,1)S(1)}, bf16[512,3072]{1,0:T(8,128)(2,1)}, u32[]{:S(2)}) copy-start(bf16[512,3072]{1,0:T(8,128)(2,1)} %param.41) | copy-start | bytes 9437188
  7.2 30.9 %all-gather.4.cloned.1.call-start = ((), (), s32[]{:S(2)}) async-start(), calls=%async_computation | async-start | bytes 9437184 | tf_op jit(solution)/shard_map/all_gather | solution.py:106
  11.2 0.9 copy-start.4
  11.2 0.9 copy-start.5
  11.2 0.9 copy-start.6
  11.3 152.2 %all-gather.6.cloned.1.call-start = ((), (), s32[]{:S(2)}) async-start(), calls=%async_computation.1 | async-start | bytes 12632064 | tf_op jit(solution)/shard_map/all_gather | solution.py:98
  12.0 516.6 %all-reduce.6.cloned.1.call-start = ((), (), s32[]{:S(2)}) async-start(), calls=%async_computation.2 | async-start | bytes 12582912
  199.2 1.8 copy-start.2
  213.3 1.3 copy-start.3
  222.3 1.8 copy-start.2
  236.4 1.3 copy-start.3
  245.4 1.8 copy-start.2
  259.5 1.3 copy-start.3
  268.5 1.8 copy-start.2
  282.6 1.3 copy-start.3
  291.6 1.8 copy-start.2
  305.7 1.3 copy-start.3
  314.7 1.8 copy-start.2
  328.7 1.3 copy-start.3
  337.7 1.8 copy-start.2
  351.8 1.3 copy-start.3
  360.8 1.8 copy-start.2
  374.9 1.3 copy-start.3
  383.9 1.8 copy-start.2
  398.0 1.3 copy-start.3
  407.0 1.8 copy-start.2
  421.1 1.3 copy-start.3
  430.1 1.8 copy-start.2
  444.2 1.3 copy-start.3
  453.2 1.8 copy-start.2
  467.3 1.3 copy-start.3
  488.2 0.7 copy-start.7
  489.5 42.8 %copy-start.1 = (bf16[512,3072]{1,0:T(8,128)(2,1)S(1)}, bf16[512,3072]{1,0:T(8,128)(2,1)}, u32[]{:S(2)}) copy-start(bf16[512,3072]{1,0:T(8,128)(2,1)} %param.41) | copy-start | bytes 9437188
Sparse Core Ops, SparseCore 0:
  11.4 26.6 all-gather.3
  41.8 121.6 all-gather.5
  488.4 40.1 all-reduce.5
where the time goes:
time: 544 us; the launch traced here: 539 us
  local copies, waits for them, and re-layouts  212 us (39%)
  waiting for transfers between devices  182 us (33%)
  matrix products  93.1 us (17%)
  other arithmetic  35.2 us (6%)
  between operations  14.6 us (3%)
    while x216, local copies, waits for them, and re-layouts  138 us
    all_gather x1, waiting for transfers between devices, on_device(): lax.all_gather(out_weight, ('dp', 'frame'), axis=0, tiled=True)  119 us
    unnamed x4, waiting for transfers between devices  39 us
    all_gather x1, waiting for transfers between devices, on_device(): whole = lax.all_gather(stacked, 'frame', axis=1, tiled=True)  24.2 us
    dot_general x12, matrix products, one_head(): jnp.einsum('fid,fojd->fioj', query_head, key_window, preferred_element_ty...  21 us
    dot_general x12, matrix products, one_head(): jnp.einsum('fid,fojd->fioj', grad_head, value_window, preferred_element_t...  17.6 us
    dot_general x12, matrix products, one_head(): jnp.einsum('fioj,fid->fojd', probs_low, grad_head, preferred_element_type...  15.6 us
    unnamed x15, local copies, waits for them, and re-layouts  15.5 us
  transfers between devices with their start and end apart: 3, of which 3 were waited for; matrix products, arithmetic and copies ran while one was open for 2% of the time, Pallas kernels for 0%

commit v1 on v0

v1 whole, which is shorter than its diff:
```python
import jax
import jax.numpy as jnp
from jax import lax
from jax.experimental import pallas as pl
from jax.experimental.pallas import tpu as pltpu
from jax.sharding import PartitionSpec as P

HEAD_DIM = 128
TILE_W = 16
TILE = 128
RADIUS = 3
FRAMES = 8
LOCAL = 512
GROUP = 1024
HALF = 768
WIDTH = 1536
DIM = 3072
PAIR = 2 * TILE
SCALE = 1.0 / HEAD_DIM**0.5
LOG2E = 1.4426950408889634

FIRST_KEY = (0, 0, 1, 3)
KEY_COUNT = (5, 7, 7, 5)
OFFSET = (0, 5, 12, 19)
SLOTS = 24
KEY_MOST = 7 * TILE
VMEM = 52 * 1024 * 1024

NT = (((1,), (1,)), ((), ()))
NN = (((1,), (0,)), ((), ()))


def dot(lhs, rhs, dims):
    return lax.dot_general(lhs, rhs, dims, preferred_element_type=jnp.float32)


def fill_bias(info, bias):
    key_cell = lax.broadcasted_iota(jnp.int32, (TILE, PAIR), 0)
    lane = lax.broadcasted_iota(jnp.int32, (TILE, PAIR), 1)
    query_cell = lane & (TILE - 1)
    key_row, key_col = key_cell >> 4, key_cell & (TILE_W - 1)
    near = (jnp.abs(key_row - (query_cell >> 4)) <= RADIUS) & (
        jnp.abs(key_col - (query_cell & (TILE_W - 1))) <= RADIUS
    )
    second = lane >= TILE
    for pair in range(4):
        left, right = 2 * pair, 2 * pair + 1
        for slot in range(KEY_COUNT[pair]):
            frame = FIRST_KEY[pair] + slot
            clip = info[1 + frame]
            left_same = (info[1 + left] == clip) & (abs(frame - left) <= RADIUS)
            right_same = (info[1 + right] == clip) & (abs(frame - right) <= RADIUS)
            linked = jnp.where(
                second, right_same.astype(jnp.int32), left_same.astype(jnp.int32)
            )
            allowed = (
                near
                & (linked > 0)
                & (key_row < info[9 + frame])
                & (key_col < info[17 + frame])
            )
            if frame == left:
                allowed = allowed | (key_cell == lane)
            if frame == right:
                allowed = allowed | (key_cell + TILE == lane)
            start = (OFFSET[pair] + slot) * TILE
            bias[start : start + TILE, :] = jnp.where(allowed, 0.0, -1e30)


def gather_rows(info, scratch, own, other):
    own_start = pl.multiple_of(info[0] * LOCAL, LOCAL)
    other_start = pl.multiple_of((1 - info[0]) * LOCAL, LOCAL)
    scratch[pl.ds(own_start, LOCAL), :] = own
    scratch[pl.ds(other_start, LOCAL), :] = other


def probs_kernel(info, q_own, q_other, k_own, k_other, probs, q_all, k_all, bias, logits):
    @pl.when(pl.program_id(0) == 0)
    def _():
        fill_bias(info, bias)

    gather_rows(info, q_all, q_own[...], q_other[...])
    gather_rows(info, k_all, k_own[...], k_other[...])
    for pair in range(4):
        query = q_all[pair * PAIR : (pair + 1) * PAIR, :]
        top = None
        for slot in range(KEY_COUNT[pair]):
            frame = FIRST_KEY[pair] + slot
            start = (OFFSET[pair] + slot) * TILE
            score = dot(k_all[frame * TILE : (frame + 1) * TILE, :], query, NT)
            score = score * (SCALE * LOG2E) + bias[start : start + TILE, :]
            logits[slot * TILE : (slot + 1) * TILE, :] = score
            part = jnp.max(score.reshape(TILE // 8, 8, PAIR), axis=0)
            top = part if top is None else jnp.maximum(top, part)
        top = jnp.max(top, axis=0, keepdims=True)
        total = None
        for slot in range(KEY_COUNT[pair]):
            rows = slice(slot * TILE, (slot + 1) * TILE)
            weight = jnp.exp2(logits[rows, :] - top)
            logits[rows, :] = weight
            part = jnp.sum(weight.reshape(TILE // 8, 8, PAIR), axis=0)
            total = part if total is None else total + part
        inverse = 1.0 / jnp.sum(total, axis=0, keepdims=True)
        for slot in range(KEY_COUNT[pair]):
            start = (OFFSET[pair] + slot) * TILE
            rows = slice(slot * TILE, (slot + 1) * TILE)
            probs[0, start : start + TILE, :] = (logits[rows, :] * inverse).astype(jnp.bfloat16)


def probs_call(info, q, q_other, k, k_other):
    own = pl.BlockSpec((LOCAL, HEAD_DIM), lambda head, info: (0, info[0] * 6 + head))
    return pl.pallas_call(
        probs_kernel,
        out_shape=jax.ShapeDtypeStruct((6, SLOTS * TILE, PAIR), jnp.bfloat16),
        grid_spec=pltpu.PrefetchScalarGridSpec(
            num_scalar_prefetch=1,
            grid=(6,),
            in_specs=[own] * 4,
            out_specs=pl.BlockSpec((1, SLOTS * TILE, PAIR), lambda head, info: (head, 0, 0)),
            scratch_shapes=[
                pltpu.VMEM((GROUP, HEAD_DIM), jnp.bfloat16),
                pltpu.VMEM((GROUP, HEAD_DIM), jnp.bfloat16),
                pltpu.VMEM((SLOTS * TILE, PAIR), jnp.float32),
                pltpu.VMEM((KEY_MOST, PAIR), jnp.float32),
            ],
        ),
        compiler_params=pltpu.CompilerParams(vmem_limit_bytes=VMEM),
        cost_estimate=pl.CostEstimate(
            flops=6 * 2 * SLOTS * TILE * PAIR * HEAD_DIM,
            bytes_accessed=12_000_000,
            transcendentals=6 * SLOTS * TILE * PAIR,
        ),
        name="probs",
    )(info, q, q_other, k, k_other)


def masked_grad(info, grad_all, start_frame, grad_out, weight):
    grad = dot(grad_out, weight, NT)
    cell = lax.broadcasted_iota(jnp.int32, (TILE, PAIR), 0)
    row, col = cell >> 4, cell & (TILE_W - 1)
    for step in range(4):
        frame = start_frame + step
        valid = (row < info[9 + frame]) & (col < info[17 + frame])
        part = grad[step * TILE : (step + 1) * TILE, :]
        part = jnp.where(valid, part, 0.0).astype(jnp.bfloat16)
        grad_all[pl.ds(pl.multiple_of(frame * TILE, TILE), TILE), :] = part


def grads_kernel(
    info, g_own, g_other, weight, probs, q_own, q_other, k_own, k_other, v_own, v_other,
    dq_own, dk_own, dv_own, dq_send, dk_send, dv_send,
    grad_all, q_all, k_all, v_all, grad_probs, grad_scores, dq_all, dk_all, dv_all,
):
    me = info[0]
    masked_grad(info, grad_all, me * 4, g_own[...], weight[...])
    masked_grad(info, grad_all, (1 - me) * 4, g_other[...], weight[...])
    gather_rows(info, q_all, q_own[...], q_other[...])
    gather_rows(info, k_all, k_own[...], k_other[...])
    gather_rows(info, v_all, v_own[...], v_other[...])
    for head in range(2):
        cols = slice(head * HEAD_DIM, (head + 1) * HEAD_DIM)
        key_turned = k_all[:, cols].T
        dk_all[...] = jnp.zeros_like(dk_all)
        dv_all[...] = jnp.zeros_like(dv_all)
        for pair in range(4):
            first, count = FIRST_KEY[pair], KEY_COUNT[pair]
            key_rows = slice(first * TILE, (first + count) * TILE)
            queries = slice(pair * PAIR, (pair + 1) * PAIR)
            grad = grad_all[queries, cols]
            delta = None
            for slot in range(count):
                frame = first + slot
                start = (OFFSET[pair] + slot) * TILE
                part = dot(v_all[frame * TILE : (frame + 1) * TILE, cols], grad, NT)
                grad_probs[slot * TILE : (slot + 1) * TILE, :] = part
                part = part * probs[head, start : start + TILE, :].astype(jnp.float32)
                part = jnp.sum(part.reshape(TILE // 8, 8, PAIR), axis=0)
                delta = part if delta is None else delta + part
            delta = jnp.sum(delta, axis=0, keepdims=True)
            for slot in range(count):
                rows = slice(slot * TILE, (slot + 1) * TILE)
                start = (OFFSET[pair] + slot) * TILE
                weights = probs[head, start : start + TILE, :].astype(jnp.float32)
                grad_scores[rows, :] = (weights * (grad_probs[rows, :] - delta)).astype(
                    jnp.bfloat16
                )
            scores = grad_scores[: count * TILE, :]
            start = OFFSET[pair] * TILE
            dq_turned = dot(key_turned[:, key_rows], scores, NN) * SCALE
            dq_all[queries, :] = dq_turned.T
            dk_all[key_rows, :] += dot(scores, q_all[queries, cols], NN)
            dv_all[key_rows, :] += dot(
                probs[head, start : start + count * TILE, :], grad, NN
            )
        own = pl.ds(pl.multiple_of(me * LOCAL, LOCAL), LOCAL)
        other = pl.ds(pl.multiple_of((1 - me) * LOCAL, LOCAL), LOCAL)
        dq_own[:, cols] = dq_all[own, :].astype(jnp.bfloat16)
        dk_own[:, cols] = (dk_all[own, :] * SCALE).astype(jnp.bfloat16)
        dv_own[:, cols] = dv_all[own, :].astype(jnp.bfloat16)
        dq_send[:, cols] = dq_all[other, :].astype(jnp.bfloat16)
        dk_send[:, cols] = (dk_all[other, :] * SCALE).astype(jnp.bfloat16)
        dv_send[:, cols] = dv_all[other, :].astype(jnp.bfloat16)


def grads_call(info, grad_out, grad_other, weight, probs, q, q_other, k, k_other, v, v_other):
    whole = pl.BlockSpec((LOCAL, DIM), lambda step, info: (0, 0))
    own = pl.BlockSpec((LOCAL, PAIR), lambda step, info: (0, info[0] * 3 + step))
    sent = pl.BlockSpec((LOCAL, PAIR), lambda step, info: (0, step))
    full = jax.ShapeDtypeStruct((LOCAL, WIDTH), jnp.bfloat16)
    half = jax.ShapeDtypeStruct((LOCAL, HALF), jnp.bfloat16)
    return pl.pallas_call(
        grads_kernel,
        out_shape=[full] * 3 + [half] * 3,
        grid_spec=pltpu.PrefetchScalarGridSpec(
            num_scalar_prefetch=1,
            grid=(3,),
            in_specs=[
                whole,
                whole,
                pl.BlockSpec((PAIR, DIM), lambda step, info: (info[0] * 3 + step, 0)),
                pl.BlockSpec((2, SLOTS * TILE, PAIR), lambda step, info: (step, 0, 0)),
            ]
            + [own] * 6,
            out_specs=[own] * 3 + [sent] * 3,
            scratch_shapes=[
                pltpu.VMEM((GROUP, PAIR), jnp.bfloat16),
                pltpu.VMEM((GROUP, PAIR), jnp.bfloat16),
                pltpu.VMEM((GROUP, PAIR), jnp.bfloat16),
                pltpu.VMEM((GROUP, PAIR), jnp.bfloat16),
                pltpu.VMEM((KEY_MOST, PAIR), jnp.float32),
                pltpu.VMEM((KEY_MOST, PAIR), jnp.bfloat16),
                pltpu.VMEM((GROUP, HEAD_DIM), jnp.float32),
                pltpu.VMEM((GROUP, HEAD_DIM), jnp.float32),
                pltpu.VMEM((GROUP, HEAD_DIM), jnp.float32),
            ],
        ),
        compiler_params=pltpu.CompilerParams(vmem_limit_bytes=VMEM),
        cost_estimate=pl.CostEstimate(
            flops=6 * 8 * SLOTS * TILE * PAIR * HEAD_DIM + 2 * GROUP * HALF * DIM,
            bytes_accessed=30_000_000,
            transcendentals=0,
        ),
        name="grads",
    )(info, grad_out, grad_other, weight, probs, q, q_other, k, k_other, v, v_other)


def merge_kernel(info, *refs):
    arrived, outs, sems = refs[3:6], refs[6:9], refs[9]
    start = pl.multiple_of((1 - info[0]) * HALF, HALF)
    copies = [
        pltpu.make_async_copy(src, dst.at[:, pl.ds(start, HALF)], sems.at[i])
        for i, (src, dst) in enumerate(zip(arrived, outs))
    ]
    for copy in copies:
        copy.start()
    for copy in copies:
        copy.wait()


def merge_call(info, own, arrived):
    full = jax.ShapeDtypeStruct((LOCAL, WIDTH), jnp.bfloat16)
    return pl.pallas_call(
        merge_kernel,
        out_shape=[full] * 3,
        grid_spec=pltpu.PrefetchScalarGridSpec(
            num_scalar_prefetch=1,
            grid=(1,),
            in_specs=[pl.BlockSpec(memory_space=pl.ANY)] * 6,
            out_specs=[pl.BlockSpec(memory_space=pl.ANY)] * 3,
            scratch_shapes=[pltpu.SemaphoreType.DMA((3,))],
        ),
        input_output_aliases={1: 0, 2: 1, 3: 2},
        name="merge",
    )(info, *own, *arrived)


def swap(value):
    return lax.ppermute(value, "frame", [(0, 1), (1, 0)])


def on_device(queries, keys, values, grad_out, out_weight, frame_clip, frame_rows, frame_cols):
    me = lax.axis_index("frame").astype(jnp.int32)
    info = jnp.concatenate([me.reshape(1), frame_clip[0], frame_rows[0], frame_cols[0]])
    weight = lax.all_gather(out_weight, ("dp", "frame"), axis=0, tiled=True)
    q_other, k_other, v_other, g_other = (swap(x) for x in (queries, keys, values, grad_out))
    probs = probs_call(info, queries, q_other, keys, k_other)
    outs = grads_call(
        info, grad_out, g_other, weight, probs, queries, q_other, keys, k_other, values, v_other
    )
    return tuple(merge_call(info, outs[:3], [swap(x) for x in outs[3:]]))


def solution(mesh):
    split = P(("dp", "frame"), None)
    table = P("dp", None)
    return jax.shard_map(
        on_device,
        mesh=mesh,
        in_specs=(split,) * 5 + (table,) * 3,
        out_specs=(split,) * 3,
        check_vma=False,
    )
```

time: 544 us -> 266 us (0.49)
  local copies, waits for them, and re-layouts: 212 us -> 17.7 us
  Pallas kernels: 0 us -> 114 us
  matrix products: 93.1 us -> 0 us
  waiting for transfers between devices: 182 us -> 114 us
  other arithmetic: 35.2 us -> 0.76 us
    while x216 -> x0, local copies, waits for them, and re-layouts: 138 us -> none
    pallas_call x0 -> x3, Pallas kernels: none -> 114 us  [the longest x1 73.3 us: merge_call(): pl.pallas_call(merge_kernel, out_shape=[full] * 3, grid_spec=pltpu.Prefet...]
    dot_general x61 -> x0, matrix products: 93.1 us -> none  [the longest x12 21 us: one_head(): jnp.einsum('fid,fojd->fioj', query_head, key_window, preferred_element_ty...]
    all_gather x2 -> x1, waiting for transfers between devices: 143 us -> 98.6 us  [on_device(): weight = lax.all_gather(out_weight, ('dp', 'frame'), axis=0, tiled=True)]
    unnamed x4 -> x1, waiting for transfers between devices: 39 us -> 0.68 us
    another operation x24 -> x0, local copies, waits for them, and re-layouts: 22.4 us -> none  [the longest x12 11.2 us: one_head(): jnp.stack([pair_head[1, offset:offset + frame_count] for offset in range(...]
    ppermute x0 -> x7, waiting for transfers between devices: none -> 14.7 us  [swap(): return lax.ppermute(value, 'frame', [(0, 1), (1, 0)])]
    dynamic_update_slice x12 -> x0, other arithmetic: 12.6 us -> none  [head_loop(): lax.dynamic_update_slice_in_dim(pair_total, pair_part, start, 3)]
  transfers between devices with their start and end apart: 3 -> 8, of which waited for: 3 -> 6; matrix products, arithmetic and copies ran while one was open for 2% -> 6% of each run, Pallas kernels for 0% -> 5%
where the time goes in v1:
time: 266 us; the launch traced here: 265 us
  waiting for transfers between devices  114 us (43%)
  Pallas kernels  114 us (43%)
  local copies, waits for them, and re-layouts  17.7 us (7%)
  between operations  14.1 us (5%)
  starting transfers between devices  4.8 us (2%)
    all_gather x1, waiting for transfers between devices, on_device(): weight = lax.all_gather(out_weight, ('dp', 'frame'), axis=0, tiled=True)  98.6 us
    pallas_call x1, Pallas kernels, merge_call(): pl.pallas_call(merge_kernel, out_shape=[full] * 3, grid_spec=pltpu.Prefet...  73.3 us
    pallas_call x1, Pallas kernels, grads_call(): pl.pallas_call(grads_kernel, out_shape=[full] * 3 + [half] * 3, grid_spec...  28.7 us
    unnamed x15, local copies, waits for them, and re-layouts  17.7 us
    ppermute x7, waiting for transfers between devices, swap(): return lax.ppermute(value, 'frame', [(0, 1), (1, 0)])  14.7 us
    pallas_call x1, Pallas kernels, probs_call(): pl.pallas_call(probs_kernel, out_shape=jax.ShapeDtypeStruct((6, SLOTS * T...  12.2 us
  transfers between devices with their start and end apart: 8, of which 6 were waited for; matrix products, arithmetic and copies ran while one was open for 6% of the time, Pallas kernels for 5%

profile of v1, /device:TPU:1, one launch (start us, length us, event | category | flops | bytes accessed | tf_op | source)
XLA Modules:
  0.0 265.5 jit_solution(2379165911065622995)
XLA Ops:
  7.2 0.0 all-gather.3.cloned.1.call-start
  7.2 0.7 all-gather.3.cloned.1.call-update
  7.9 3.3 %collective-permute-start = (bf16[512,3072]{1,0:T(8,128)(2,1)}, bf16[512,3072]{1,0:T(8,128)(2,1)}, u32[]{:S(2)}, u32[]{:S(2)}) collective-permute-start(bf16[512,3072]{1,0:T(8,128)(2,1)} %g_own.1), channel_id=1, source_target_pairs={{0,1},{1,0},{2,3},{3,2},{4,5},{5,4},{6,7},{7,6},{8,9},{9,8},{10,11... | collective-permute-start | bytes 9437192 | tf_op jit(solution)/shard_map/ppermute | solution.py:278
  11.2 0.1 collective-permute-start.1
  11.3 0.4 collective-permute-start.2
  11.7 0.1 collective-permute-start.3
  11.8 0.8 pad_add_fusion.info
  12.6 0.0 copy-start.1
  12.6 8.5 %collective-permute-done.1.q_other = bf16[512,1536]{1,0:T(8,128)(2,1)S(1)} collective-permute-done((bf16[512,1536]{1,0:T(8,128)(2,1)}, bf16[512,1536]{1,0:T(8,128)(2,1)S(1)}, u32[]{:S(2)}, u32[]{:S(2)}) %collective-permute-start.1) | collective-permute-done | bytes 1572896 | tf_op jit(solution)/shard_map/ppermute | solution.py:278
  21.1 0.0 copy-start.2
  21.1 2.2 collective-permute-done.2.k_other
  23.3 0.0 copy-done.2
  23.3 0.0 copy-start.3
  23.3 1.1 copy-done.3
  24.5 0.0 copy-start
  24.5 1.4 copy-done
  25.9 12.2 %probs.1 = bf16[6,3072,256]{2,1,0:T(8,128)(2,1)} custom-call(s32[25]{0:T(128)S(1)} %pad_add_fusion.info, bf16[512,1536]{1,0:T(8,128)(2,1)S(1)} %copy-done, bf16[512,1536]{1,0:T(8,128)(2,1)} %copy-done.2, bf16[512,1536]{1,0:T(8,128)(2,1)} %k_own.3, bf16[512,1536]{1,0:T(8,128)(2,1)} %copy-done.3), custom_call_target="tpu_custom_call" | custom-call | flops 1207959552 | bytes 12000000 | tf_op jit(solution)/shard_map/probs/pallas_call | solution.py:112
  38.1 98.6 %all-gather.3.cloned.1.call-done = bf16[256,6,3072]{2,1,0:T(8,128)(2,1)} async-done(((bf16[1,6,3072]{2,1,0:T(8,128)(2,1)}), bf16[256,6,3072]{2,1,0:T(8,128)(2,1)}) %all-gather.3.cloned.1.call-update) | async-done | bytes 9437200 | tf_op jit(solution)/shard_map/all_gather | solution.py:284
  136.6 14.2 %reshape.11.weight = bf16[1536,3072]{1,0:T(8,128)(2,1)} reshape(bf16[256,6,3072]{2,1,0:T(8,128)(2,1)} %all-gather.3.cloned.1.call-done) | data formatting | bytes 18874368
  150.8 0.0 collective-permute-done.3.v_other
  150.8 0.0 collective-permute-done.g_other
  150.8 0.0 copy-done.1
  150.8 28.7 %grads.1 = (bf16[512,1536]{1,0:T(8,128)(2,1)}, bf16[512,1536]{1,0:T(8,128)(2,1)}, bf16[512,1536]{1,0:T(8,128)(2,1)}, bf16[512,768]{1,0:T(8,128)(2,1)S(1)}, bf16[...) custom-call(s32[25]{0:T(128)S(1)} %pad_add_fusion.info, bf16[512,3072]{1,0:T(8,128)(2,1)} %g_own.1, ...), custom_call_target="tpu_custom_call" | custom-call | flops 9663676416 | bytes 30000000 | tf_op jit(solution)/shard_map/grads/pallas_call | solution.py:211
  179.6 0.3 collective-permute-start.4
  179.9 0.3 collective-permute-start.5
  180.2 0.2 collective-permute-start.6
  180.4 1.5 collective-permute-done.4.refs_3_
  182.0 0.0 copy-start.4
  182.0 2.2 collective-permute-done.5.refs_4_
  184.2 0.0 copy-start.5
  184.2 0.2 collective-permute-done.6.refs_5_
  184.4 0.0 copy-start.6
  184.4 0.0 copy-done.4
  184.4 0.7 copy-done.5
  185.1 0.3 copy-done.6
  185.3 73.3 %merge.1 = (bf16[512,1536]{1,0:T(8,128)(2,1)}, bf16[512,1536]{1,0:T(8,128)(2,1)}, bf16[512,1536]{1,0:T(8,128)(2,1)}) custom-call(s32[25]{0:T(128)} %copy-done.1, bf16[512,1536]{1,0:T(8,128)(2,1)} %get-tuple-element.9.refs_0_, bf16[512,1536]{1,0:T(8,128)(2,1)} %get-tuple-element.10.refs_1_, ...), custom_call_target="tpu_custom_call", output_to_operand_aliasing={{0}: (1, {}), {1}: (2, {}), {2}: (3, {})} | custom-call | tf_op jit(solution)/shard_map/merge/pallas_call | solution.py:262
Async XLA Ops:
  7.2 129.5 %all-gather.3.cloned.1.call-start = ((), (), s32[]{:S(2)}) async-start(), calls=%async_computation | async-start | bytes 12632064 | tf_op jit(solution)/shard_map/all_gather | solution.py:284
  7.9 142.9 %collective-permute-start = (bf16[512,3072]{1,0:T(8,128)(2,1)}, bf16[512,3072]{1,0:T(8,128)(2,1)}, u32[]{:S(2)}, u32[]{:S(2)}) collective-permute-start(bf16[512,3072]{1,0:T(8,128)(2,1)} %g_own.1), channel_id=1, source_target_pairs={{0,1},{1,0},{2,3},{3,2},{4,5},{5,4},{6,7},{7,6},{8,9},{9,8},{10,11... | collective-permute-start | bytes 9437192 | tf_op jit(solution)/shard_map/ppermute | solution.py:278
  11.2 9.9 %collective-permute-start.1 = (bf16[512,1536]{1,0:T(8,128)(2,1)}, bf16[512,1536]{1,0:T(8,128)(2,1)S(1)}, u32[]{:S(2)}, u32[]{:S(2)}) collective-permute-start(bf16[512,1536]{1,0:T(8,128)(2,1)} %q_own.3), channel_id=1, source_target_pairs={{0,1},{1,0},{2,3},{3,2},{4,5},{5,4},{6,7},{7,6},{8,9},{9,8},{10,11... | collective-permute-start | bytes 4718600 | tf_op jit(solution)/shard_map/ppermute | solution.py:278
  11.3 12.0 %collective-permute-start.2 = (bf16[512,1536]{1,0:T(8,128)(2,1)}, bf16[512,1536]{1,0:T(8,128)(2,1)S(1)}, u32[]{:S(2)}, u32[]{:S(2)}) collective-permute-start(bf16[512,1536]{1,0:T(8,128)(2,1)} %k_own.3), channel_id=1, source_target_pairs={{0,1},{1,0},{2,3},{3,2},{4,5},{5,4},{6,7},{7,6},{8,9},{9,8},{10,11... | collective-permute-start | bytes 4718600 | tf_op jit(solution)/shard_map/ppermute | solution.py:278
  11.7 139.1 %collective-permute-start.3 = (bf16[512,1536]{1,0:T(8,128)(2,1)}, bf16[512,1536]{1,0:T(8,128)(2,1)}, u32[]{:S(2)}, u32[]{:S(2)}) collective-permute-start(bf16[512,1536]{1,0:T(8,128)(2,1)} %v_own.1), channel_id=1, source_target_pairs={{0,1},{1,0},{2,3},{3,2},{4,5},{5,4},{6,7},{7,6},{8,9},{9,8},{10,11... | collective-permute-start | bytes 4718600 | tf_op jit(solution)/shard_map/ppermute | solution.py:278
  12.6 138.2 %copy-start.1 = (s32[25]{0:T(128)}, s32[25]{0:T(128)S(1)}, u32[]{:S(2)}) copy-start(s32[25]{0:T(128)S(1)} %pad_add_fusion.info) | copy-start | bytes 304
  21.1 2.3 copy-start.2
  23.3 1.1 copy-start.3
  24.5 1.4 copy-start
  179.6 2.4 collective-permute-start.4
  179.9 4.3 %collective-permute-start.5 = (bf16[512,768]{1,0:T(8,128)(2,1)S(1)}, bf16[512,768]{1,0:T(8,128)(2,1)S(1)}, u32[]{:S(2)}, u32[]{:S(2)}) collective-permute-start(bf16[512,768]{1,0:T(8,128)(2,1)S(1)} %get-tuple-element.13), channel_id=1, source_target_pairs={{0,1},{1,0},{2,3},{3,2},{4,5},{5,4},{6,7},{7,6},{8,9},{9,8},{10,11... | collective-permute-start | bytes 2359304 | tf_op jit(solution)/shard_map/ppermute | solution.py:278
  180.2 4.2 %collective-permute-start.6 = (bf16[512,768]{1,0:T(8,128)(2,1)}, bf16[512,768]{1,0:T(8,128)(2,1)S(1)}, u32[]{:S(2)}, u32[]{:S(2)}) collective-permute-start(bf16[512,768]{1,0:T(8,128)(2,1)} %get-tuple-element.14), channel_id=1, source_target_pairs={{0,1},{1,0},{2,3},{3,2},{4,5},{5,4},{6,7},{7,6},{8,9},{9,8},{10,11... | collective-permute-start | bytes 2359304 | tf_op jit(solution)/shard_map/ppermute | solution.py:278
  182.0 2.5 copy-start.4
  184.2 0.9 copy-start.5
  184.4 0.9 copy-start.6
Sparse Core Ops, SparseCore 0:
  11.7 124.8 all-gather.2

commit v2 on v1

v2 whole, which is shorter than its diff:
```python
import functools

import jax
import jax.numpy as jnp
import numpy as np
from jax import lax
from jax.experimental import pallas as pl
from jax.experimental.pallas import tpu as pltpu
from jax.sharding import PartitionSpec as P

HEAD_DIM = 128
TILE_W = 16
TILE = 128
RADIUS = 3
FRAMES = 8
LOCAL = 512
GROUP = 1024
HALF = 768
WIDTH = 1536
DIM = 3072
PAIR = 2 * TILE
SCALE = 1.0 / HEAD_DIM**0.5
LOG2E = 1.4426950408889634

FIRST_KEY = (0, 0, 1, 3)
KEY_COUNT = (5, 7, 7, 5)
OFFSET = (0, 5, 12, 19)
SLOTS = 24
KEY_MOST = 7 * TILE
VMEM = 24 * 1024 * 1024

CHUNK = 48
SLAB = 192
NZ, NY, NX = 8, 4, 4
SLOT_SHIFT = (0, 1, 3, 2)
ME, MINE, THEIRS, INNER, ROWS_EARLY, ROWS_LATE = range(6)

NT = (((1,), (1,)), ((), ()))
NN = (((1,), (0,)), ((), ()))


def dot(lhs, rhs, dims):
    return lax.dot_general(lhs, rhs, dims, preferred_element_type=jnp.float32)


def fill_bias(clips, valid_rows, valid_cols, bias):
    key_cell = lax.broadcasted_iota(jnp.int32, (TILE, PAIR), 0)
    lane = lax.broadcasted_iota(jnp.int32, (TILE, PAIR), 1)
    query_cell = lane & (TILE - 1)
    key_row, key_col = key_cell >> 4, key_cell & (TILE_W - 1)
    near = (jnp.abs(key_row - (query_cell >> 4)) <= RADIUS) & (
        jnp.abs(key_col - (query_cell & (TILE_W - 1))) <= RADIUS
    )
    second = lane >= TILE
    for pair in range(4):
        left, right = 2 * pair, 2 * pair + 1
        for slot in range(KEY_COUNT[pair]):
            frame = FIRST_KEY[pair] + slot
            clip = clips[0, frame]
            left_same = (clips[0, left] == clip) & (abs(frame - left) <= RADIUS)
            right_same = (clips[0, right] == clip) & (abs(frame - right) <= RADIUS)
            linked = jnp.where(
                second, right_same.astype(jnp.int32), left_same.astype(jnp.int32)
            )
            allowed = (
                near
                & (linked > 0)
                & (key_row < valid_rows[0, frame])
                & (key_col < valid_cols[0, frame])
            )
            if frame == left:
                allowed = allowed | (key_cell == lane)
            if frame == right:
                allowed = allowed | (key_cell + TILE == lane)
            start = (OFFSET[pair] + slot) * TILE
            bias[start : start + TILE, :] = jnp.where(allowed, 0.0, -1e30)


def gather_rows(info, scratch, own, other):
    own_start = pl.multiple_of(info[ME] * LOCAL, LOCAL)
    other_start = pl.multiple_of((1 - info[ME]) * LOCAL, LOCAL)
    scratch[pl.ds(own_start, LOCAL), :] = own
    scratch[pl.ds(other_start, LOCAL), :] = other


def probs_kernel(
    info, clips, valid_rows, valid_cols, q_own, k_own, q_other, k_other, slab,
    probs, slab_out, q_all, k_all, bias, logits,
):
    @pl.when(pl.program_id(0) == 0)
    def _():
        fill_bias(clips, valid_rows, valid_cols, bias)

    gather_rows(info, q_all, q_own[...], q_other[0])
    gather_rows(info, k_all, k_own[...], k_other[0])
    for pair in range(4):
        query = q_all[pair * PAIR : (pair + 1) * PAIR, :]
        top = None
        for slot in range(KEY_COUNT[pair]):
            frame = FIRST_KEY[pair] + slot
            start = (OFFSET[pair] + slot) * TILE
            score = dot(k_all[frame * TILE : (frame + 1) * TILE, :], query, NT)
            score = score * (SCALE * LOG2E) + bias[start : start + TILE, :]
            logits[slot * TILE : (slot + 1) * TILE, :] = score
            part = jnp.max(score.reshape(TILE // 8, 8, PAIR), axis=0)
            top = part if top is None else jnp.maximum(top, part)
        top = jnp.max(top, axis=0, keepdims=True)
        total = None
        for slot in range(KEY_COUNT[pair]):
            rows = slice(slot * TILE, (slot + 1) * TILE)
            weight = jnp.exp2(logits[rows, :] - top)
            logits[rows, :] = weight
            part = jnp.sum(weight.reshape(TILE // 8, 8, PAIR), axis=0)
            total = part if total is None else total + part
        inverse = 1.0 / jnp.sum(total, axis=0, keepdims=True)
        for slot in range(KEY_COUNT[pair]):
            start = (OFFSET[pair] + slot) * TILE
            rows = slice(slot * TILE, (slot + 1) * TILE)
            probs[0, start : start + TILE, :] = (logits[rows, :] * inverse).astype(jnp.bfloat16)


def probs_call(tables, q, k, others, slab):
    own = pl.BlockSpec((LOCAL, HEAD_DIM), lambda head, info, *_: (0, info[ME] * 6 + head))
    q_other, k_other = (
        pl.BlockSpec(
            (1, LOCAL, HEAD_DIM),
            functools.partial(lambda which, head, *_: (which, 0, head), which),
        )
        for which in range(2)
    )
    return pl.pallas_call(
        probs_kernel,
        out_shape=[
            jax.ShapeDtypeStruct((6, SLOTS * TILE, PAIR), jnp.bfloat16),
            jax.ShapeDtypeStruct(slab.shape, slab.dtype),
        ],
        grid_spec=pltpu.PrefetchScalarGridSpec(
            num_scalar_prefetch=4,
            grid=(6,),
            in_specs=[own, own, q_other, k_other, pl.BlockSpec(memory_space=pl.ANY)],
            out_specs=[
                pl.BlockSpec((1, SLOTS * TILE, PAIR), lambda head, *_: (head, 0, 0)),
                pl.BlockSpec(memory_space=pl.ANY),
            ],
            scratch_shapes=[
                pltpu.VMEM((GROUP, HEAD_DIM), jnp.bfloat16),
                pltpu.VMEM((GROUP, HEAD_DIM), jnp.bfloat16),
                pltpu.VMEM((SLOTS * TILE, PAIR), jnp.float32),
                pltpu.VMEM((KEY_MOST, PAIR), jnp.float32),
            ],
        ),
        compiler_params=pltpu.CompilerParams(vmem_limit_bytes=VMEM),
        cost_estimate=pl.CostEstimate(
            flops=6 * 2 * SLOTS * TILE * PAIR * HEAD_DIM,
            bytes_accessed=12_000_000,
            transcendentals=6 * SLOTS * TILE * PAIR,
        ),
        input_output_aliases={8: 1},
        name="probs",
    )(*tables, q, k, others, others, slab)


def project(info, valid_rows, valid_cols, grad_all, grad_own, grad_other, weight):
    cell = lax.broadcasted_iota(jnp.int32, (TILE, HEAD_DIM), 0)
    row, col = cell >> 4, cell & (TILE_W - 1)
    for begin, grad_out in ((info[ME] * 4, grad_own), ((1 - info[ME]) * 4, grad_other)):
        grad = dot(grad_out[...], weight, NT)
        for step in range(4):
            frame = begin + step
            valid = (row < valid_rows[0, frame]) & (col < valid_cols[0, frame])
            rows = pl.ds(pl.multiple_of(frame * TILE, TILE), TILE)
            for head in range(2):
                part = grad[step * TILE : (step + 1) * TILE, head * TILE : (head + 1) * TILE]
                grad_all[head, rows, :] = jnp.where(valid, part, 0.0).astype(jnp.bfloat16)


def place_weight(info, pieces, refs, weight):
    for (slab, slots), ref in zip(pieces, refs):
        for index, slot in enumerate(slots):
            chunk = lax.rem(info[INNER] + SLOT_SHIFT[slot], 4)
            start = pl.multiple_of(slab * SLAB + chunk * CHUNK, 16)
            weight[pl.ds(start, CHUNK), :] = ref[index]


def grads_kernel(
    pieces, row_slot, aliased, info, clips, valid_rows, valid_cols, *refs
):
    weight_refs, refs = refs[: len(pieces)], refs[len(pieces) + aliased :]
    grad_own, grad_other, probs = refs[:3]
    q_own, k_own, v_own, q_other, k_other, v_other = refs[3:9]
    dq_own, dk_own, dv_own, dq_send, dk_send, dv_send = refs[9:15]
    weight, grad_all, q_all, k_all, v_all, grad_probs, grad_scores = refs[15:22]
    dq_all, dk_all, dv_all = refs[22:]
    me = info[ME]
    step = pl.program_id(0)

    @pl.when(step == 0)
    def _():
        place_weight(info, pieces, weight_refs, weight)

    @pl.when(lax.rem(step, 2) == 0)
    def _():
        start = pl.multiple_of(info[row_slot] + step * HEAD_DIM, 64)
        rows = weight[pl.ds(start, PAIR), :]
        project(info, valid_rows, valid_cols, grad_all, grad_own, grad_other, rows)

    probs = probs.at[0]
    gather_rows(info, q_all, q_own[...], q_other[0])
    gather_rows(info, k_all, k_own[...], k_other[0])
    gather_rows(info, v_all, v_own[...], v_other[0])
    grads = grad_all.at[lax.rem(step, 2)]
    key_turned = k_all[...].T
    dk_all[...] = jnp.zeros_like(dk_all)
    dv_all[...] = jnp.zeros_like(dv_all)
    for pair in range(4):
        first, count = FIRST_KEY[pair], KEY_COUNT[pair]
        key_rows = slice(first * TILE, (first + count) * TILE)
        queries = slice(pair * PAIR, (pair + 1) * PAIR)
        grad = grads[queries, :]
        delta = None
        grad_probs[: count * TILE, :] = dot(v_all[key_rows, :], grad, NT)
        for slot in range(count):
            start = (OFFSET[pair] + slot) * TILE
            part = grad_probs[slot * TILE : (slot + 1) * TILE, :]
            part = part * probs[start : start + TILE, :].astype(jnp.float32)
            part = jnp.sum(part.reshape(TILE // 8, 8, PAIR), axis=0)
            delta = part if delta is None else delta + part
        delta = jnp.sum(delta, axis=0, keepdims=True)
        for slot in range(count):
            rows = slice(slot * TILE, (slot + 1) * TILE)
            start = (OFFSET[pair] + slot) * TILE
            weights = probs[start : start + TILE, :].astype(jnp.float32)
            grad_scores[rows, :] = (weights * (grad_probs[rows, :] - delta)).astype(jnp.bfloat16)
        scores = grad_scores[: count * TILE, :]
        start = OFFSET[pair] * TILE
        dq_turned = dot(key_turned[:, key_rows], scores, NN) * SCALE
        dq_all[queries, :] = dq_turned.T
        dk_all[key_rows, :] += dot(scores, q_all[queries, :], NN)
        dv_all[key_rows, :] += dot(probs[start : start + count * TILE, :], grad, NN)
    own = pl.ds(pl.multiple_of(me * LOCAL, LOCAL), LOCAL)
    other = pl.ds(pl.multiple_of((1 - me) * LOCAL, LOCAL), LOCAL)
    dq_own[...] = dq_all[own, :].astype(jnp.bfloat16)
    dk_own[...] = (dk_all[own, :] * SCALE).astype(jnp.bfloat16)
    dv_own[...] = dv_all[own, :].astype(jnp.bfloat16)
    dq_send[...] = dq_all[other, :].astype(jnp.bfloat16)
    dk_send[...] = (dk_all[other, :] * SCALE).astype(jnp.bfloat16)
    dv_send[...] = dv_all[other, :].astype(jnp.bfloat16)


def grads_call(tables, pieces, earlier, begin, heads, row_slot, tokens, probs):
    def head_at(step, info):
        return lax.rem(info[MINE] + begin + step, 6)

    whole = pl.BlockSpec(memory_space=pltpu.VMEM)
    own = pl.BlockSpec(
        (LOCAL, HEAD_DIM), lambda step, info, *_: (0, info[ME] * 6 + head_at(step, info))
    )
    other = [
        pl.BlockSpec(
            (1, LOCAL, HEAD_DIM),
            functools.partial(
                lambda which, step, info, *_: (which, 0, head_at(step, info)), which
            ),
        )
        for which in range(3)
    ]
    sent = pl.BlockSpec((LOCAL, HEAD_DIM), lambda step, *_: (0, step))
    anywhere = pl.BlockSpec(memory_space=pl.ANY)
    full = jax.ShapeDtypeStruct((LOCAL, WIDTH), jnp.bfloat16)
    send = jax.ShapeDtypeStruct((LOCAL, heads * HEAD_DIM), jnp.bfloat16)
    arrays = [piece for _, _, piece in pieces]
    layout = tuple((slab, slots) for slab, slots, _ in pieces)
    return pl.pallas_call(
        lambda *refs: grads_kernel(layout, row_slot, len(earlier), *refs),
        out_shape=[full] * 3 + [send] * 3,
        grid_spec=pltpu.PrefetchScalarGridSpec(
            num_scalar_prefetch=4,
            grid=(heads,),
            in_specs=[whole] * len(arrays)
            + [anywhere] * len(earlier)
            + [whole] * 2
            + [
                pl.BlockSpec(
                    (1, SLOTS * TILE, PAIR), lambda step, info, *_: (head_at(step, info), 0, 0)
                )
            ]
            + [own] * 3
            + other,
            out_specs=[own] * 3 + [sent] * 3,
            scratch_shapes=[
                pltpu.VMEM((3 * SLAB, DIM), jnp.bfloat16),
                pltpu.VMEM((2, GROUP, HEAD_DIM), jnp.bfloat16),
                pltpu.VMEM((GROUP, HEAD_DIM), jnp.bfloat16),
                pltpu.VMEM((GROUP, HEAD_DIM), jnp.bfloat16),
                pltpu.VMEM((GROUP, HEAD_DIM), jnp.bfloat16),
                pltpu.VMEM((KEY_MOST, PAIR), jnp.float32),
                pltpu.VMEM((KEY_MOST, PAIR), jnp.bfloat16),
                pltpu.VMEM((GROUP, HEAD_DIM), jnp.float32),
                pltpu.VMEM((GROUP, HEAD_DIM), jnp.float32),
                pltpu.VMEM((GROUP, HEAD_DIM), jnp.float32),
            ],
        ),
        input_output_aliases={4 + len(arrays) + i: i for i in range(len(earlier))},
        compiler_params=pltpu.CompilerParams(vmem_limit_bytes=VMEM),
        cost_estimate=pl.CostEstimate(
            flops=heads * (8 * SLOTS * TILE * PAIR * HEAD_DIM + 2 * GROUP * HEAD_DIM * DIM),
            bytes_accessed=5_000_000 * heads,
            transcendentals=0,
        ),
        name="grads",
    )(*tables, *arrays, *earlier, *tokens[:2], probs, *tokens[2:5], *[tokens[5]] * 3)


def merge_kernel(info, *refs):
    arrived, outs, sems = refs[3:9], refs[9:12], refs[12]
    copies = []
    for begin, heads, parts in ((0, 4, arrived[:3]), (4, 2, arrived[3:])):
        for step in range(heads):
            head = (1 - info[ME]) * 6 + lax.rem(info[THEIRS] + begin + step, 6)
            cols = pl.ds(pl.multiple_of(head * HEAD_DIM, HEAD_DIM), HEAD_DIM)
            for part, out in zip(parts, outs):
                copies.append(
                    pltpu.make_async_copy(
                        part.at[:, step * HEAD_DIM : (step + 1) * HEAD_DIM],
                        out.at[:, cols],
                        sems.at[len(copies)],
                    )
                )
    for copy in copies:
        copy.start()
    for copy in copies:
        copy.wait()


def merge_call(info, own, arrived):
    full = jax.ShapeDtypeStruct((LOCAL, WIDTH), jnp.bfloat16)
    return pl.pallas_call(
        merge_kernel,
        out_shape=[full] * 3,
        grid_spec=pltpu.PrefetchScalarGridSpec(
            num_scalar_prefetch=1,
            grid=(1,),
            in_specs=[pl.BlockSpec(memory_space=pl.ANY)] * 3
            + [pl.BlockSpec(memory_space=pltpu.VMEM)] * 6,
            out_specs=[pl.BlockSpec(memory_space=pl.ANY)] * 3,
            scratch_shapes=[pltpu.SemaphoreType.DMA((18,))],
        ),
        input_output_aliases={1: 0, 2: 1, 3: 2},
        compiler_params=pltpu.CompilerParams(vmem_limit_bytes=VMEM),
        name="merge",
    )(info, *own, *arrived)


def place_table():
    table = np.zeros((NZ * NY * NX, 2, 6), np.int32)
    for dp in range(NZ * NY * NX):
        y, quarter = dp // NX % NY, dp // (NY * NX) % 4
        for core in range(2):
            outer, inner = (y, quarter) if core == 0 else (quarter, y)
            begin = (5, 0, 2, 3)
            rows = 64 * (1 - outer % 2)
            table[dp, core] = (core, begin[outer], begin[inner], inner, rows, 128 + rows)
    return table.reshape(-1, 6)


def place(z, y, x, core):
    return (((z % NZ) * NY + y % NY) * NX + x % NX) * 2 + core


def move(value, source):
    places = [
        (z, y, x, core) for z in range(NZ) for y in range(NY) for x in range(NX) for core in range(2)
    ]
    pairs = [(source(*taker), place(*taker)) for taker in places]
    return lax.ppermute(value, ("dp", "frame"), pairs)


def first_rows(step):
    def source(z, y, x, core):
        inner, outer = (z % 4, y) if core == 0 else (y, z % 4)
        return 128 * core + 8 * (4 * outer + inner) + 2 * x + ((z // 4) ^ step)

    return source


def along(last, distance):
    def source(z, y, x, core):
        if (core == 0) == last:
            return place(z, y + distance, x, core)
        return place(z + distance, y, x, core)

    return source


def line_rows(out_weight, z):
    x_lines = [
        [(z * NY + y) * NX + x for x in range(NX)] for z in range(NZ) for y in range(NY)
    ]
    even, odd = (move(out_weight, first_rows(step)) for step in range(2))
    rows = jnp.stack([jnp.where(z >= 4, odd, even), jnp.where(z >= 4, even, odd)])
    return lax.all_to_all(
        jnp.broadcast_to(rows[None], (NX,) + rows.shape),
        "dp",
        0,
        0,
        axis_index_groups=x_lines,
        tiled=True,
    ).reshape(1, CHUNK, DIM)


def beside_rows(rows):
    return [move(rows, along(False, distance)) for distance in (1, -1, 2)]


def far_slab(after_low, before_high):
    return move(after_low, along(True, 1)), move(before_high, along(True, -1))


def swap(value):
    return lax.ppermute(value, "frame", [(0, 1), (1, 0)])


def other_half(value, me):
    return jnp.where(me == 0, value[:, HALF:], value[:, :HALF])


def on_device(queries, keys, values, grad_out, out_weight, frame_clip, frame_rows, frame_cols):
    me = lax.axis_index("frame")
    dp = lax.axis_index("dp")
    info = lax.dynamic_index_in_dim(jnp.asarray(place_table()), dp * 2 + me, 0, keepdims=False)
    tables = (info, frame_clip, frame_rows, frame_cols)
    g_other = swap(grad_out)
    others = swap(jnp.stack([other_half(x, me) for x in (queries, keys, values)]))
    rows = line_rows(out_weight, dp // (NY * NX))
    slab = jnp.concatenate([rows] + beside_rows(rows))
    after_low, before_high = move(slab[:2], along(True, 1)), move(slab[2:], along(True, -1))
    probs, slab = probs_call(tables, queries, keys, others, slab)
    after_high, before_low = move(slab[2:], along(True, 1)), move(slab[:2], along(True, -1))
    far_low, far_high = far_slab(after_low, before_high)
    tokens = (grad_out, g_other, queries, keys, values, others)
    low, high, both = (0, 1), (2, 3), (0, 1, 2, 3)
    pieces = (
        (0, low, before_low),
        (0, high, before_high),
        (1, both, slab),
        (2, low, after_low),
        (2, high, after_high),
    )
    early = grads_call(tables, pieces, (), 0, 4, ROWS_EARLY, tokens, probs)
    pieces = (
        (0, low, after_low),
        (0, high, after_high),
        (1, low, far_low),
        (1, high, far_high),
        (2, low, before_low),
        (2, high, before_high),
    )
    late = grads_call(tables, pieces, tuple(early[:3]), 4, 2, ROWS_LATE, tokens, probs)
    sent = [swap(x) for x in early[3:]] + [swap(x) for x in late[3:]]
    return tuple(merge_call(info, late[:3], sent))


def solution(mesh):
    split = P(("dp", "frame"), None)
    table = P("dp", None)
    return jax.shard_map(
        on_device,
        mesh=mesh,
        in_specs=(split,) * 5 + (table,) * 3,
        out_specs=(split,) * 3,
        check_vma=False,
    )
```

time: 266 us -> 111 us (0.42)
  waiting for transfers between devices: 114 us -> 13.8 us
  Pallas kernels: 114 us -> 47.1 us
  starting transfers between devices: 4.8 us -> 32.2 us
  local copies, waits for them, and re-layouts: 17.7 us -> 1.22 us
  between operations: 14.1 us -> 1.03 us
  blocking collectives: 0 us -> 10.4 us
  other arithmetic: 0.76 us -> 4.96 us
    all_gather x1 -> x0, waiting for transfers between devices: 98.6 us -> none  [on_device(): weight = lax.all_gather(out_weight, ('dp', 'frame'), axis=0, tiled=True)]
    pallas_call x1, Pallas kernels: 73.3 us -> 2.1 us  [merge_call(): pl.pallas_call(merge_kernel, out_shape=[full] * 3, grid_spec=pltpu.Prefet...]
    ppermute x0 -> x11, starting transfers between devices: none -> 25 us  [move(): return lax.ppermute(value, ('dp', 'frame'), pairs)]
    unnamed x15 -> x14, local copies, waits for them, and re-layouts: 17.7 us -> 0.04 us
    ppermute x7 -> x8, waiting for transfers between devices: 14.7 us -> 2.78 us  [swap(): return lax.ppermute(value, 'frame', [(0, 1), (1, 0)])]
    ppermute x0 -> x11, waiting for transfers between devices: none -> 11 us  [move(): return lax.ppermute(value, ('dp', 'frame'), pairs)]
    all_to_all x0 -> x1, blocking collectives: none -> 10.4 us  [line_rows(): lax.all_to_all(jnp.broadcast_to(rows[None], (NX,) + rows.shape), 'dp', 0,...]
    another operation x0 -> x5, other arithmetic: none -> 4.7 us  [the longest x3 4.67 us: on_device(): jnp.stack([other_half(x, me) for x in (queries, keys, values)])]
  transfers between devices with their start and end apart: 8 -> 19, of which waited for: 6 -> 7; matrix products, arithmetic and copies ran while one was open for 6% -> 6% of each run, Pallas kernels for 5% -> 29%
where the time goes in v2:
time: 111 us
  Pallas kernels  47.1 us (42%)
  starting transfers between devices  32.2 us (29%)
  waiting for transfers between devices  13.8 us (12%)
  blocking collectives  10.4 us (9%)
  other arithmetic  4.96 us (4%)
  local copies, waits for them, and re-layouts  1.22 us (1%)
    pallas_call x2, Pallas kernels, grads_call(): pl.pallas_call(lambda *refs: grads_kernel(layout, row_slot, len(earlier),...  35.2 us
    ppermute x11, starting transfers between devices, move(): return lax.ppermute(value, ('dp', 'frame'), pairs)  25 us
    ppermute x11, waiting for transfers between devices, move(): return lax.ppermute(value, ('dp', 'frame'), pairs)  11 us
    all_to_all x1, blocking collectives, line_rows(): lax.all_to_all(jnp.broadcast_to(rows[None], (NX,) + rows.shape), 'dp', 0,...  10.4 us
    pallas_call x1, Pallas kernels, probs_call(): pl.pallas_call(probs_kernel, out_shape=[jax.ShapeDtypeStruct((6, SLOTS *...  9.89 us
    ppermute x8, starting transfers between devices, swap(): return lax.ppermute(value, 'frame', [(0, 1), (1, 0)])  7.23 us
    another operation x3, other arithmetic, on_device(): jnp.stack([other_half(x, me) for x in (queries, keys, values)])  4.67 us
    ppermute x8, waiting for transfers between devices, swap(): return lax.ppermute(value, 'frame', [(0, 1), (1, 0)])  2.78 us
  transfers between devices with their start and end apart: 19, of which 7 were waited for; matrix products, arithmetic and copies ran while one was open for 6% of the time, Pallas kernels for 29%

profile of v2, /device:TPU:1, one launch (start us, length us, event | category | flops | bytes accessed | tf_op | source)
XLA Modules:
  0.0 110.7 jit_solution(7725743605263415073)
XLA Ops:
  0.6 0.0 copy-start.1
  0.6 10.3 %collective-permute-start.1 = (bf16[6,3072]{1,0:T(8,128)(2,1)}, bf16[6,3072]{1,0:T(8,128)(2,1)S(1)}, u32[]{:S(2)}, u32[]{:S(2)}) collective-permute-start(bf16[6,3072]{1,0:T(8,128)(2,1)} %param.13), channel_id=1, source_target_pairs={{0,0},{128,1},{2,2},{130,3},{4,4},{132,5},{6,6},{134,7},{32,8},{13... | collective-permute-start | bytes 110600 | tf_op jit(solution)/shard_map/ppermute | solution.py:375
  11.0 0.1 collective-permute-start
  11.1 1.5 %select_bitcast_fusion.2 = bf16[1,512,768]{2,1,0:T(8,128)(2,1)S(1)} fusion(bf16[512,1536]{1,0:T(8,128)(2,1)} %refs_16_.1, pred[]{:T(512)S(6)} %eq.2), kind=kLoop, calls=%fused_computation.4 | loop fusion | flops 393216 | bytes 2359297 | tf_op jit(solution)/shard_map/stack | solution.py:433
  12.6 1.5 %select_bitcast_fusion = (bf16[1,512,768]{2,1,0:T(8,128)(2,1)S(1)}, bf16[1,512,768]{2,1,0:T(8,128)(2,1)S(1)}) fusion(bf16[512,1536]{1,0:T(8,128)(2,1)} %refs_18_.1, pred[]{:T(512)S(6)} %eq.2, bf16[512,1536]{1,0:T(8,128)(2,1)S(1)} %copy-done.1), kind=kLoop, calls=%fused_computation.2 | loop fusion | flops 786432 | bytes 4718593 | tf_op jit(solution)/shard_map/stack | solution.py:433
  14.1 1.7 %pad_maximum_fusion = bf16[3,512,768]{2,1,0:T(8,128)(2,1)} fusion(bf16[1,512,768]{2,1,0:T(8,128)(2,1)S(1)} %get-tuple-element.35, bf16[1,512,768]{2,1,0:T(8,128)(2,1)S(1)} %get-tuple-element.36, bf16[1,512,768]{2,1,0:T(8,128)(2,1)S(1)} %select_bitcast_fusion.2), kind=kLoop, calls=%fused_computation | loop fusion | flops 2359296 | bytes 4718592 | tf_op jit(solution)/shard_map/stack | solution.py:433
  15.8 0.4 collective-permute-start.4
  16.2 0.1 collective-permute-start.12
  16.3 1.8 %collective-permute-done = bf16[6,3072]{1,0:T(8,128)(2,1)S(1)} collective-permute-done((bf16[6,3072]{1,0:T(8,128)(2,1)}, bf16[6,3072]{1,0:T(8,128)(2,1)S(1)}, u32[]{:S(2)}, u32[]{:S(2)}) %collective-permute-start) | collective-permute-done | bytes 36896 | tf_op jit(solution)/shard_map/ppermute | solution.py:375
  18.2 0.1 copy.19
  18.3 0.2 broadcast_in_dim.2
  18.4 10.4 %all_to_all.5 = bf16[4,2,6,3072]{3,1,2,0:T(2,128)(2,1)S(1)} all-to-all(bf16[4,2,6,3072]{3,1,2,0:T(2,128)(2,1)S(1)} %broadcast_in_dim.2), channel_id=1, replica_groups={{0,2,4,6},{8,10,12,14},{16,18,20,22},{24,26,28,30},{32,34,36,38},{40,42..., dimensions={0} | all-to-all | bytes 589824 | tf_op jit(solution)/shard_map/all_to_all | solution.py:401
  28.8 0.1 copy.20
  28.9 0.1 reshape.10
  29.0 3.0 %collective-permute-start.6 = (bf16[1,48,3072]{2,1,0:T(8,128)(2,1)S(1)}, bf16[1,48,3072]{2,1,0:T(8,128)(2,1)S(1)}, u32[]{:S(2)}, u32[]{:S(2)}) collective-permute-start(bf16[1,48,3072]{2,1,0:T(8,128)(2,1)S(1)} %reshape.10), channel_id=1, source_target_pairs={{64,0},{17,1},{66,2},{19,3},{68,4},{21,5},{70,6},{23,7},{72,8},{25... | collective-permute-start | bytes 884744 | tf_op jit(solution)/shard_map/ppermute | solution.py:375
  32.0 0.7 dynamic-slice_bitcast_fusion.info.refs_0_
  32.7 2.7 %collective-permute-start.2 = (bf16[1,48,3072]{2,1,0:T(8,128)(2,1)S(1)}, bf16[1,48,3072]{2,1,0:T(8,128)(2,1)S(1)}, u32[]{:S(2)}, u32[]{:S(2)}) collective-permute-start(bf16[1,48,3072]{2,1,0:T(8,128)(2,1)S(1)} %reshape.10), channel_id=1, source_target_pairs={{32,0},{9,1},{34,2},{11,3},{36,4},{13,5},{38,6},{15,7},{40,8},{17,... | collective-permute-start | bytes 884744 | tf_op jit(solution)/shard_map/ppermute | solution.py:375
  35.3 0.9 collective-permute-done.6
  36.2 3.4 %collective-permute-done.5 = bf16[1,48,3072]{2,1,0:T(8,128)(2,1)S(1)} collective-permute-done((bf16[1,48,3072]{2,1,0:T(8,128)(2,1)S(1)}, bf16[1,48,3072]{2,1,0:T(8,128)(2,1)S(1)}, u32[]{:S(2)}, u32[]{:S(2)}) %collective-permute-start.5) | collective-permute-done | bytes 294944 | tf_op jit(solution)/shard_map/ppermute | solution.py:375
  39.6 0.1 pad_maximum_fusion.3
  39.7 0.0 copy-start
  39.7 0.0 copy-start.2
  39.7 0.0 copy-start.4
  39.7 0.0 copy-start.5
  39.7 0.0 copy-start.6
  39.7 1.1 collective-permute-start.9
  40.8 0.1 pad_maximum_fusion.2
  40.9 2.4 %collective-permute-start.3 = (bf16[2,48,3072]{2,1,0:T(8,128)(2,1)S(1)}, bf16[2,48,3072]{2,1,0:T(8,128)(2,1)S(1)}, u32[]{:S(2)}, u32[]{:S(2)}) collective-permute-start(bf16[2,48,3072]{2,1,0:T(8,128)(2,1)S(1)} %pad_maximum_fusion.2), channel_id=1, source_target_pairs={{8,0},{33,1},{10,2},{35,3},{12,4},{37,5},{14,6},{39,7},{16,8},{41,... | collective-permute-start | bytes 1769480 | tf_op jit(solution)/shard_map/ppermute | solution.py:375
  43.2 0.1 pad_maximum_fusion.1.slab
  43.4 9.9 %probs.1 = (bf16[6,3072,256]{2,1,0:T(8,128)(2,1)S(1)}, bf16[4,48,3072]{2,1,0:T(8,128)(2,1)S(1)}) custom-call(s32[6]{0:T(128)S(1)} %dynamic-slice_bitcast_fusion.info.refs_0_, s32[1,8]{1,0:T(1,128)S(1)} %copy-done.4, s32[1,8]{1,0:T(1,128)S(1)} %copy-done.5, s32[1,8]{1,0:T(1,128)S(1)} %copy-done.6, ...), custom_call_target="tpu_custom_call", output_to_operand_aliasing={{1}: (8, {})} | custom-call | flops 1207959552 | bytes 12000000 | tf_op jit(solution)/shard_map/probs/pallas_call | solution.py:131
  53.3 0.0 copy-start.3
  53.4 0.1 fusion
  53.4 0.1 collective-permute-start.11
  53.5 2.7 %collective-permute-start.7 = (bf16[2,48,3072]{2,1,0:T(8,128)(2,1)S(1)}, bf16[2,48,3072]{2,1,0:T(8,128)(2,1)S(1)}, u32[]{:S(2)}, u32[]{:S(2)}) collective-permute-start(bf16[2,48,3072]{2,1,0:T(8,128)(2,1)S(1)} %get-tuple-element.32), channel_id=1, source_target_pairs={{8,0},{33,1},{10,2},{35,3},{12,4},{37,5},{14,6},{39,7},{16,8},{41,... | collective-permute-start | bytes 1769480 | tf_op jit(solution)/shard_map/ppermute | solution.py:375
  56.2 2.7 %collective-permute-start.8 = (bf16[2,48,3072]{2,1,0:T(8,128)(2,1)S(1)}, bf16[2,48,3072]{2,1,0:T(8,128)(2,1)S(1)}, u32[]{:S(2)}, u32[]{:S(2)}) collective-permute-start(bf16[2,48,3072]{2,1,0:T(8,128)(2,1)S(1)} %collective-permute-done.3.refs_7_.refs_4_), channel_id=1, source_target_pairs={{8,0},{33,1},{10,2},{35,3},{12,4},{37,5},{14,6},{39,7},{16,8},{41,... | collective-permute-start | bytes 1769480 | tf_op jit(solution)/shard_map/ppermute | solution.py:375
  58.9 4.9 %collective-permute-done.11.refs_4_.refs_8_ = bf16[2,48,3072]{2,1,0:T(8,128)(2,1)S(1)} collective-permute-done((bf16[2,48,3072]{2,1,0:T(8,128)(2,1)S(1)}, bf16[2,48,3072]{2,1,0:T(8,128)(2,1)S(1)}, u32[]{:S(2)}, u32[]{:S(2)}) %collective-permute-start.11) | collective-permute-done | bytes 589856 | tf_op jit(solution)/shard_map/ppermute | solution.py:375
  63.8 22.1 %grads.2 = (bf16[512,1536]{1,0:T(8,128)(2,1)}, bf16[512,1536]{1,0:T(8,128)(2,1)}, bf16[512,1536]{1,0:T(8,128)(2,1)}, bf16[512,512]{1,0:T(8,128)(2,1)S(1)}, bf16[...) custom-call(s32[6]{0:T(128)S(1)} %dynamic-slice_bitcast_fusion.info.refs_0_, s32[1,8]{1,0:T(1,128)S(1)} %copy-done.4, ...), custom_call_target="tpu_custom_call" | custom-call | flops 6442450944 | bytes 20000000 | tf_op jit(solution)/shard_map/grads/pallas_call | solution.py:273
  85.8 13.1 %grads.3 = (bf16[512,1536]{1,0:T(8,128)(2,1)}, bf16[512,1536]{1,0:T(8,128)(2,1)}, bf16[512,1536]{1,0:T(8,128)(2,1)}, bf16[512,256]{1,0:T(8,128)(2,1)S(1)}, bf16[...) custom-call(s32[6]{0:T(128)S(1)} %dynamic-slice_bitcast_fusion.info., ...), custom_call_target="tpu_custom_call", output_to_operand_aliasing={{0}: (10, {}), {1}: (11, {}), {2}: (12, {})} | custom-call | flops 3221225472 | bytes 10000000 | tf_op jit(solution)/shard_map/grads/pallas_call | solution.py:273
  98.9 5.3 %collective-permute-start.16 = (bf16[512,256]{1,0:T(8,128)(2,1)S(1)}, bf16[512,256]{1,0:T(8,128)(2,1)S(1)}, u32[]{:S(2)}, u32[]{:S(2)}) collective-permute-start(bf16[512,256]{1,0:T(8,128)(2,1)S(1)} %get-tuple-element.28), channel_id=1, source_target_pairs={{0,1},{1,0},{2,3},{3,2},{4,5},{5,4},{6,7},{7,6},{8,9},{9,8},{10,11... | collective-permute-start | bytes 786440 | tf_op jit(solution)/shard_map/ppermute | solution.py:420
  104.3 0.0 collective-permute-start.13
  104.3 0.5 collective-permute-start.14
  104.8 0.0 collective-permute-start.15
  104.8 0.5 collective-permute-start.17
  105.3 0.1 collective-permute-done.16.refs_6_
  105.4 0.4 collective-permute-start.18
  105.8 2.2 %collective-permute-done.17.refs_7_ = bf16[512,256]{1,0:T(8,128)(2,1)S(1)} collective-permute-done((bf16[512,256]{1,0:T(8,128)(2,1)S(1)}, bf16[512,256]{1,0:T(8,128)(2,1)S(1)}, u32[]{:S(2)}, u32[]{:S(2)}) %collective-permute-start.17) | collective-permute-done | bytes 262176 | tf_op jit(solution)/shard_map/ppermute | solution.py:420
  108.1 0.4 collective-permute-done.18.refs_8_
  108.4 2.1 %merge.1 = (bf16[512,1536]{1,0:T(8,128)(2,1)}, bf16[512,1536]{1,0:T(8,128)(2,1)}, bf16[512,1536]{1,0:T(8,128)(2,1)}) custom-call(s32[6]{0:T(128)S(1)} %dynamic-slice_bitcast_fusion.info.refs_0_, bf16[512,1536]{1,0:T(8,128)(2,1)} %get-tuple-element.22.refs_0_, ...), custom_call_target="tpu_custom_call", output_to_operand_aliasing={{0}: (1, {}), {1}: (2, {}), {2}: (3, {})} | custom-call | tf_op jit(solution)/shard_map/merge/pallas_call | solution.py:337
  (23 shorter events, 0.1 us)
Async XLA Ops:
  0.6 11.9 %copy-start.1 = (bf16[512,1536]{1,0:T(8,128)(2,1)S(1)}, bf16[512,1536]{1,0:T(8,128)(2,1)}, u32[]{:S(2)}) copy-start(bf16[512,1536]{1,0:T(8,128)(2,1)} %refs_17_.1) | copy-start | bytes 4718596
  0.6 15.7 %collective-permute-start.1 = (bf16[6,3072]{1,0:T(8,128)(2,1)}, bf16[6,3072]{1,0:T(8,128)(2,1)S(1)}, u32[]{:S(2)}, u32[]{:S(2)}) collective-permute-start(bf16[6,3072]{1,0:T(8,128)(2,1)} %param.13), channel_id=1, source_target_pairs={{0,0},{128,1},{2,2},{130,3},{4,4},{132,5},{6,6},{134,7},{32,8},{13... | collective-permute-start | bytes 110600 | tf_op jit(solution)/shard_map/ppermute | solution.py:375
  11.0 7.1 %collective-permute-start = (bf16[6,3072]{1,0:T(8,128)(2,1)}, bf16[6,3072]{1,0:T(8,128)(2,1)S(1)}, u32[]{:S(2)}, u32[]{:S(2)}) collective-permute-start(bf16[6,3072]{1,0:T(8,128)(2,1)} %param.13), channel_id=1, source_target_pairs={{1,0},{129,1},{3,2},{131,3},{5,4},{133,5},{7,6},{135,7},{33,8},{13... | collective-permute-start | bytes 110600 | tf_op jit(solution)/shard_map/ppermute | solution.py:375
  15.8 27.6 %collective-permute-start.4 = (bf16[3,512,768]{2,1,0:T(8,128)(2,1)}, bf16[3,512,768]{2,1,0:T(8,128)(2,1)S(1)}, u32[]{:S(2)}, u32[]{:S(2)}) collective-permute-start(bf16[3,512,768]{2,1,0:T(8,128)(2,1)} %pad_maximum_fusion), channel_id=1, source_target_pairs={{0,1},{1,0},{2,3},{3,2},{4,5},{5,4},{6,7},{7,6},{8,9},{9,8},{10,11... | collective-permute-start | bytes 7077896 | tf_op jit(solution)/shard_map/ppermute | solution.py:420
  16.2 47.6 %collective-permute-start.12 = (bf16[512,3072]{1,0:T(8,128)(2,1)}, bf16[512,3072]{1,0:T(8,128)(2,1)}, u32[]{:S(2)}, u32[]{:S(2)}) collective-permute-start(bf16[512,3072]{1,0:T(8,128)(2,1)} %refs_13_.3), channel_id=1, source_target_pairs={{0,1},{1,0},{2,3},{3,2},{4,5},{5,4},{6,7},{7,6},{8,9},{9,8},{10,11... | collective-permute-start | bytes 9437192 | tf_op jit(solution)/shard_map/ppermute | solution.py:420
  29.0 7.2 %collective-permute-start.6 = (bf16[1,48,3072]{2,1,0:T(8,128)(2,1)S(1)}, bf16[1,48,3072]{2,1,0:T(8,128)(2,1)S(1)}, u32[]{:S(2)}, u32[]{:S(2)}) collective-permute-start(bf16[1,48,3072]{2,1,0:T(8,128)(2,1)S(1)} %reshape.10), channel_id=1, source_target_pairs={{64,0},{17,1},{66,2},{19,3},{68,4},{21,5},{70,6},{23,7},{72,8},{25... | collective-permute-start | bytes 884744 | tf_op jit(solution)/shard_map/ppermute | solution.py:375
  32.0 7.6 %collective-permute-start.5 = (bf16[1,48,3072]{2,1,0:T(8,128)(2,1)S(1)}, bf16[1,48,3072]{2,1,0:T(8,128)(2,1)S(1)}, u32[]{:S(2)}, u32[]{:S(2)}) collective-permute-start(bf16[1,48,3072]{2,1,0:T(8,128)(2,1)S(1)} %reshape.10), channel_id=1, source_target_pairs={{224,0},{25,1},{226,2},{27,3},{228,4},{29,5},{230,6},{31,7},{232,8... | collective-permute-start | bytes 884744 | tf_op jit(solution)/shard_map/ppermute | solution.py:375
  32.7 8.1 %collective-permute-start.2 = (bf16[1,48,3072]{2,1,0:T(8,128)(2,1)S(1)}, bf16[1,48,3072]{2,1,0:T(8,128)(2,1)S(1)}, u32[]{:S(2)}, u32[]{:S(2)}) collective-permute-start(bf16[1,48,3072]{2,1,0:T(8,128)(2,1)S(1)} %reshape.10), channel_id=1, source_target_pairs={{32,0},{9,1},{34,2},{11,3},{36,4},{13,5},{38,6},{15,7},{40,8},{17,... | collective-permute-start | bytes 884744 | tf_op jit(solution)/shard_map/ppermute | solution.py:375
  39.7 3.7 %copy-start = (bf16[512,1536]{1,0:T(8,128)(2,1)S(1)}, bf16[512,1536]{1,0:T(8,128)(2,1)}, u32[]{:S(2)}) copy-start(bf16[512,1536]{1,0:T(8,128)(2,1)} %refs_16_.1) | copy-start | bytes 4718596
  39.7 3.7 %copy-start.2 = (bf16[512,1536]{1,0:T(8,128)(2,1)S(1)}, bf16[512,1536]{1,0:T(8,128)(2,1)}, u32[]{:S(2)}) copy-start(bf16[512,1536]{1,0:T(8,128)(2,1)} %refs_17_.1) | copy-start | bytes 4718596
  39.7 3.7 %copy-start.4 = (s32[1,8]{1,0:T(1,128)S(1)}, s32[1,8]{1,0:T(1,128)}, u32[]{:S(2)}) copy-start(s32[1,8]{1,0:T(1,128)} %refs_1_.3) | copy-start | bytes 100
  39.7 3.7 %copy-start.5 = (s32[1,8]{1,0:T(1,128)S(1)}, s32[1,8]{1,0:T(1,128)}, u32[]{:S(2)}) copy-start(s32[1,8]{1,0:T(1,128)} %refs_2_.3) | copy-start | bytes 100
  39.7 3.7 %copy-start.6 = (s32[1,8]{1,0:T(1,128)S(1)}, s32[1,8]{1,0:T(1,128)}, u32[]{:S(2)}) copy-start(s32[1,8]{1,0:T(1,128)} %refs_3_.3) | copy-start | bytes 100
  39.7 16.5 %collective-permute-start.9 = (bf16[2,48,3072]{2,1,0:T(8,128)(2,1)S(1)}, bf16[2,48,3072]{2,1,0:T(8,128)(2,1)S(1)}, u32[]{:S(2)}, u32[]{:S(2)}) collective-permute-start(bf16[2,48,3072]{2,1,0:T(8,128)(2,1)S(1)} %pad_maximum_fusion.3), channel_id=1, source_target_pairs={{24,0},{225,1},{26,2},{227,3},{28,4},{229,5},{30,6},{231,7},{0,8},... | collective-permute-start | bytes 1769480 | tf_op jit(solution)/shard_map/ppermute | solution.py:375
  40.9 15.3 %collective-permute-start.3 = (bf16[2,48,3072]{2,1,0:T(8,128)(2,1)S(1)}, bf16[2,48,3072]{2,1,0:T(8,128)(2,1)S(1)}, u32[]{:S(2)}, u32[]{:S(2)}) collective-permute-start(bf16[2,48,3072]{2,1,0:T(8,128)(2,1)S(1)} %pad_maximum_fusion.2), channel_id=1, source_target_pairs={{8,0},{33,1},{10,2},{35,3},{12,4},{37,5},{14,6},{39,7},{16,8},{41,... | collective-permute-start | bytes 1769480 | tf_op jit(solution)/shard_map/ppermute | solution.py:375
  53.3 10.4 %copy-start.3 = (bf16[512,1536]{1,0:T(8,128)(2,1)S(1)}, bf16[512,1536]{1,0:T(8,128)(2,1)}, u32[]{:S(2)}) copy-start(bf16[512,1536]{1,0:T(8,128)(2,1)} %refs_18_.1) | copy-start | bytes 4718596
  53.4 10.3 %collective-permute-start.11 = (bf16[2,48,3072]{2,1,0:T(8,128)(2,1)S(1)}, bf16[2,48,3072]{2,1,0:T(8,128)(2,1)S(1)}, u32[]{:S(2)}, u32[]{:S(2)}) collective-permute-start(bf16[2,48,3072]{2,1,0:T(8,128)(2,1)S(1)} %get-tuple-element.31), channel_id=1, source_target_pairs={{24,0},{225,1},{26,2},{227,3},{28,4},{229,5},{30,6},{231,7},{0,8},... | collective-permute-start | bytes 1769480 | tf_op jit(solution)/shard_map/ppermute | solution.py:375
  53.5 10.2 %collective-permute-start.7 = (bf16[2,48,3072]{2,1,0:T(8,128)(2,1)S(1)}, bf16[2,48,3072]{2,1,0:T(8,128)(2,1)S(1)}, u32[]{:S(2)}, u32[]{:S(2)}) collective-permute-start(bf16[2,48,3072]{2,1,0:T(8,128)(2,1)S(1)} %get-tuple-element.32), channel_id=1, source_target_pairs={{8,0},{33,1},{10,2},{35,3},{12,4},{37,5},{14,6},{39,7},{16,8},{41,... | collective-permute-start | bytes 1769480 | tf_op jit(solution)/shard_map/ppermute | solution.py:375
  56.2 29.6 %collective-permute-start.10 = (bf16[2,48,3072]{2,1,0:T(8,128)(2,1)S(1)}, bf16[2,48,3072]{2,1,0:T(8,128)(2,1)S(1)}, u32[]{:S(2)}, u32[]{:S(2)}) collective-permute-start(bf16[2,48,3072]{2,1,0:T(8,128)(2,1)S(1)} %collective-permute-done.9.refs_5_.refs_9_), channel_id=1, source_target_pairs={{24,0},{225,1},{26,2},{227,3},{28,4},{229,5},{30,6},{231,7},{0,8},... | collective-permute-start | bytes 1769480 | tf_op jit(solution)/shard_map/ppermute | solution.py:375
  56.2 29.6 %collective-permute-start.8 = (bf16[2,48,3072]{2,1,0:T(8,128)(2,1)S(1)}, bf16[2,48,3072]{2,1,0:T(8,128)(2,1)S(1)}, u32[]{:S(2)}, u32[]{:S(2)}) collective-permute-start(bf16[2,48,3072]{2,1,0:T(8,128)(2,1)S(1)} %collective-permute-done.3.refs_7_.refs_4_), channel_id=1, source_target_pairs={{8,0},{33,1},{10,2},{35,3},{12,4},{37,5},{14,6},{39,7},{16,8},{41,... | collective-permute-start | bytes 1769480 | tf_op jit(solution)/shard_map/ppermute | solution.py:375
  98.9 6.5 %collective-permute-start.16 = (bf16[512,256]{1,0:T(8,128)(2,1)S(1)}, bf16[512,256]{1,0:T(8,128)(2,1)S(1)}, u32[]{:S(2)}, u32[]{:S(2)}) collective-permute-start(bf16[512,256]{1,0:T(8,128)(2,1)S(1)} %get-tuple-element.28), channel_id=1, source_target_pairs={{0,1},{1,0},{2,3},{3,2},{4,5},{5,4},{6,7},{7,6},{8,9},{9,8},{10,11... | collective-permute-start | bytes 786440 | tf_op jit(solution)/shard_map/ppermute | solution.py:420
  104.3 4.2 %collective-permute-start.13 = (bf16[512,512]{1,0:T(8,128)(2,1)S(1)}, bf16[512,512]{1,0:T(8,128)(2,1)S(1)}, u32[]{:S(2)}, u32[]{:S(2)}) collective-permute-start(bf16[512,512]{1,0:T(8,128)(2,1)S(1)} %get-tuple-element.25), channel_id=1, source_target_pairs={{0,1},{1,0},{2,3},{3,2},{4,5},{5,4},{6,7},{7,6},{8,9},{9,8},{10,11... | collective-permute-start | bytes 1572872 | tf_op jit(solution)/shard_map/ppermute | solution.py:420
  104.3 4.1 %collective-permute-start.14 = (bf16[512,512]{1,0:T(8,128)(2,1)S(1)}, bf16[512,512]{1,0:T(8,128)(2,1)S(1)}, u32[]{:S(2)}, u32[]{:S(2)}) collective-permute-start(bf16[512,512]{1,0:T(8,128)(2,1)S(1)} %get-tuple-element.26), channel_id=1, source_target_pairs={{0,1},{1,0},{2,3},{3,2},{4,5},{5,4},{6,7},{7,6},{8,9},{9,8},{10,11... | collective-permute-start | bytes 1572872 | tf_op jit(solution)/shard_map/ppermute | solution.py:420
  104.8 3.7 %collective-permute-start.15 = (bf16[512,512]{1,0:T(8,128)(2,1)S(1)}, bf16[512,512]{1,0:T(8,128)(2,1)S(1)}, u32[]{:S(2)}, u32[]{:S(2)}) collective-permute-start(bf16[512,512]{1,0:T(8,128)(2,1)S(1)} %get-tuple-element.27), channel_id=1, source_target_pairs={{0,1},{1,0},{2,3},{3,2},{4,5},{5,4},{6,7},{7,6},{8,9},{9,8},{10,11... | collective-permute-start | bytes 1572872 | tf_op jit(solution)/shard_map/ppermute | solution.py:420
  104.8 3.2 %collective-permute-start.17 = (bf16[512,256]{1,0:T(8,128)(2,1)S(1)}, bf16[512,256]{1,0:T(8,128)(2,1)S(1)}, u32[]{:S(2)}, u32[]{:S(2)}) collective-permute-start(bf16[512,256]{1,0:T(8,128)(2,1)S(1)} %get-tuple-element.29), channel_id=1, source_target_pairs={{0,1},{1,0},{2,3},{3,2},{4,5},{5,4},{6,7},{7,6},{8,9},{9,8},{10,11... | collective-permute-start | bytes 786440 | tf_op jit(solution)/shard_map/ppermute | solution.py:420
  105.4 3.0 %collective-permute-start.18 = (bf16[512,256]{1,0:T(8,128)(2,1)S(1)}, bf16[512,256]{1,0:T(8,128)(2,1)S(1)}, u32[]{:S(2)}, u32[]{:S(2)}) collective-permute-start(bf16[512,256]{1,0:T(8,128)(2,1)S(1)} %get-tuple-element.30), channel_id=1, source_target_pairs={{0,1},{1,0},{2,3},{3,2},{4,5},{5,4},{6,7},{7,6},{8,9},{9,8},{10,11... | collective-permute-start | bytes 786440 | tf_op jit(solution)/shard_map/ppermute | solution.py:420

commit v3 on v2

v3 whole, which is shorter than its diff:
```python
import functools

import jax
import jax.numpy as jnp
import numpy as np
from jax import lax
from jax.experimental import pallas as pl
from jax.experimental.pallas import tpu as pltpu
from jax.sharding import PartitionSpec as P

HEAD_DIM = 128
TILE_W = 16
TILE = 128
RADIUS = 3
FRAMES = 8
LOCAL = 512
GROUP = 1024
HALF = 768
WIDTH = 1536
DIM = 3072
PAIR = 2 * TILE
SCALE = 1.0 / HEAD_DIM**0.5
LOG2E = 1.4426950408889634

FIRST_KEY = (0, 0, 1, 3)
KEY_COUNT = (5, 7, 7, 5)
OFFSET = (0, 5, 12, 19)
SLOTS = 24
KEY_MOST = 7 * TILE
VMEM = 26 * 1024 * 1024

CHUNK = 48
SLAB = 192
NZ, NY, NX = 8, 4, 4
SLOT_SHIFT = (0, 1, 3, 2)
ME, MINE, THEIRS, INNER, ROWS_EARLY, ROWS_LATE = range(6)

NT = (((1,), (1,)), ((), ()))
TN = (((0,), (0,)), ((), ()))
NN = (((1,), (0,)), ((), ()))


def dot(lhs, rhs, dims):
    return lax.dot_general(lhs, rhs, dims, preferred_element_type=jnp.float32)


def fill_bias(clips, valid_rows, valid_cols, bias):
    key_cell = lax.broadcasted_iota(jnp.int32, (TILE, PAIR), 0)
    lane = lax.broadcasted_iota(jnp.int32, (TILE, PAIR), 1)
    query_cell = lane & (TILE - 1)
    key_row, key_col = key_cell >> 4, key_cell & (TILE_W - 1)
    near = (jnp.abs(key_row - (query_cell >> 4)) <= RADIUS) & (
        jnp.abs(key_col - (query_cell & (TILE_W - 1))) <= RADIUS
    )
    second = lane >= TILE
    for pair in range(4):
        left, right = 2 * pair, 2 * pair + 1
        for slot in range(KEY_COUNT[pair]):
            frame = FIRST_KEY[pair] + slot
            clip = clips[0, frame]
            left_same = (clips[0, left] == clip) & (abs(frame - left) <= RADIUS)
            right_same = (clips[0, right] == clip) & (abs(frame - right) <= RADIUS)
            linked = jnp.where(
                second, right_same.astype(jnp.int32), left_same.astype(jnp.int32)
            )
            allowed = (
                near
                & (linked > 0)
                & (key_row < valid_rows[0, frame])
                & (key_col < valid_cols[0, frame])
            )
            if frame == left:
                allowed = allowed | (key_cell == lane)
            if frame == right:
                allowed = allowed | (key_cell + TILE == lane)
            start = (OFFSET[pair] + slot) * TILE
            bias[start : start + TILE, :] = jnp.where(allowed, 0.0, -1e30)


def gather_rows(info, scratch, own, other):
    own_start = pl.multiple_of(info[ME] * LOCAL, LOCAL)
    other_start = pl.multiple_of((1 - info[ME]) * LOCAL, LOCAL)
    scratch[pl.ds(own_start, LOCAL), :] = own
    scratch[pl.ds(other_start, LOCAL), :] = other


def probs_kernel(
    info, clips, valid_rows, valid_cols, q_own, k_own, q_other, k_other, slab,
    probs_early, probs_late, slab_out, q_all, k_all, bias, logits_all,
):
    @pl.when(pl.program_id(0) == 0)
    def _():
        fill_bias(clips, valid_rows, valid_cols, bias)

    gather_rows(info, q_all, q_own[...], q_other[0])
    gather_rows(info, k_all, k_own[...], k_other[0])

    def find_logits(pair):
        first, count, offset = FIRST_KEY[pair], KEY_COUNT[pair], OFFSET[pair]
        query = q_all[pair * PAIR : (pair + 1) * PAIR, :]
        score = dot(k_all[first * TILE : (first + count) * TILE, :], query, NT)
        top = None
        for slot in range(count):
            rows = slice(slot * TILE, (slot + 1) * TILE)
            start = (offset + slot) * TILE
            part = score[rows, :] * (SCALE * LOG2E) + bias[start : start + TILE, :]
            logits_all[pair % 2, rows, :] = part
            part = jnp.max(part.reshape(TILE // 8, 8, PAIR), axis=0)
            top = part if top is None else jnp.maximum(top, part)
        return jnp.max(top, axis=0, keepdims=True)

    def find_probs(pair, top, kept):
        count, offset = KEY_COUNT[pair], OFFSET[pair]
        logits = logits_all.at[pair % 2]
        total = None
        for slot in range(count):
            rows = slice(slot * TILE, (slot + 1) * TILE)
            weight = jnp.exp2(logits[rows, :] - top)
            logits[rows, :] = weight
            part = jnp.sum(weight.reshape(TILE // 8, 8, PAIR), axis=0)
            total = part if total is None else total + part
        inverse = 1.0 / jnp.sum(total, axis=0, keepdims=True)
        for slot in range(count):
            rows = slice(slot * TILE, (slot + 1) * TILE)
            start = (offset + slot) * TILE
            kept[start : start + TILE, :] = (logits[rows, :] * inverse).astype(jnp.bfloat16)

    def find_all(kept):
        top = find_logits(0)
        for pair in range(4):
            later = find_logits(pair + 1) if pair < 3 else None
            find_probs(pair, top, kept)
            top = later

    @pl.when(pl.program_id(0) < 4)
    def _():
        find_all(probs_early.at[0])

    @pl.when(pl.program_id(0) >= 4)
    def _():
        find_all(probs_late.at[0])


def probs_call(tables, q, k, others, slab):
    def head_at(step, info):
        return lax.rem(info[MINE] + step, 6)

    def other_block(which):
        return pl.BlockSpec(
            (1, LOCAL, HEAD_DIM), lambda step, info, *_: (which, 0, head_at(step, info))
        )

    own = pl.BlockSpec(
        (LOCAL, HEAD_DIM), lambda step, info, *_: (0, info[ME] * 6 + head_at(step, info))
    )
    block = (1, SLOTS * TILE, PAIR)
    return pl.pallas_call(
        probs_kernel,
        out_shape=[
            jax.ShapeDtypeStruct((4, SLOTS * TILE, PAIR), jnp.bfloat16),
            jax.ShapeDtypeStruct((2, SLOTS * TILE, PAIR), jnp.bfloat16),
            jax.ShapeDtypeStruct(slab.shape, slab.dtype),
        ],
        grid_spec=pltpu.PrefetchScalarGridSpec(
            num_scalar_prefetch=4,
            grid=(6,),
            in_specs=[own, own, other_block(0), other_block(1), pl.BlockSpec(memory_space=pl.ANY)],
            out_specs=[
                pl.BlockSpec(block, lambda step, *_: (jnp.minimum(step, 3), 0, 0)),
                pl.BlockSpec(block, lambda step, *_: (jnp.maximum(step, 4) - 4, 0, 0)),
                pl.BlockSpec(memory_space=pl.ANY),
            ],
            scratch_shapes=[
                pltpu.VMEM((GROUP, HEAD_DIM), jnp.bfloat16),
                pltpu.VMEM((GROUP, HEAD_DIM), jnp.bfloat16),
                pltpu.VMEM((SLOTS * TILE, PAIR), jnp.float32),
                pltpu.VMEM((2, KEY_MOST, PAIR), jnp.float32),
            ],
        ),
        compiler_params=pltpu.CompilerParams(vmem_limit_bytes=VMEM),
        cost_estimate=pl.CostEstimate(
            flops=6 * 2 * SLOTS * TILE * PAIR * HEAD_DIM,
            bytes_accessed=12_000_000,
            transcendentals=6 * SLOTS * TILE * PAIR,
        ),
        input_output_aliases={8: 2},
        name="probs",
    )(*tables, q, k, others, others, slab)


def project(info, valid_rows, valid_cols, grad_all, grad_own, grad_other, weight):
    cell = lax.broadcasted_iota(jnp.int32, (TILE, HEAD_DIM), 0)
    row, col = cell >> 4, cell & (TILE_W - 1)
    for begin, grad_out in ((info[ME] * 4, grad_own), ((1 - info[ME]) * 4, grad_other)):
        grad = dot(grad_out[...], weight, NT)
        for step in range(4):
            frame = begin + step
            valid = (row < valid_rows[0, frame]) & (col < valid_cols[0, frame])
            rows = pl.ds(pl.multiple_of(frame * TILE, TILE), TILE)
            for head in range(2):
                part = grad[step * TILE : (step + 1) * TILE, head * TILE : (head + 1) * TILE]
                grad_all[head, rows, :] = jnp.where(valid, part, 0.0).astype(jnp.bfloat16)


def place_weight(info, pieces, refs, weight):
    for (slab, slots), ref in zip(pieces, refs):
        for index, slot in enumerate(slots):
            chunk = lax.rem(info[INNER] + SLOT_SHIFT[slot], 4)
            start = pl.multiple_of(slab * SLAB + chunk * CHUNK, 16)
            weight[pl.ds(start, CHUNK), :] = ref[index]


def grads_kernel(pieces, row_slot, info, clips, valid_rows, valid_cols, *refs):
    weight_refs, refs = refs[: len(pieces)], refs[len(pieces) :]
    grad_own, grad_other, probs = refs[:3]
    own_heads, other_heads = (refs[3:6], refs[6:9]), (refs[9:12], refs[12:15])
    kept, sent, weight, grad_all, q_all, k_all, v_all, grad_probs_all, grad_scores_all = refs[15:24]
    dq_all, dk_all, dv_all = refs[24:]
    me = info[ME]
    step = pl.program_id(0)
    probs_heads = [probs.at[2 * step + head] for head in range(2)]

    @pl.when(step == 0)
    def _():
        place_weight(info, pieces, weight_refs, weight)

    start = pl.multiple_of(info[row_slot] + step * PAIR, 64)
    rows = weight[pl.ds(start, PAIR), :]
    project(info, valid_rows, valid_cols, grad_all, grad_own, grad_other, rows)
    for head in range(2):
        for scratch, own, other in zip(
            (q_all, k_all, v_all), own_heads[head], other_heads[head]
        ):
            gather_rows(info, scratch.at[head], own[...], other[0])

    def spans(pair):
        first, count = FIRST_KEY[pair], KEY_COUNT[pair]
        key_rows = slice(first * TILE, (first + count) * TILE)
        table_rows = slice(OFFSET[pair] * TILE, (OFFSET[pair] + count) * TILE)
        return key_rows, slice(pair * PAIR, (pair + 1) * PAIR), table_rows, count

    def find_grad_probs(item):
        head, pair = divmod(item, 4)
        key_rows, queries, _, count = spans(pair)
        grad_probs_all[item % 2, : count * TILE, :] = dot(
            v_all[head, key_rows, :], grad_all[head, queries, :], NT
        )

    def find_grad_scores(item):
        head, pair = divmod(item, 4)
        _, _, table_rows, count = spans(pair)
        grad_probs, grad_scores = grad_probs_all.at[item % 2], grad_scores_all.at[item % 2]
        probs = probs_heads[head]
        delta = None
        for slot in range(count):
            rows = slice(slot * TILE, (slot + 1) * TILE)
            start = table_rows.start + slot * TILE
            part = grad_probs[rows, :] * probs[start : start + TILE, :].astype(jnp.float32)
            part = jnp.sum(part.reshape(TILE // 8, 8, PAIR), axis=0)
            delta = part if delta is None else delta + part
        delta = jnp.sum(delta, axis=0, keepdims=True)
        for slot in range(count):
            rows = slice(slot * TILE, (slot + 1) * TILE)
            start = table_rows.start + slot * TILE
            weights = probs[start : start + TILE, :].astype(jnp.float32)
            grad_scores[rows, :] = (weights * (grad_probs[rows, :] - delta)).astype(jnp.bfloat16)

    def add_grads(item):
        head, pair = divmod(item, 4)
        key_rows, queries, table_rows, count = spans(pair)
        scores = grad_scores_all[item % 2, : count * TILE, :]
        dq_all[head, queries, :] = dot(scores, k_all[head, key_rows, :], TN)
        dk_all[head, key_rows, :] += dot(scores, q_all[head, queries, :], NN)
        dv_all[head, key_rows, :] += dot(
            probs_heads[head][table_rows, :], grad_all[head, queries, :], NN
        )

    def hand_over(head):
        cols = slice(head * HEAD_DIM, (head + 1) * HEAD_DIM)
        own = pl.ds(pl.multiple_of(me * LOCAL, LOCAL), LOCAL)
        other = pl.ds(pl.multiple_of((1 - me) * LOCAL, LOCAL), LOCAL)
        for index, (part, scale) in enumerate(((dq_all, SCALE), (dk_all, SCALE), (dv_all, 1.0))):
            kept[index, :, cols] = (part[head, own, :] * scale).astype(jnp.bfloat16)
            sent[index, :, cols] = (part[head, other, :] * scale).astype(jnp.bfloat16)

    dk_all[...] = jnp.zeros_like(dk_all)
    dv_all[...] = jnp.zeros_like(dv_all)
    find_grad_probs(0)
    for item in range(8):
        if item < 7:
            find_grad_probs(item + 1)
        if item > 0:
            add_grads(item - 1)
        find_grad_scores(item)
        if item == 5:
            hand_over(0)
    add_grads(7)
    hand_over(1)


def grads_call(tables, pieces, begin, heads, row_slot, tokens, probs):
    def head_at(parity, step, info):
        return lax.rem(info[MINE] + begin + 2 * step + parity, 6)

    def own_block(parity):
        return pl.BlockSpec(
            (LOCAL, HEAD_DIM),
            lambda step, info, *_: (0, info[ME] * 6 + head_at(parity, step, info)),
        )

    def other_block(parity, which):
        return pl.BlockSpec(
            (1, LOCAL, HEAD_DIM),
            lambda step, info, *_: (which, 0, head_at(parity, step, info)),
        )

    whole = pl.BlockSpec(memory_space=pltpu.VMEM)
    result = jax.ShapeDtypeStruct((3, LOCAL, heads * HEAD_DIM), jnp.bfloat16)
    arrays = [piece for _, _, piece in pieces]
    layout = tuple((slab, slots) for slab, slots, _ in pieces)
    grad_own, grad_other, *own, other = tokens
    return pl.pallas_call(
        functools.partial(grads_kernel, layout, row_slot),
        out_shape=[result] * 2,
        grid_spec=pltpu.PrefetchScalarGridSpec(
            num_scalar_prefetch=4,
            grid=(heads // 2,),
            in_specs=[whole] * (len(arrays) + 3)
            + [own_block(parity) for parity in range(2) for _ in range(3)]
            + [other_block(parity, which) for parity in range(2) for which in range(3)],
            out_specs=[pl.BlockSpec((3, LOCAL, PAIR), lambda step, *_: (0, 0, step))] * 2,
            scratch_shapes=[
                pltpu.VMEM((3 * SLAB, DIM), jnp.bfloat16),
                pltpu.VMEM((2, GROUP, HEAD_DIM), jnp.bfloat16),
                pltpu.VMEM((2, GROUP, HEAD_DIM), jnp.bfloat16),
                pltpu.VMEM((2, GROUP, HEAD_DIM), jnp.bfloat16),
                pltpu.VMEM((2, GROUP, HEAD_DIM), jnp.bfloat16),
                pltpu.VMEM((2, KEY_MOST, PAIR), jnp.float32),
                pltpu.VMEM((2, KEY_MOST, PAIR), jnp.bfloat16),
                pltpu.VMEM((2, GROUP, HEAD_DIM), jnp.float32),
                pltpu.VMEM((2, GROUP, HEAD_DIM), jnp.float32),
                pltpu.VMEM((2, GROUP, HEAD_DIM), jnp.float32),
            ],
        ),
        compiler_params=pltpu.CompilerParams(vmem_limit_bytes=VMEM),
        cost_estimate=pl.CostEstimate(
            flops=heads * (8 * SLOTS * TILE * PAIR * HEAD_DIM + 2 * GROUP * HEAD_DIM * DIM),
            bytes_accessed=5_000_000 * heads,
            transcendentals=0,
        ),
        name="grads",
    )(*tables, *arrays, grad_own, grad_other, probs, *own, *own, *[other] * 6)


def merge_kernel(plan, count, info, *refs):
    parts, outs, sems = refs[count : count + len(plan)], refs[-4:-1], refs[-1]
    copies = []
    for part, (theirs, begin, heads) in zip(parts, plan):
        core, first = (1 - info[ME], info[THEIRS]) if theirs else (info[ME], info[MINE])
        for step in range(heads):
            head = core * 6 + lax.rem(first + begin + step, 6)
            cols = pl.ds(pl.multiple_of(head * HEAD_DIM, HEAD_DIM), HEAD_DIM)
            for index, out in enumerate(outs):
                copies.append(
                    pltpu.make_async_copy(
                        part.at[index, :, step * HEAD_DIM : (step + 1) * HEAD_DIM],
                        out.at[:, cols],
                        sems.at[len(copies)],
                    )
                )
    for copy in copies:
        copy.start()
    for copy in copies:
        copy.wait()


def merge_call(info, earlier, parts):
    full = jax.ShapeDtypeStruct((LOCAL, WIDTH), jnp.bfloat16)
    plan = tuple(part[:3] for part in parts)
    copies = sum(3 * heads for _, _, heads in plan)
    return pl.pallas_call(
        functools.partial(merge_kernel, plan, len(earlier)),
        out_shape=[full] * 3,
        grid_spec=pltpu.PrefetchScalarGridSpec(
            num_scalar_prefetch=1,
            grid=(1,),
            in_specs=[pl.BlockSpec(memory_space=pl.ANY)] * len(earlier)
            + [pl.BlockSpec(memory_space=pltpu.VMEM)] * len(parts),
            out_specs=[pl.BlockSpec(memory_space=pl.ANY)] * 3,
            scratch_shapes=[pltpu.SemaphoreType.DMA((copies,))],
        ),
        input_output_aliases={1 + i: i for i in range(len(earlier))},
        compiler_params=pltpu.CompilerParams(vmem_limit_bytes=VMEM),
        name="merge",
    )(info, *earlier, *[part[3] for part in parts])


def place_table():
    table = np.zeros((NZ * NY * NX, 2, 6), np.int32)
    for dp in range(NZ * NY * NX):
        y, quarter = dp // NX % NY, dp // (NY * NX) % 4
        for core in range(2):
            outer, inner = (y, quarter) if core == 0 else (quarter, y)
            begin = (5, 0, 2, 3)
            rows = 64 * (1 - outer % 2)
            table[dp, core] = (core, begin[outer], begin[inner], inner, rows, 128 + rows)
    return table.reshape(-1, 6)


def place(z, y, x, core):
    return (((z % NZ) * NY + y % NY) * NX + x % NX) * 2 + core


def move(value, source):
    places = [
        (z, y, x, core) for z in range(NZ) for y in range(NY) for x in range(NX) for core in range(2)
    ]
    pairs = [(source(*taker), place(*taker)) for taker in places]
    return lax.ppermute(value, ("dp", "frame"), pairs)


def first_rows(step):
    def source(z, y, x, core):
        inner, outer = (z % 4, y) if core == 0 else (y, z % 4)
        return 128 * core + 8 * (4 * outer + inner) + 2 * x + ((z // 4) ^ step)

    return source


def along(last, distance):
    def source(z, y, x, core):
        if (core == 0) == last:
            return place(z, y + distance, x, core)
        return place(z + distance, y, x, core)

    return source


def line_rows(out_weight, z):
    x_lines = [
        [(z * NY + y) * NX + x for x in range(NX)] for z in range(NZ) for y in range(NY)
    ]
    even, odd = (move(out_weight, first_rows(step)) for step in range(2))
    rows = jnp.stack([jnp.where(z >= 4, odd, even), jnp.where(z >= 4, even, odd)])
    return lax.all_to_all(
        jnp.broadcast_to(rows[None], (NX,) + rows.shape),
        "dp",
        0,
        0,
        axis_index_groups=x_lines,
        tiled=True,
    ).reshape(1, CHUNK, DIM)


def beside_rows(rows):
    return [move(rows, along(False, distance)) for distance in (1, -1, 2)]


def far_slab(after_low, before_high):
    return move(after_low, along(True, 1)), move(before_high, along(True, -1))


def swap(value):
    return lax.ppermute(value, "frame", [(0, 1), (1, 0)])


def other_half(value, me):
    return jnp.where(me == 0, value[:, HALF:], value[:, :HALF])


def on_device(queries, keys, values, grad_out, out_weight, frame_clip, frame_rows, frame_cols):
    me = lax.axis_index("frame")
    dp = lax.axis_index("dp")
    info = lax.dynamic_index_in_dim(jnp.asarray(place_table()), dp * 2 + me, 0, keepdims=False)
    tables = (info, frame_clip, frame_rows, frame_cols)
    g_other = swap(grad_out)
    others = swap(jnp.stack([other_half(x, me) for x in (queries, keys, values)]))
    rows = line_rows(out_weight, dp // (NY * NX))
    slab = jnp.concatenate([rows] + beside_rows(rows))
    after_low, before_high = move(slab[:2], along(True, 1)), move(slab[2:], along(True, -1))
    probs_early, probs_late, slab = probs_call(tables, queries, keys, others, slab)
    after_high, before_low = move(slab[2:], along(True, 1)), move(slab[:2], along(True, -1))
    far_low, far_high = far_slab(after_low, before_high)
    tokens = (grad_out, g_other, queries, keys, values, others)
    low, high, both = (0, 1), (2, 3), (0, 1, 2, 3)
    pieces = (
        (0, low, before_low),
        (0, high, before_high),
        (1, both, slab),
        (2, low, after_low),
        (2, high, after_high),
    )
    kept, sent = grads_call(tables, pieces, 0, 4, ROWS_EARLY, tokens, probs_early)
    arrived = swap(sent)
    pieces = (
        (0, low, after_low),
        (0, high, after_high),
        (1, low, far_low),
        (1, high, far_high),
        (2, low, before_low),
        (2, high, before_high),
    )
    kept_late, sent_late = grads_call(tables, pieces, 4, 2, ROWS_LATE, tokens, probs_late)
    arrived_late = swap(sent_late)
    parts = ((False, 0, 4, kept), (False, 4, 2, kept_late), (True, 0, 4, arrived))
    outs = merge_call(info, (), parts)
    return tuple(merge_call(info, tuple(outs), ((True, 4, 2, arrived_late),)))


def solution(mesh):
    split = P(("dp", "frame"), None)
    table = P("dp", None)
    return jax.shard_map(
        on_device,
        mesh=mesh,
        in_specs=(split,) * 5 + (table,) * 3,
        out_specs=(split,) * 3,
        check_vma=False,
    )
```

time: 111 us -> 106 us (0.955)
  Pallas kernels: 47.1 us -> 40.5 us
  starting transfers between devices: 32.2 us -> 37.5 us
  waiting for transfers between devices: 13.8 us -> 9.83 us
    pallas_call x4 -> x5, Pallas kernels: 47.1 us -> 40.5 us  [the longest x2 26.6 us: grads_call(): pl.pallas_call(functools.partial(grads_kernel, layout, row_slot), out_sha...]
    ppermute x8 -> x4, starting transfers between devices: 7.23 us -> 11.6 us  [swap(): return lax.ppermute(value, 'frame', [(0, 1), (1, 0)])]
    ppermute x8 -> x4, waiting for transfers between devices: 2.78 us -> 0.01 us  [swap(): return lax.ppermute(value, 'frame', [(0, 1), (1, 0)])]
    ppermute x11, waiting for transfers between devices: 11 us -> 9.81 us  [move(): return lax.ppermute(value, ('dp', 'frame'), pairs)]
  transfers between devices with their start and end apart: 19 -> 15, of which waited for: 7 -> 3; matrix products, arithmetic and copies ran while one was open for 6% -> 6% of each run, Pallas kernels for 29% -> 37%
where the time goes in v3:
time: 106 us; the launch traced here: 105 us
  Pallas kernels  40.5 us (38%)
  starting transfers between devices  37.5 us (35%)
  blocking collectives  10.4 us (10%)
  waiting for transfers between devices  9.83 us (9%)
  other arithmetic  4.95 us (5%)
  local copies, waits for them, and re-layouts  1.22 us (1%)
  between operations  1.07 us (1%)
    pallas_call x2, Pallas kernels, grads_call(): pl.pallas_call(functools.partial(grads_kernel, layout, row_slot), out_sha...  26.6 us
    ppermute x11, starting transfers between devices, move(): return lax.ppermute(value, ('dp', 'frame'), pairs)  25.9 us
    ppermute x4, starting transfers between devices, swap(): return lax.ppermute(value, 'frame', [(0, 1), (1, 0)])  11.6 us
    all_to_all x1, blocking collectives, line_rows(): lax.all_to_all(jnp.broadcast_to(rows[None], (NX,) + rows.shape), 'dp', 0,...  10.4 us
    ppermute x11, waiting for transfers between devices, move(): return lax.ppermute(value, ('dp', 'frame'), pairs)  9.81 us
    pallas_call x1, Pallas kernels, probs_call(): pl.pallas_call(probs_kernel, out_shape=[jax.ShapeDtypeStruct((4, SLOTS *...  9.79 us
    another operation x3, other arithmetic, on_device(): jnp.stack([other_half(x, me) for x in (queries, keys, values)])  4.65 us
    pallas_call x2, Pallas kernels, merge_call(): pl.pallas_call(functools.partial(merge_kernel, plan, len(earlier)), out_s...  4.19 us
  transfers between devices with their start and end apart: 15, of which 3 were waited for; matrix products, arithmetic and copies ran while one was open for 6% of the time, Pallas kernels for 37%

profile of v3, /device:TPU:1, one launch (start us, length us, event | category | flops | bytes accessed | tf_op | source)
XLA Modules:
  0.0 105.5 jit_solution(1248823487299831454)
XLA Ops:
  0.6 0.0 copy-start.1
  0.6 3.3 %collective-permute-start.1 = (bf16[6,3072]{1,0:T(8,128)(2,1)}, bf16[6,3072]{1,0:T(8,128)(2,1)S(1)}, u32[]{:S(2)}, u32[]{:S(2)}) collective-permute-start(bf16[6,3072]{1,0:T(8,128)(2,1)} %param.13), channel_id=1, source_target_pairs={{1,0},{129,1},{3,2},{131,3},{5,4},{133,5},{7,6},{135,7},{33,8},{13... | collective-permute-start | bytes 110600 | tf_op jit(solution)/shard_map/ppermute | solution.py:419
  4.0 7.1 %collective-permute-start.2 = (bf16[6,3072]{1,0:T(8,128)(2,1)}, bf16[6,3072]{1,0:T(8,128)(2,1)S(1)}, u32[]{:S(2)}, u32[]{:S(2)}) collective-permute-start(bf16[6,3072]{1,0:T(8,128)(2,1)} %param.13), channel_id=1, source_target_pairs={{0,0},{128,1},{2,2},{130,3},{4,4},{132,5},{6,6},{134,7},{32,8},{13... | collective-permute-start | bytes 110600 | tf_op jit(solution)/shard_map/ppermute | solution.py:419
  11.1 1.5 %select_bitcast_fusion.2 = bf16[1,512,768]{2,1,0:T(8,128)(2,1)S(1)} fusion(bf16[512,1536]{1,0:T(8,128)(2,1)} %refs_12_.3, pred[]{:T(512)S(6)} %eq.2), kind=kLoop, calls=%fused_computation.4 | loop fusion | flops 393216 | bytes 2359297 | tf_op jit(solution)/shard_map/stack | solution.py:477
  12.6 1.5 %select_bitcast_fusion = (bf16[1,512,768]{2,1,0:T(8,128)(2,1)S(1)}, bf16[1,512,768]{2,1,0:T(8,128)(2,1)S(1)}) fusion(bf16[512,1536]{1,0:T(8,128)(2,1)} %refs_14_.1, pred[]{:T(512)S(6)} %eq.2, bf16[512,1536]{1,0:T(8,128)(2,1)S(1)} %copy-done.1), kind=kLoop, calls=%fused_computation.2 | loop fusion | flops 786432 | bytes 4718593 | tf_op jit(solution)/shard_map/stack | solution.py:477
  14.1 1.7 %pad_maximum_fusion = bf16[3,512,768]{2,1,0:T(8,128)(2,1)} fusion(bf16[1,512,768]{2,1,0:T(8,128)(2,1)S(1)} %get-tuple-element.27, bf16[1,512,768]{2,1,0:T(8,128)(2,1)S(1)} %get-tuple-element.28, bf16[1,512,768]{2,1,0:T(8,128)(2,1)S(1)} %select_bitcast_fusion.2), kind=kLoop, calls=%fused_computation | loop fusion | flops 2359296 | bytes 4718592 | tf_op jit(solution)/shard_map/stack | solution.py:477
  15.8 0.5 collective-permute-start.10
  16.3 0.0 collective-permute-done.1
  16.3 0.0 collective-permute-done.2
  16.3 0.1 copy.16
  16.4 0.2 broadcast_in_dim.2
  16.6 10.4 %all_to_all.5 = bf16[4,2,6,3072]{3,1,2,0:T(2,128)(2,1)S(1)} all-to-all(bf16[4,2,6,3072]{3,1,2,0:T(2,128)(2,1)S(1)} %broadcast_in_dim.2), channel_id=1, replica_groups={{0,2,4,6},{8,10,12,14},{16,18,20,22},{24,26,28,30},{32,34,36,38},{40,42..., dimensions={0} | all-to-all | bytes 589824 | tf_op jit(solution)/shard_map/all_to_all | solution.py:445
  27.0 0.1 copy.17
  27.0 0.1 reshape.10
  27.1 2.0 %collective-permute-start.4 = (bf16[1,48,3072]{2,1,0:T(8,128)(2,1)S(1)}, bf16[1,48,3072]{2,1,0:T(8,128)(2,1)S(1)}, u32[]{:S(2)}, u32[]{:S(2)}) collective-permute-start(bf16[1,48,3072]{2,1,0:T(8,128)(2,1)S(1)} %reshape.10), channel_id=1, source_target_pairs={{224,0},{25,1},{226,2},{27,3},{228,4},{29,5},{230,6},{31,7},{232,8... | collective-permute-start | bytes 884744 | tf_op jit(solution)/shard_map/ppermute | solution.py:419
  29.2 3.8 %collective-permute-start.5 = (bf16[1,48,3072]{2,1,0:T(8,128)(2,1)S(1)}, bf16[1,48,3072]{2,1,0:T(8,128)(2,1)S(1)}, u32[]{:S(2)}, u32[]{:S(2)}) collective-permute-start(bf16[1,48,3072]{2,1,0:T(8,128)(2,1)S(1)} %reshape.10), channel_id=1, source_target_pairs={{64,0},{17,1},{66,2},{19,3},{68,4},{21,5},{70,6},{23,7},{72,8},{25... | collective-permute-start | bytes 884744 | tf_op jit(solution)/shard_map/ppermute | solution.py:419
  33.0 0.7 dynamic-slice_bitcast_fusion.info
  33.7 1.4 %collective-permute-start.3 = (bf16[1,48,3072]{2,1,0:T(8,128)(2,1)S(1)}, bf16[1,48,3072]{2,1,0:T(8,128)(2,1)S(1)}, u32[]{:S(2)}, u32[]{:S(2)}) collective-permute-start(bf16[1,48,3072]{2,1,0:T(8,128)(2,1)S(1)} %reshape.10), channel_id=1, source_target_pairs={{32,0},{9,1},{34,2},{11,3},{36,4},{13,5},{38,6},{15,7},{40,8},{17,... | collective-permute-start | bytes 884744 | tf_op jit(solution)/shard_map/ppermute | solution.py:419
  35.0 1.1 %collective-permute-done.4 = bf16[1,48,3072]{2,1,0:T(8,128)(2,1)S(1)} collective-permute-done((bf16[1,48,3072]{2,1,0:T(8,128)(2,1)S(1)}, bf16[1,48,3072]{2,1,0:T(8,128)(2,1)S(1)}, u32[]{:S(2)}, u32[]{:S(2)}) %collective-permute-start.4) | collective-permute-done | bytes 294944 | tf_op jit(solution)/shard_map/ppermute | solution.py:419
  36.2 4.1 %collective-permute-done.5 = bf16[1,48,3072]{2,1,0:T(8,128)(2,1)S(1)} collective-permute-done((bf16[1,48,3072]{2,1,0:T(8,128)(2,1)S(1)}, bf16[1,48,3072]{2,1,0:T(8,128)(2,1)S(1)}, u32[]{:S(2)}, u32[]{:S(2)}) %collective-permute-start.5) | collective-permute-done | bytes 294944 | tf_op jit(solution)/shard_map/ppermute | solution.py:419
  40.3 0.1 pad_maximum_fusion.2
  40.3 0.0 copy-start
  40.3 0.0 copy-start.2
  40.3 0.0 copy-start.4
  40.4 0.0 copy-start.5
  40.4 0.0 copy-start.6
  40.4 1.1 %collective-permute-start.7 = (bf16[2,48,3072]{2,1,0:T(8,128)(2,1)S(1)}, bf16[2,48,3072]{2,1,0:T(8,128)(2,1)S(1)}, u32[]{:S(2)}, u32[]{:S(2)}) collective-permute-start(bf16[2,48,3072]{2,1,0:T(8,128)(2,1)S(1)} %pad_maximum_fusion.2), channel_id=1, source_target_pairs={{24,0},{225,1},{26,2},{227,3},{28,4},{229,5},{30,6},{231,7},{0,8},... | collective-permute-start | bytes 1769480 | tf_op jit(solution)/shard_map/ppermute | solution.py:419
  41.5 0.0 collective-permute-done.3
  41.5 0.1 pad_maximum_fusion.3
  41.5 1.7 %collective-permute-start.8 = (bf16[2,48,3072]{2,1,0:T(8,128)(2,1)S(1)}, bf16[2,48,3072]{2,1,0:T(8,128)(2,1)S(1)}, u32[]{:S(2)}, u32[]{:S(2)}) collective-permute-start(bf16[2,48,3072]{2,1,0:T(8,128)(2,1)S(1)} %pad_maximum_fusion.3), channel_id=1, source_target_pairs={{8,0},{33,1},{10,2},{35,3},{12,4},{37,5},{14,6},{39,7},{16,8},{41,... | collective-permute-start | bytes 1769480 | tf_op jit(solution)/shard_map/ppermute | solution.py:419
  43.3 0.1 pad_maximum_fusion.1.slab
  43.5 9.8 %probs.1 = (bf16[4,3072,256]{2,1,0:T(8,128)(2,1)S(1)}, bf16[2,3072,256]{2,1,0:T(8,128)(2,1)S(1)}, bf16[4,48,3072]{2,1,0:T(8,128)(2,1)S(1)}) custom-call(s32[6]{0:T(128)S(1)} %dynamic-slice_bitcast_fusion.info, s32[1,8]{1,0:T(1,128)S(1)} %copy-done.4, s32[1,8]{1,0:T(1,128)S(1)} %copy-done.5, s32[1,8]{1,0:T(1,128)S(1)} %copy-done.6, ...), custom_call_target="tpu_custom_call", output_to_operand_aliasing={{2}: (8, {})} | custom-call | flops 1207959552 | bytes 12000000 | tf_op jit(solution)/shard_map/probs/pallas_call | solution.py:157
  53.3 0.0 copy-start.3
  53.3 0.1 fusion
  53.4 0.1 collective-permute-start.6
  53.5 2.7 %collective-permute-start.9 = (bf16[2,48,3072]{2,1,0:T(8,128)(2,1)S(1)}, bf16[2,48,3072]{2,1,0:T(8,128)(2,1)S(1)}, u32[]{:S(2)}, u32[]{:S(2)}) collective-permute-start(bf16[2,48,3072]{2,1,0:T(8,128)(2,1)S(1)} %get-tuple-element.23), channel_id=1, source_target_pairs={{8,0},{33,1},{10,2},{35,3},{12,4},{37,5},{14,6},{39,7},{16,8},{41,... | collective-permute-start | bytes 1769480 | tf_op jit(solution)/shard_map/ppermute | solution.py:419
  56.1 0.0 collective-permute-done.7.refs_1_.refs_5_
  56.1 0.0 collective-permute-start.12
  56.1 0.0 collective-permute-done.8.refs_3_.refs_0_
  56.1 2.7 %collective-permute-start.11 = (bf16[2,48,3072]{2,1,0:T(8,128)(2,1)S(1)}, bf16[2,48,3072]{2,1,0:T(8,128)(2,1)S(1)}, u32[]{:S(2)}, u32[]{:S(2)}) collective-permute-start(bf16[2,48,3072]{2,1,0:T(8,128)(2,1)S(1)} %collective-permute-done.8.refs_3_.refs_0_), channel_id=1, source_target_pairs={{8,0},{33,1},{10,2},{35,3},{12,4},{37,5},{14,6},{39,7},{16,8},{41,... | collective-permute-start | bytes 1769480 | tf_op jit(solution)/shard_map/ppermute | solution.py:419
  58.8 4.6 %collective-permute-done.6.refs_0_.refs_4_ = bf16[2,48,3072]{2,1,0:T(8,128)(2,1)S(1)} collective-permute-done((bf16[2,48,3072]{2,1,0:T(8,128)(2,1)S(1)}, bf16[2,48,3072]{2,1,0:T(8,128)(2,1)S(1)}, u32[]{:S(2)}, u32[]{:S(2)}) %collective-permute-start.6) | collective-permute-done | bytes 589856 | tf_op jit(solution)/shard_map/ppermute | solution.py:419
  63.4 0.0 collective-permute-done.10.refs_6_.refs_7_
  63.4 16.9 %grads.2 = (bf16[3,512,512]{2,1,0:T(8,128)(2,1)S(1)}, bf16[3,512,512]{2,1,0:T(8,128)(2,1)S(1)}) custom-call(s32[6]{0:T(128)S(1)} %dynamic-slice_bitcast_fusion.info, s32[1,8]{1,0:T(1,128)S(1)} %copy-done.4, s32[1,8]{1,0:T(1,128)S(1)} %copy-done.5, s32[1,8]{1,0:T(1,128)S(1)} %copy-done.6, bf16[2,48,3072]{2,1,0:T(8,128)(2,1)S(1)} %collective-permute-done.6.refs_0_.refs_4_, ...), custom_call_target="tpu_custom_call" | custom-call | flops 6442450944 | bytes 20000000 | tf_op jit(solution)/shard_map/grads/pallas_call | solution.py:322
  80.3 11.0 %collective-permute-start.13 = (bf16[3,512,512]{2,1,0:T(8,128)(2,1)S(1)}, bf16[3,512,512]{2,1,0:T(8,128)(2,1)S(1)}, u32[]{:S(2)}, u32[]{:S(2)}) collective-permute-start(bf16[3,512,512]{2,1,0:T(8,128)(2,1)S(1)} %get-tuple-element.18), channel_id=1, source_target_pairs={{0,1},{1,0},{2,3},{3,2},{4,5},{5,4},{6,7},{7,6},{8,9},{9,8},{10,11... | collective-permute-start | bytes 4718600 | tf_op jit(solution)/shard_map/ppermute | solution.py:464
  91.2 9.7 %grads.3 = (bf16[3,512,256]{2,1,0:T(8,128)(2,1)S(1)}, bf16[3,512,256]{2,1,0:T(8,128)(2,1)S(1)}) custom-call(s32[6]{0:T(128)S(1)} %dynamic-slice_bitcast_fusion.info, s32[1,8]{1,0:T(1,128)S(1)} %copy-done.4, s32[1,8]{1,0:T(1,128)S(1)} %copy-done.5, s32[1,8]{1,0:T(1,128)S(1)} %copy-done.6, bf16[2,48,3072]{2,1,0:T(8,128)(2,1)S(1)} %collective-permute-done.8.refs_3_.refs_0_, ...), custom_call_target="tpu_custom_call" | custom-call | flops 3221225472 | bytes 10000000 | tf_op jit(solution)/shard_map/grads/pallas_call | solution.py:322
  101.0 0.1 collective-permute-start.14
  101.1 2.7 %merge.2 = (bf16[512,1536]{1,0:T(8,128)(2,1)}, bf16[512,1536]{1,0:T(8,128)(2,1)}, bf16[512,1536]{1,0:T(8,128)(2,1)}) custom-call(s32[6]{0:T(128)S(1)} %dynamic-slice_bitcast_fusion.info, bf16[3,512,512]{2,1,0:T(8,128)(2,1)S(1)} %get-tuple-element.15.refs_0_, bf16[3,512,256]{2,1,0:T(8,128)(2,1)S(1)} %get-tuple-element.17.refs_1_, ...), custom_call_target="tpu_custom_call" | custom-call | tf_op jit(solution)/shard_map/merge/pallas_call | solution.py:381
  103.8 1.5 %merge.3 = (bf16[512,1536]{1,0:T(8,128)(2,1)}, bf16[512,1536]{1,0:T(8,128)(2,1)}, bf16[512,1536]{1,0:T(8,128)(2,1)}) custom-call(s32[6]{0:T(128)S(1)} %dynamic-slice_bitcast_fusion.info, bf16[512,1536]{1,0:T(8,128)(2,1)} %get-tuple-element.19.refs_0_, ...), custom_call_target="tpu_custom_call", output_to_operand_aliasing={{0}: (1, {}), {1}: (2, {}), {2}: (3, {})} | custom-call | tf_op jit(solution)/shard_map/merge/pallas_call | solution.py:381
  (16 shorter events, 0.1 us)
Async XLA Ops:
  0.6 11.9 %copy-start.1 = (bf16[512,1536]{1,0:T(8,128)(2,1)S(1)}, bf16[512,1536]{1,0:T(8,128)(2,1)}, u32[]{:S(2)}) copy-start(bf16[512,1536]{1,0:T(8,128)(2,1)} %refs_13_.3) | copy-start | bytes 4718596
  0.6 15.6 %collective-permute-start.1 = (bf16[6,3072]{1,0:T(8,128)(2,1)}, bf16[6,3072]{1,0:T(8,128)(2,1)S(1)}, u32[]{:S(2)}, u32[]{:S(2)}) collective-permute-start(bf16[6,3072]{1,0:T(8,128)(2,1)} %param.13), channel_id=1, source_target_pairs={{1,0},{129,1},{3,2},{131,3},{5,4},{133,5},{7,6},{135,7},{33,8},{13... | collective-permute-start | bytes 110600 | tf_op jit(solution)/shard_map/ppermute | solution.py:419
  4.0 12.3 %collective-permute-start.2 = (bf16[6,3072]{1,0:T(8,128)(2,1)}, bf16[6,3072]{1,0:T(8,128)(2,1)S(1)}, u32[]{:S(2)}, u32[]{:S(2)}) collective-permute-start(bf16[6,3072]{1,0:T(8,128)(2,1)} %param.13), channel_id=1, source_target_pairs={{0,0},{128,1},{2,2},{130,3},{4,4},{132,5},{6,6},{134,7},{32,8},{13... | collective-permute-start | bytes 110600 | tf_op jit(solution)/shard_map/ppermute | solution.py:419
  15.8 27.7 %collective-permute-start = (bf16[3,512,768]{2,1,0:T(8,128)(2,1)}, bf16[3,512,768]{2,1,0:T(8,128)(2,1)S(1)}, u32[]{:S(2)}, u32[]{:S(2)}) collective-permute-start(bf16[3,512,768]{2,1,0:T(8,128)(2,1)} %pad_maximum_fusion), channel_id=1, source_target_pairs={{0,1},{1,0},{2,3},{3,2},{4,5},{5,4},{6,7},{7,6},{8,9},{9,8},{10,11... | collective-permute-start | bytes 7077896 | tf_op jit(solution)/shard_map/ppermute | solution.py:464
  15.8 47.6 %collective-permute-start.10 = (bf16[512,3072]{1,0:T(8,128)(2,1)}, bf16[512,3072]{1,0:T(8,128)(2,1)}, u32[]{:S(2)}, u32[]{:S(2)}) collective-permute-start(bf16[512,3072]{1,0:T(8,128)(2,1)} %refs_6_.1), channel_id=1, source_target_pairs={{0,1},{1,0},{2,3},{3,2},{4,5},{5,4},{6,7},{7,6},{8,9},{9,8},{10,11... | collective-permute-start | bytes 9437192 | tf_op jit(solution)/shard_map/ppermute | solution.py:464
  27.1 9.0 %collective-permute-start.4 = (bf16[1,48,3072]{2,1,0:T(8,128)(2,1)S(1)}, bf16[1,48,3072]{2,1,0:T(8,128)(2,1)S(1)}, u32[]{:S(2)}, u32[]{:S(2)}) collective-permute-start(bf16[1,48,3072]{2,1,0:T(8,128)(2,1)S(1)} %reshape.10), channel_id=1, source_target_pairs={{224,0},{25,1},{226,2},{27,3},{228,4},{29,5},{230,6},{31,7},{232,8... | collective-permute-start | bytes 884744 | tf_op jit(solution)/shard_map/ppermute | solution.py:419
  29.2 11.1 %collective-permute-start.5 = (bf16[1,48,3072]{2,1,0:T(8,128)(2,1)S(1)}, bf16[1,48,3072]{2,1,0:T(8,128)(2,1)S(1)}, u32[]{:S(2)}, u32[]{:S(2)}) collective-permute-start(bf16[1,48,3072]{2,1,0:T(8,128)(2,1)S(1)} %reshape.10), channel_id=1, source_target_pairs={{64,0},{17,1},{66,2},{19,3},{68,4},{21,5},{70,6},{23,7},{72,8},{25... | collective-permute-start | bytes 884744 | tf_op jit(solution)/shard_map/ppermute | solution.py:419
  33.7 7.8 %collective-permute-start.3 = (bf16[1,48,3072]{2,1,0:T(8,128)(2,1)S(1)}, bf16[1,48,3072]{2,1,0:T(8,128)(2,1)S(1)}, u32[]{:S(2)}, u32[]{:S(2)}) collective-permute-start(bf16[1,48,3072]{2,1,0:T(8,128)(2,1)S(1)} %reshape.10), channel_id=1, source_target_pairs={{32,0},{9,1},{34,2},{11,3},{36,4},{13,5},{38,6},{15,7},{40,8},{17,... | collective-permute-start | bytes 884744 | tf_op jit(solution)/shard_map/ppermute | solution.py:419
  40.3 3.1 %copy-start = (bf16[512,1536]{1,0:T(8,128)(2,1)S(1)}, bf16[512,1536]{1,0:T(8,128)(2,1)}, u32[]{:S(2)}) copy-start(bf16[512,1536]{1,0:T(8,128)(2,1)} %refs_12_.3) | copy-start | bytes 4718596
  40.3 3.1 %copy-start.2 = (bf16[512,1536]{1,0:T(8,128)(2,1)S(1)}, bf16[512,1536]{1,0:T(8,128)(2,1)}, u32[]{:S(2)}) copy-start(bf16[512,1536]{1,0:T(8,128)(2,1)} %refs_13_.3) | copy-start | bytes 4718596
  40.3 3.1 %copy-start.4 = (s32[1,8]{1,0:T(1,128)S(1)}, s32[1,8]{1,0:T(1,128)}, u32[]{:S(2)}) copy-start(s32[1,8]{1,0:T(1,128)} %clips.5) | copy-start | bytes 100
  40.4 3.1 %copy-start.5 = (s32[1,8]{1,0:T(1,128)S(1)}, s32[1,8]{1,0:T(1,128)}, u32[]{:S(2)}) copy-start(s32[1,8]{1,0:T(1,128)} %valid_rows.5) | copy-start | bytes 100
  40.4 3.1 %copy-start.6 = (s32[1,8]{1,0:T(1,128)S(1)}, s32[1,8]{1,0:T(1,128)}, u32[]{:S(2)}) copy-start(s32[1,8]{1,0:T(1,128)} %valid_cols.5) | copy-start | bytes 100
  40.4 15.8 %collective-permute-start.7 = (bf16[2,48,3072]{2,1,0:T(8,128)(2,1)S(1)}, bf16[2,48,3072]{2,1,0:T(8,128)(2,1)S(1)}, u32[]{:S(2)}, u32[]{:S(2)}) collective-permute-start(bf16[2,48,3072]{2,1,0:T(8,128)(2,1)S(1)} %pad_maximum_fusion.2), channel_id=1, source_target_pairs={{24,0},{225,1},{26,2},{227,3},{28,4},{229,5},{30,6},{231,7},{0,8},... | collective-permute-start | bytes 1769480 | tf_op jit(solution)/shard_map/ppermute | solution.py:419
  41.5 14.6 %collective-permute-start.8 = (bf16[2,48,3072]{2,1,0:T(8,128)(2,1)S(1)}, bf16[2,48,3072]{2,1,0:T(8,128)(2,1)S(1)}, u32[]{:S(2)}, u32[]{:S(2)}) collective-permute-start(bf16[2,48,3072]{2,1,0:T(8,128)(2,1)S(1)} %pad_maximum_fusion.3), channel_id=1, source_target_pairs={{8,0},{33,1},{10,2},{35,3},{12,4},{37,5},{14,6},{39,7},{16,8},{41,... | collective-permute-start | bytes 1769480 | tf_op jit(solution)/shard_map/ppermute | solution.py:419
  53.3 10.1 %copy-start.3 = (bf16[512,1536]{1,0:T(8,128)(2,1)S(1)}, bf16[512,1536]{1,0:T(8,128)(2,1)}, u32[]{:S(2)}) copy-start(bf16[512,1536]{1,0:T(8,128)(2,1)} %refs_14_.1) | copy-start | bytes 4718596
  53.4 10.0 %collective-permute-start.6 = (bf16[2,48,3072]{2,1,0:T(8,128)(2,1)S(1)}, bf16[2,48,3072]{2,1,0:T(8,128)(2,1)S(1)}, u32[]{:S(2)}, u32[]{:S(2)}) collective-permute-start(bf16[2,48,3072]{2,1,0:T(8,128)(2,1)S(1)} %get-tuple-element.24), channel_id=1, source_target_pairs={{24,0},{225,1},{26,2},{227,3},{28,4},{229,5},{30,6},{231,7},{0,8},... | collective-permute-start | bytes 1769480 | tf_op jit(solution)/shard_map/ppermute | solution.py:419
  53.5 9.9 %collective-permute-start.9 = (bf16[2,48,3072]{2,1,0:T(8,128)(2,1)S(1)}, bf16[2,48,3072]{2,1,0:T(8,128)(2,1)S(1)}, u32[]{:S(2)}, u32[]{:S(2)}) collective-permute-start(bf16[2,48,3072]{2,1,0:T(8,128)(2,1)S(1)} %get-tuple-element.23), channel_id=1, source_target_pairs={{8,0},{33,1},{10,2},{35,3},{12,4},{37,5},{14,6},{39,7},{16,8},{41,... | collective-permute-start | bytes 1769480 | tf_op jit(solution)/shard_map/ppermute | solution.py:419
  56.1 35.1 %collective-permute-start.12 = (bf16[2,48,3072]{2,1,0:T(8,128)(2,1)S(1)}, bf16[2,48,3072]{2,1,0:T(8,128)(2,1)S(1)}, u32[]{:S(2)}, u32[]{:S(2)}) collective-permute-start(bf16[2,48,3072]{2,1,0:T(8,128)(2,1)S(1)} %collective-permute-done.7.refs_1_.refs_5_), channel_id=1, source_target_pairs={{24,0},{225,1},{26,2},{227,3},{28,4},{229,5},{30,6},{231,7},{0,8},... | collective-permute-start | bytes 1769480 | tf_op jit(solution)/shard_map/ppermute | solution.py:419
  56.1 35.1 %collective-permute-start.11 = (bf16[2,48,3072]{2,1,0:T(8,128)(2,1)S(1)}, bf16[2,48,3072]{2,1,0:T(8,128)(2,1)S(1)}, u32[]{:S(2)}, u32[]{:S(2)}) collective-permute-start(bf16[2,48,3072]{2,1,0:T(8,128)(2,1)S(1)} %collective-permute-done.8.refs_3_.refs_0_), channel_id=1, source_target_pairs={{8,0},{33,1},{10,2},{35,3},{12,4},{37,5},{14,6},{39,7},{16,8},{41,... | collective-permute-start | bytes 1769480 | tf_op jit(solution)/shard_map/ppermute | solution.py:419
  80.3 20.8 %collective-permute-start.13 = (bf16[3,512,512]{2,1,0:T(8,128)(2,1)S(1)}, bf16[3,512,512]{2,1,0:T(8,128)(2,1)S(1)}, u32[]{:S(2)}, u32[]{:S(2)}) collective-permute-start(bf16[3,512,512]{2,1,0:T(8,128)(2,1)S(1)} %get-tuple-element.18), channel_id=1, source_target_pairs={{0,1},{1,0},{2,3},{3,2},{4,5},{5,4},{6,7},{7,6},{8,9},{9,8},{10,11... | collective-permute-start | bytes 4718600 | tf_op jit(solution)/shard_map/ppermute | solution.py:464
  101.0 2.9 %collective-permute-start.14 = (bf16[3,512,256]{2,1,0:T(8,128)(2,1)S(1)}, bf16[3,512,256]{2,1,0:T(8,128)(2,1)S(1)}, u32[]{:S(2)}, u32[]{:S(2)}) collective-permute-start(bf16[3,512,256]{2,1,0:T(8,128)(2,1)S(1)} %get-tuple-element.22), channel_id=1, source_target_pairs={{0,1},{1,0},{2,3},{3,2},{4,5},{5,4},{6,7},{7,6},{8,9},{9,8},{10,11... | collective-permute-start | bytes 2359304 | tf_op jit(solution)/shard_map/ppermute | solution.py:464

commit v4 on v3

--- a/solution.py
+++ b/solution.py
@@ -85,9 +85,24 @@
 
 
 def probs_kernel(
-    info, clips, valid_rows, valid_cols, q_own, k_own, q_other, k_other, slab,
-    probs_early, probs_late, slab_out, q_all, k_all, bias, logits_all,
+    passing, loading, info, clips, valid_rows, valid_cols, q_own, k_own, q_other, k_other, *refs
 ):
+    loads, refs = refs[:loading], refs[loading + passing :]
+    kept = refs[0].at[0]
+    loaded, refs = refs[1 : 1 + loading // 2], refs[1 + loading // 2 + passing :]
+    q_all, k_all, bias, logits_all = refs[:4]
+    step = pl.program_id(0)
+    copies = []
+    for index, part in enumerate(loads):
+        core = (info[ME], 1 - info[ME])[index]
+        rows = pl.ds(pl.multiple_of(core * LOCAL, LOCAL), LOCAL)
+        copies.append(pltpu.make_async_copy(part, loaded[0].at[rows, :], refs[4].at[index]))
+
+    @pl.when(step == 0)
+    def _():
+        for copy in copies:
+            copy.start()
+
     @pl.when(pl.program_id(0) == 0)
     def _():
         fill_bias(clips, valid_rows, valid_cols, bias)
@@ -109,7 +124,7 @@
             top = part if top is None else jnp.maximum(top, part)
         return jnp.max(top, axis=0, keepdims=True)
 
-    def find_probs(pair, top, kept):
+    def find_probs(pair, top):
         count, offset = KEY_COUNT[pair], OFFSET[pair]
         logits = logits_all.at[pair % 2]
         total = None
@@ -125,25 +140,21 @@
             start = (offset + slot) * TILE
             kept[start : start + TILE, :] = (logits[rows, :] * inverse).astype(jnp.bfloat16)
 
-    def find_all(kept):
-        top = find_logits(0)
-        for pair in range(4):
-            later = find_logits(pair + 1) if pair < 3 else None
-            find_probs(pair, top, kept)
-            top = later
-
-    @pl.when(pl.program_id(0) < 4)
+    top = find_logits(0)
+    for pair in range(4):
+        later = find_logits(pair + 1) if pair < 3 else None
+        find_probs(pair, top)
+        top = later
+
+    @pl.when(step == pl.num_programs(0) - 1)
     def _():
-        find_all(probs_early.at[0])
-
-    @pl.when(pl.program_id(0) >= 4)
-    def _():
-        find_all(probs_late.at[0])
-
-
-def probs_call(tables, q, k, others, slab):
+        for copy in copies:
+            copy.wait()
+
+
+def probs_call(tables, q, k, others, begin, heads, passing, loads=()):
     def head_at(step, info):
-        return lax.rem(info[MINE] + step, 6)
+        return lax.rem(info[MINE] + begin + step, 6)
 
     def other_block(which):
         return pl.BlockSpec(
@@ -154,49 +165,52 @@
         (LOCAL, HEAD_DIM), lambda step, info, *_: (0, info[ME] * 6 + head_at(step, info))
     )
     block = (1, SLOTS * TILE, PAIR)
+    anywhere = pl.BlockSpec(memory_space=pl.ANY)
+    loaded = [jax.ShapeDtypeStruct((GROUP, DIM), jnp.bfloat16)] * (len(loads) // 2)
     return pl.pallas_call(
-        probs_kernel,
-        out_shape=[
-            jax.ShapeDtypeStruct((4, SLOTS * TILE, PAIR), jnp.bfloat16),
-            jax.ShapeDtypeStruct((2, SLOTS * TILE, PAIR), jnp.bfloat16),
-            jax.ShapeDtypeStruct(slab.shape, slab.dtype),
-        ],
+        functools.partial(probs_kernel, len(passing), len(loads)),
+        out_shape=[jax.ShapeDtypeStruct((heads, SLOTS * TILE, PAIR), jnp.bfloat16)]
+        + loaded
+        + [jax.ShapeDtypeStruct(x.shape, x.dtype) for x in passing],
         grid_spec=pltpu.PrefetchScalarGridSpec(
             num_scalar_prefetch=4,
-            grid=(6,),
-            in_specs=[own, own, other_block(0), other_block(1), pl.BlockSpec(memory_space=pl.ANY)],
-            out_specs=[
-                pl.BlockSpec(block, lambda step, *_: (jnp.minimum(step, 3), 0, 0)),
-                pl.BlockSpec(block, lambda step, *_: (jnp.maximum(step, 4) - 4, 0, 0)),
-                pl.BlockSpec(memory_space=pl.ANY),
-            ],
+            grid=(heads,),
+            in_specs=[own, own, other_block(0), other_block(1)]
+            + [pl.BlockSpec(memory_space=pl.ANY)] * len(loads)
+            + [anywhere] * len(passing),
+            out_specs=[pl.BlockSpec(block, lambda step, *_: (step, 0, 0))]
+            + [pl.BlockSpec(memory_space=pltpu.VMEM)] * len(loaded)
+            + [anywhere] * len(passing),
             scratch_shapes=[
                 pltpu.VMEM((GROUP, HEAD_DIM), jnp.bfloat16),
                 pltpu.VMEM((GROUP, HEAD_DIM), jnp.bfloat16),
                 pltpu.VMEM((SLOTS * TILE, PAIR), jnp.float32),
                 pltpu.VMEM((2, KEY_MOST, PAIR), jnp.float32),
+                pltpu.SemaphoreType.DMA((2,)),
             ],
         ),
         compiler_params=pltpu.CompilerParams(vmem_limit_bytes=VMEM),
         cost_estimate=pl.CostEstimate(
-            flops=6 * 2 * SLOTS * TILE * PAIR * HEAD_DIM,
-            bytes_accessed=12_000_000,
-            transcendentals=6 * SLOTS * TILE * PAIR,
+            flops=heads * 2 * SLOTS * TILE * PAIR * HEAD_DIM,
+            bytes_accessed=2_000_000 * heads,
+            transcendentals=heads * SLOTS * TILE * PAIR,
         ),
-        input_output_aliases={8: 2},
+        input_output_aliases={
+            8 + len(loads) + i: 1 + len(loaded) + i for i in range(len(passing))
+        },
         name="probs",
-    )(*tables, q, k, others, others, slab)
-
-
-def project(info, valid_rows, valid_cols, grad_all, grad_own, grad_other, weight):
+    )(*tables, q, k, others, others, *loads, *passing)
+
+
+def project(valid_rows, valid_cols, grad_all, grad_out, weight):
     cell = lax.broadcasted_iota(jnp.int32, (TILE, HEAD_DIM), 0)
     row, col = cell >> 4, cell & (TILE_W - 1)
-    for begin, grad_out in ((info[ME] * 4, grad_own), ((1 - info[ME]) * 4, grad_other)):
-        grad = dot(grad_out[...], weight, NT)
+    for half in range(2):
+        grad = dot(grad_out[half * LOCAL : (half + 1) * LOCAL, :], weight, NT)
         for step in range(4):
-            frame = begin + step
+            frame = half * 4 + step
             valid = (row < valid_rows[0, frame]) & (col < valid_cols[0, frame])
-            rows = pl.ds(pl.multiple_of(frame * TILE, TILE), TILE)
+            rows = slice(frame * TILE, (frame + 1) * TILE)
             for head in range(2):
                 part = grad[step * TILE : (step + 1) * TILE, head * TILE : (head + 1) * TILE]
                 grad_all[head, rows, :] = jnp.where(valid, part, 0.0).astype(jnp.bfloat16)
@@ -212,10 +226,10 @@
 
 def grads_kernel(pieces, row_slot, info, clips, valid_rows, valid_cols, *refs):
     weight_refs, refs = refs[: len(pieces)], refs[len(pieces) :]
-    grad_own, grad_other, probs = refs[:3]
-    own_heads, other_heads = (refs[3:6], refs[6:9]), (refs[9:12], refs[12:15])
-    kept, sent, weight, grad_all, q_all, k_all, v_all, grad_probs_all, grad_scores_all = refs[15:24]
-    dq_all, dk_all, dv_all = refs[24:]
+    grad_out, probs = refs[:2]
+    own_heads, other_heads = (refs[2:5], refs[5:8]), (refs[8:11], refs[11:14])
+    kept, sent, weight, grad_all, q_all, k_all, v_all, grad_probs_all, grad_scores_all = refs[14:23]
+    dq_all, dk_all, dv_all = refs[23:]
     me = info[ME]
     step = pl.program_id(0)
     probs_heads = [probs.at[2 * step + head] for head in range(2)]
@@ -226,7 +240,7 @@
 
     start = pl.multiple_of(info[row_slot] + step * PAIR, 64)
     rows = weight[pl.ds(start, PAIR), :]
-    project(info, valid_rows, valid_cols, grad_all, grad_own, grad_other, rows)
+    project(valid_rows, valid_cols, grad_all, grad_out, rows)
     for head in range(2):
         for scratch, own, other in zip(
             (q_all, k_all, v_all), own_heads[head], other_heads[head]
@@ -318,14 +332,14 @@
     result = jax.ShapeDtypeStruct((3, LOCAL, heads * HEAD_DIM), jnp.bfloat16)
     arrays = [piece for _, _, piece in pieces]
     layout = tuple((slab, slots) for slab, slots, _ in pieces)
-    grad_own, grad_other, *own, other = tokens
+    grad_out, *own, other = tokens
     return pl.pallas_call(
         functools.partial(grads_kernel, layout, row_slot),
         out_shape=[result] * 2,
         grid_spec=pltpu.PrefetchScalarGridSpec(
             num_scalar_prefetch=4,
             grid=(heads // 2,),
-            in_specs=[whole] * (len(arrays) + 3)
+            in_specs=[whole] * (len(arrays) + 2)
             + [own_block(parity) for parity in range(2) for _ in range(3)]
             + [other_block(parity, which) for parity in range(2) for which in range(3)],
             out_specs=[pl.BlockSpec((3, LOCAL, PAIR), lambda step, *_: (0, 0, step))] * 2,
@@ -349,7 +363,7 @@
             transcendentals=0,
         ),
         name="grads",
-    )(*tables, *arrays, grad_own, grad_other, probs, *own, *own, *[other] * 6)
+    )(*tables, *arrays, grad_out, probs, *own, *own, *[other] * 6)
 
 
 def merge_kernel(plan, count, info, *refs):
@@ -464,8 +478,33 @@
     return lax.ppermute(value, "frame", [(0, 1), (1, 0)])
 
 
-def other_half(value, me):
-    return jnp.where(me == 0, value[:, HALF:], value[:, :HALF])
+def halves_kernel(info, *refs):
+    values, out, sems = refs[:3], refs[3], refs[4]
+    cols = pl.ds(pl.multiple_of((1 - info[ME]) * HALF, HALF), HALF)
+    copies = [
+        pltpu.make_async_copy(value.at[:, cols], out.at[index], sems.at[index])
+        for index, value in enumerate(values)
+    ]
+    for copy in copies:
+        copy.start()
+    for copy in copies:
+        copy.wait()
+
+
+def other_halves(info, values):
+    return pl.pallas_call(
+        halves_kernel,
+        out_shape=jax.ShapeDtypeStruct((3, LOCAL, HALF), jnp.bfloat16),
+        grid_spec=pltpu.PrefetchScalarGridSpec(
+            num_scalar_prefetch=1,
+            grid=(1,),
+            in_specs=[pl.BlockSpec(memory_space=pl.ANY)] * 3,
+            out_specs=pl.BlockSpec(memory_space=pltpu.VMEM),
+            scratch_shapes=[pltpu.SemaphoreType.DMA((3,))],
+        ),
+        compiler_params=pltpu.CompilerParams(vmem_limit_bytes=60 * 1024 * 1024),
+        name="halves",
+    )(info, *values)
 
 
 def on_device(queries, keys, values, grad_out, out_weight, frame_clip, frame_rows, frame_cols):
@@ -474,14 +513,16 @@
     info = lax.dynamic_index_in_dim(jnp.asarray(place_table()), dp * 2 + me, 0, keepdims=False)
     tables = (info, frame_clip, frame_rows, frame_cols)
     g_other = swap(grad_out)
-    others = swap(jnp.stack([other_half(x, me) for x in (queries, keys, values)]))
+    others = swap(other_halves(info, (queries, keys, values)))
     rows = line_rows(out_weight, dp // (NY * NX))
     slab = jnp.concatenate([rows] + beside_rows(rows))
     after_low, before_high = move(slab[:2], along(True, 1)), move(slab[2:], along(True, -1))
-    probs_early, probs_late, slab = probs_call(tables, queries, keys, others, slab)
+    attend = functools.partial(probs_call, tables, queries, keys, others)
+    probs_early, g_all, slab = attend(0, 4, (slab,), (grad_out, g_other))
     after_high, before_low = move(slab[2:], along(True, 1)), move(slab[:2], along(True, -1))
+    probs_late, after_low, before_high = attend(4, 2, (after_low, before_high))
     far_low, far_high = far_slab(after_low, before_high)
-    tokens = (grad_out, g_other, queries, keys, values, others)
+    tokens = (g_all, queries, keys, values, others)
     low, high, both = (0, 1), (2, 3), (0, 1, 2, 3)
     pieces = (
         (0, low, before_low),

time: 106 us -> 101 us (0.953)
  other arithmetic: 4.95 us -> 0.3 us
  local copies, waits for them, and re-layouts: 1.22 us -> 3.62 us
    pallas_call x1 -> x3, Pallas kernels: 9.79 us -> 15.2 us  [the longest x2 11.5 us: probs_call(): pl.pallas_call(functools.partial(probs_kernel, len(passing), len(loads)),...]
    pallas_call x2, Pallas kernels: 26.6 us -> 21.2 us  [grads_call(): pl.pallas_call(functools.partial(grads_kernel, layout, row_slot), out_sha...]
    another operation x3 -> x0, other arithmetic: 4.65 us -> none  [on_device(): jnp.stack([other_half(x, me) for x in (queries, keys, values)])]
    ppermute x11, starting transfers between devices: 25.9 us -> 21.9 us  [move(): return lax.ppermute(value, ('dp', 'frame'), pairs)]
    ppermute x4, starting transfers between devices: 11.6 us -> 14.6 us  [swap(): return lax.ppermute(value, 'frame', [(0, 1), (1, 0)])]
    unnamed x14 -> x16, local copies, waits for them, and re-layouts: 0.04 us -> 1.93 us
  transfers between devices with their start and end apart: 15 -> 15, of which waited for: 3 -> 4; matrix products, arithmetic and copies ran while one was open for 6% -> 2% of each run, Pallas kernels for 37% -> 39%
where the time goes in v4:
time: 101 us
  Pallas kernels  40.6 us (40%)
  starting transfers between devices  36.5 us (36%)
  blocking collectives  9.87 us (10%)
  waiting for transfers between devices  8.91 us (9%)
  local copies, waits for them, and re-layouts  3.62 us (4%)
  between operations  1.11 us (1%)
    ppermute x11, starting transfers between devices, move(): return lax.ppermute(value, ('dp', 'frame'), pairs)  21.9 us
    pallas_call x2, Pallas kernels, grads_call(): pl.pallas_call(functools.partial(grads_kernel, layout, row_slot), out_sha...  21.2 us
    ppermute x4, starting transfers between devices, swap(): return lax.ppermute(value, 'frame', [(0, 1), (1, 0)])  14.6 us
    pallas_call x2, Pallas kernels, probs_call(): pl.pallas_call(functools.partial(probs_kernel, len(passing), len(loads)),...  11.5 us
    all_to_all x1, blocking collectives, line_rows(): lax.all_to_all(jnp.broadcast_to(rows[None], (NX,) + rows.shape), 'dp', 0,...  9.87 us
    ppermute x11, waiting for transfers between devices, move(): return lax.ppermute(value, ('dp', 'frame'), pairs)  8.9 us
    pallas_call x2, Pallas kernels, merge_call(): pl.pallas_call(functools.partial(merge_kernel, plan, len(earlier)), out_s...  4.19 us
    pallas_call x1, Pallas kernels, other_halves(): pl.pallas_call(halves_kernel, out_shape=jax.ShapeDtypeStruct((3, LOCAL, H...  3.71 us
  transfers between devices with their start and end apart: 15, of which 4 were waited for; matrix products, arithmetic and copies ran while one was open for 2% of the time, Pallas kernels for 39%

profile of v4, /device:TPU:1, one launch (start us, length us, event | category | flops | bytes accessed | tf_op | source)
XLA Modules:
  0.0 100.9 jit_solution(5843410003617315967)
XLA Ops:
  0.6 3.3 %collective-permute-start.1 = (bf16[512,3072]{1,0:T(8,128)(2,1)}, bf16[512,3072]{1,0:T(8,128)(2,1)}, u32[]{:S(2)}, u32[]{:S(2)}) collective-permute-start(bf16[512,3072]{1,0:T(8,128)(2,1)} %refs_0_.3), channel_id=1, source_target_pairs={{0,1},{1,0},{2,3},{3,2},{4,5},{5,4},{6,7},{7,6},{8,9},{9,8},{10,11... | collective-permute-start | bytes 9437192 | tf_op jit(solution)/shard_map/ppermute | solution.py:478
  4.0 0.1 collective-permute-start.2
  4.1 7.4 %collective-permute-start.3 = (bf16[6,3072]{1,0:T(8,128)(2,1)}, bf16[6,3072]{1,0:T(8,128)(2,1)S(1)}, u32[]{:S(2)}, u32[]{:S(2)}) collective-permute-start(bf16[6,3072]{1,0:T(8,128)(2,1)} %param.13), channel_id=1, source_target_pairs={{0,0},{128,1},{2,2},{130,3},{4,4},{132,5},{6,6},{134,7},{32,8},{13... | collective-permute-start | bytes 110600 | tf_op jit(solution)/shard_map/ppermute | solution.py:433
  11.4 1.2 %dynamic-slice_bitcast_fusion.info = s32[6]{0:T(128)} fusion(s32[256,6]{1,0:T(8,128)} %constant.34.clone, s32[]{:T(128)S(6)} %select_n.21), kind=kLoop, calls=%fused_computation.6 | loop fusion | bytes 52 | tf_op jit(solution)/shard_map/jit(dynamic_index_in_dim)/squeeze | solution.py:513
  12.6 3.7 %halves.1 = bf16[3,512,768]{2,1,0:T(8,128)(2,1)} custom-call(s32[6]{0:T(128)} %dynamic-slice_bitcast_fusion.info, bf16[512,1536]{1,0:T(8,128)(2,1)} %refs_11_.3, bf16[512,1536]{1,0:T(8,128)(2,1)} %refs_12_.3, bf16[512,1536]{1,0:T(8,128)(2,1)} %refs_13_.1), custom_call_target="tpu_custom_call" | custom-call | tf_op jit(solution)/shard_map/halves/pallas_call | solution.py:495
  16.4 0.1 collective-permute-start
  16.5 0.0 collective-permute-done.2
  16.6 0.1 copy.18
  16.6 0.2 broadcast_in_dim.2
  16.8 9.9 %all_to_all.5 = bf16[4,2,6,3072]{3,1,2,0:T(2,128)(2,1)S(1)} all-to-all(bf16[4,2,6,3072]{3,1,2,0:T(2,128)(2,1)S(1)} %broadcast_in_dim.2), channel_id=1, replica_groups={{0,2,4,6},{8,10,12,14},{16,18,20,22},{24,26,28,30},{32,34,36,38},{40,42..., dimensions={0} | all-to-all | bytes 589824 | tf_op jit(solution)/shard_map/all_to_all | solution.py:459
  26.7 0.1 copy.19
  26.7 0.1 reshape.10
  26.9 3.3 %collective-permute-start.5 = (bf16[1,48,3072]{2,1,0:T(8,128)(2,1)S(1)}, bf16[1,48,3072]{2,1,0:T(8,128)(2,1)S(1)}, u32[]{:S(2)}, u32[]{:S(2)}) collective-permute-start(bf16[1,48,3072]{2,1,0:T(8,128)(2,1)S(1)} %reshape.10), channel_id=1, source_target_pairs={{224,0},{25,1},{226,2},{27,3},{228,4},{29,5},{230,6},{31,7},{232,8... | collective-permute-start | bytes 884744 | tf_op jit(solution)/shard_map/ppermute | solution.py:433
  30.1 3.8 %collective-permute-start.6 = (bf16[1,48,3072]{2,1,0:T(8,128)(2,1)S(1)}, bf16[1,48,3072]{2,1,0:T(8,128)(2,1)S(1)}, u32[]{:S(2)}, u32[]{:S(2)}) collective-permute-start(bf16[1,48,3072]{2,1,0:T(8,128)(2,1)S(1)} %reshape.10), channel_id=1, source_target_pairs={{64,0},{17,1},{66,2},{19,3},{68,4},{21,5},{70,6},{23,7},{72,8},{25... | collective-permute-start | bytes 884744 | tf_op jit(solution)/shard_map/ppermute | solution.py:433
  34.0 1.4 %collective-permute-start.4 = (bf16[1,48,3072]{2,1,0:T(8,128)(2,1)S(1)}, bf16[1,48,3072]{2,1,0:T(8,128)(2,1)S(1)}, u32[]{:S(2)}, u32[]{:S(2)}) collective-permute-start(bf16[1,48,3072]{2,1,0:T(8,128)(2,1)S(1)} %reshape.10), channel_id=1, source_target_pairs={{32,0},{9,1},{34,2},{11,3},{36,4},{13,5},{38,6},{15,7},{40,8},{17,... | collective-permute-start | bytes 884744 | tf_op jit(solution)/shard_map/ppermute | solution.py:433
  35.3 1.7 %collective-permute-done.5 = bf16[1,48,3072]{2,1,0:T(8,128)(2,1)S(1)} collective-permute-done((bf16[1,48,3072]{2,1,0:T(8,128)(2,1)S(1)}, bf16[1,48,3072]{2,1,0:T(8,128)(2,1)S(1)}, u32[]{:S(2)}, u32[]{:S(2)}) %collective-permute-start.5) | collective-permute-done | bytes 294944 | tf_op jit(solution)/shard_map/ppermute | solution.py:433
  37.0 4.2 %collective-permute-done.6 = bf16[1,48,3072]{2,1,0:T(8,128)(2,1)S(1)} collective-permute-done((bf16[1,48,3072]{2,1,0:T(8,128)(2,1)S(1)}, bf16[1,48,3072]{2,1,0:T(8,128)(2,1)S(1)}, u32[]{:S(2)}, u32[]{:S(2)}) %collective-permute-start.6) | collective-permute-done | bytes 294944 | tf_op jit(solution)/shard_map/ppermute | solution.py:433
  41.2 0.1 pad_maximum_fusion.2
  41.3 0.0 copy-start
  41.3 0.0 copy-start.1
  41.3 0.0 copy-start.4
  41.3 0.0 copy-start.5
  41.4 0.0 copy-start.6
  41.4 0.0 copy-start.7
  41.4 1.1 %collective-permute-start.9 = (bf16[2,48,3072]{2,1,0:T(8,128)(2,1)S(1)}, bf16[2,48,3072]{2,1,0:T(8,128)(2,1)S(1)}, u32[]{:S(2)}, u32[]{:S(2)}) collective-permute-start(bf16[2,48,3072]{2,1,0:T(8,128)(2,1)S(1)} %pad_maximum_fusion.2), channel_id=1, source_target_pairs={{24,0},{225,1},{26,2},{227,3},{28,4},{229,5},{30,6},{231,7},{0,8},... | collective-permute-start | bytes 1769480 | tf_op jit(solution)/shard_map/ppermute | solution.py:433
  42.5 0.0 collective-permute-done.4
  42.5 0.1 pad_maximum_fusion.1
  42.6 1.7 %collective-permute-start.8 = (bf16[2,48,3072]{2,1,0:T(8,128)(2,1)S(1)}, bf16[2,48,3072]{2,1,0:T(8,128)(2,1)S(1)}, u32[]{:S(2)}, u32[]{:S(2)}) collective-permute-start(bf16[2,48,3072]{2,1,0:T(8,128)(2,1)S(1)} %pad_maximum_fusion.1), channel_id=1, source_target_pairs={{8,0},{33,1},{10,2},{35,3},{12,4},{37,5},{14,6},{39,7},{16,8},{41,... | collective-permute-start | bytes 1769480 | tf_op jit(solution)/shard_map/ppermute | solution.py:433
  44.3 0.1 pad_maximum_fusion.refs_2_
  44.4 0.0 collective-permute-done.1.refs_1_
  44.5 0.0 copy-start.3
  44.5 1.9 %copy-done.3 = bf16[512,3072]{1,0:T(8,128)(2,1)S(1)} copy-done((bf16[512,3072]{1,0:T(8,128)(2,1)S(1)}, bf16[512,3072]{1,0:T(8,128)(2,1)}, u32[]{:S(2)}) %copy-start.3) | copy-done | bytes 3145752
  46.4 7.3 %probs.2 = (bf16[4,3072,256]{2,1,0:T(8,128)(2,1)S(1)}, bf16[1024,3072]{1,0:T(8,128)(2,1)S(1)}, bf16[4,48,3072]{2,1,0:T(8,128)(2,1)S(1)}) custom-call(s32[6]{0:T(128)S(1)} %copy-done.4, s32[1,8]{1,0:T(1,128)S(1)} %copy-done.5, s32[1,8]{1,0:T(1,128)S(1)} %copy-done.6, s32[1,8]{1,0:T(1,128)S(1)} %copy-done.7, ...), custom_call_target="tpu_custom_call", output_to_operand_aliasing={{2}: (10, {})} | custom-call | flops 805306368 | bytes 8000000 | tf_op jit(solution)/shard_map/probs/pallas_call | solution.py:170
  53.7 0.1 fusion
  53.8 0.1 collective-permute-start.10
  53.9 1.4 %collective-permute-start.7 = (bf16[2,48,3072]{2,1,0:T(8,128)(2,1)S(1)}, bf16[2,48,3072]{2,1,0:T(8,128)(2,1)S(1)}, u32[]{:S(2)}, u32[]{:S(2)}) collective-permute-start(bf16[2,48,3072]{2,1,0:T(8,128)(2,1)S(1)} %get-tuple-element.30), channel_id=1, source_target_pairs={{24,0},{225,1},{26,2},{227,3},{28,4},{229,5},{30,6},{231,7},{0,8},... | collective-permute-start | bytes 1769480 | tf_op jit(solution)/shard_map/ppermute | solution.py:433
  55.4 0.0 collective-permute-done.9.refs_1_
  55.4 0.0 collective-permute-done.8.refs_0_
  55.4 4.2 %probs.3 = (bf16[2,3072,256]{2,1,0:T(8,128)(2,1)S(1)}, bf16[2,48,3072]{2,1,0:T(8,128)(2,1)S(1)}, bf16[2,48,3072]{2,1,0:T(8,128)(2,1)S(1)}) custom-call(s32[6]{0:T(128)S(1)} %copy-done.4, s32[1,8]{1,0:T(1,128)S(1)} %copy-done.5, s32[1,8]{1,0:T(1,128)S(1)} %copy-done.6, s32[1,8]{1,0:T(1,128)S(1)} %copy-done.7, ...), custom_call_target="tpu_custom_call", output_to_operand_aliasing={{1}: (8, {}), {2}: (9, {})} | custom-call | flops 402653184 | bytes 4000000 | tf_op jit(solution)/shard_map/probs/pallas_call | solution.py:170
  59.6 1.6 %collective-permute-start.11 = (bf16[2,48,3072]{2,1,0:T(8,128)(2,1)S(1)}, bf16[2,48,3072]{2,1,0:T(8,128)(2,1)S(1)}, u32[]{:S(2)}, u32[]{:S(2)}) collective-permute-start(bf16[2,48,3072]{2,1,0:T(8,128)(2,1)S(1)} %get-tuple-element.18.refs_3_.refs_0_), channel_id=1, source_target_pairs={{8,0},{33,1},{10,2},{35,3},{12,4},{37,5},{14,6},{39,7},{16,8},{41,... | collective-permute-start | bytes 1769480 | tf_op jit(solution)/shard_map/ppermute | solution.py:433
  61.1 1.5 %collective-permute-done.10.refs_4_.refs_1_ = bf16[2,48,3072]{2,1,0:T(8,128)(2,1)S(1)} collective-permute-done((bf16[2,48,3072]{2,1,0:T(8,128)(2,1)S(1)}, bf16[2,48,3072]{2,1,0:T(8,128)(2,1)S(1)}, u32[]{:S(2)}, u32[]{:S(2)}) %collective-permute-start.10) | collective-permute-done | bytes 589856 | tf_op jit(solution)/shard_map/ppermute | solution.py:433
  62.6 1.5 %collective-permute-done.7.refs_0_.refs_4_ = bf16[2,48,3072]{2,1,0:T(8,128)(2,1)S(1)} collective-permute-done((bf16[2,48,3072]{2,1,0:T(8,128)(2,1)S(1)}, bf16[2,48,3072]{2,1,0:T(8,128)(2,1)S(1)}, u32[]{:S(2)}, u32[]{:S(2)}) %collective-permute-start.7) | collective-permute-done | bytes 589856 | tf_op jit(solution)/shard_map/ppermute | solution.py:433
  64.1 14.3 %grads.2 = (bf16[3,512,512]{2,1,0:T(8,128)(2,1)S(1)}, bf16[3,512,512]{2,1,0:T(8,128)(2,1)S(1)}) custom-call(s32[6]{0:T(128)S(1)} %copy-done.4, s32[1,8]{1,0:T(1,128)S(1)} %copy-done.5, s32[1,8]{1,0:T(1,128)S(1)} %copy-done.6, s32[1,8]{1,0:T(1,128)S(1)} %copy-done.7, bf16[2,48,3072]{2,1,0:T(8,128)(2,1)S(1)} %collective-permute-done.7.refs_0_.refs_4_, ...), custom_call_target="tpu_custom_call" | custom-call | flops 6442450944 | bytes 20000000 | tf_op jit(solution)/shard_map/grads/pallas_call | solution.py:336
  78.4 11.0 %collective-permute-start.13 = (bf16[3,512,512]{2,1,0:T(8,128)(2,1)S(1)}, bf16[3,512,512]{2,1,0:T(8,128)(2,1)S(1)}, u32[]{:S(2)}, u32[]{:S(2)}) collective-permute-start(bf16[3,512,512]{2,1,0:T(8,128)(2,1)S(1)} %get-tuple-element.24), channel_id=1, source_target_pairs={{0,1},{1,0},{2,3},{3,2},{4,5},{5,4},{6,7},{7,6},{8,9},{9,8},{10,11... | collective-permute-start | bytes 4718600 | tf_op jit(solution)/shard_map/ppermute | solution.py:478
  89.4 6.9 %grads.3 = (bf16[3,512,256]{2,1,0:T(8,128)(2,1)S(1)}, bf16[3,512,256]{2,1,0:T(8,128)(2,1)S(1)}) custom-call(s32[6]{0:T(128)S(1)} %copy-done.4, s32[1,8]{1,0:T(1,128)S(1)} %copy-done.5, s32[1,8]{1,0:T(1,128)S(1)} %copy-done.6, s32[1,8]{1,0:T(1,128)S(1)} %copy-done.7, bf16[2,48,3072]{2,1,0:T(8,128)(2,1)S(1)} %get-tuple-element.18.refs_3_.refs_0_, ...), custom_call_target="tpu_custom_call" | custom-call | flops 3221225472 | bytes 10000000 | tf_op jit(solution)/shard_map/grads/pallas_call | solution.py:336
  96.3 0.1 collective-permute-start.14
  96.5 2.7 %merge.2 = (bf16[512,1536]{1,0:T(8,128)(2,1)}, bf16[512,1536]{1,0:T(8,128)(2,1)}, bf16[512,1536]{1,0:T(8,128)(2,1)}) custom-call(s32[6]{0:T(128)S(1)} %copy-done.4, bf16[3,512,512]{2,1,0:T(8,128)(2,1)S(1)} %get-tuple-element.21.refs_0_, bf16[3,512,256]{2,1,0:T(8,128)(2,1)S(1)} %get-tuple-element.23.refs_1_, ...), custom_call_target="tpu_custom_call" | custom-call | tf_op jit(solution)/shard_map/merge/pallas_call | solution.py:395
  99.2 1.5 %merge.3 = (bf16[512,1536]{1,0:T(8,128)(2,1)}, bf16[512,1536]{1,0:T(8,128)(2,1)}, bf16[512,1536]{1,0:T(8,128)(2,1)}) custom-call(s32[6]{0:T(128)S(1)} %copy-done.4, bf16[512,1536]{1,0:T(8,128)(2,1)} %get-tuple-element.25.refs_0_, bf16[512,1536]{1,0:T(8,128)(2,1)} %get-tuple-element.26.refs_1_, ...), custom_call_target="tpu_custom_call", output_to_operand_aliasing={{0}: (1, {}), {1}: (2, {}), {2}: (3, {})} | custom-call | tf_op jit(solution)/shard_map/merge/pallas_call | solution.py:395
  (17 shorter events, 0.1 us)
Async XLA Ops:
  0.6 43.8 %collective-permute-start.1 = (bf16[512,3072]{1,0:T(8,128)(2,1)}, bf16[512,3072]{1,0:T(8,128)(2,1)}, u32[]{:S(2)}, u32[]{:S(2)}) collective-permute-start(bf16[512,3072]{1,0:T(8,128)(2,1)} %refs_0_.3), channel_id=1, source_target_pairs={{0,1},{1,0},{2,3},{3,2},{4,5},{5,4},{6,7},{7,6},{8,9},{9,8},{10,11... | collective-permute-start | bytes 9437192 | tf_op jit(solution)/shard_map/ppermute | solution.py:478
  4.0 12.5 %collective-permute-start.2 = (bf16[6,3072]{1,0:T(8,128)(2,1)}, bf16[6,3072]{1,0:T(8,128)(2,1)S(1)}, u32[]{:S(2)}, u32[]{:S(2)}) collective-permute-start(bf16[6,3072]{1,0:T(8,128)(2,1)} %param.13), channel_id=1, source_target_pairs={{1,0},{129,1},{3,2},{131,3},{5,4},{133,5},{7,6},{135,7},{33,8},{13... | collective-permute-start | bytes 110600 | tf_op jit(solution)/shard_map/ppermute | solution.py:433
  4.1 12.4 %collective-permute-start.3 = (bf16[6,3072]{1,0:T(8,128)(2,1)}, bf16[6,3072]{1,0:T(8,128)(2,1)S(1)}, u32[]{:S(2)}, u32[]{:S(2)}) collective-permute-start(bf16[6,3072]{1,0:T(8,128)(2,1)} %param.13), channel_id=1, source_target_pairs={{0,0},{128,1},{2,2},{130,3},{4,4},{132,5},{6,6},{134,7},{32,8},{13... | collective-permute-start | bytes 110600 | tf_op jit(solution)/shard_map/ppermute | solution.py:433
  16.4 28.1 %collective-permute-start = (bf16[3,512,768]{2,1,0:T(8,128)(2,1)}, bf16[3,512,768]{2,1,0:T(8,128)(2,1)S(1)}, u32[]{:S(2)}, u32[]{:S(2)}) collective-permute-start(bf16[3,512,768]{2,1,0:T(8,128)(2,1)} %halves.1), channel_id=1, source_target_pairs={{0,1},{1,0},{2,3},{3,2},{4,5},{5,4},{6,7},{7,6},{8,9},{9,8},{10,11... | collective-permute-start | bytes 7077896 | tf_op jit(solution)/shard_map/ppermute | solution.py:478
  26.9 10.2 %collective-permute-start.5 = (bf16[1,48,3072]{2,1,0:T(8,128)(2,1)S(1)}, bf16[1,48,3072]{2,1,0:T(8,128)(2,1)S(1)}, u32[]{:S(2)}, u32[]{:S(2)}) collective-permute-start(bf16[1,48,3072]{2,1,0:T(8,128)(2,1)S(1)} %reshape.10), channel_id=1, source_target_pairs={{224,0},{25,1},{226,2},{27,3},{228,4},{29,5},{230,6},{31,7},{232,8... | collective-permute-start | bytes 884744 | tf_op jit(solution)/shard_map/ppermute | solution.py:433
  30.1 11.1 %collective-permute-start.6 = (bf16[1,48,3072]{2,1,0:T(8,128)(2,1)S(1)}, bf16[1,48,3072]{2,1,0:T(8,128)(2,1)S(1)}, u32[]{:S(2)}, u32[]{:S(2)}) collective-permute-start(bf16[1,48,3072]{2,1,0:T(8,128)(2,1)S(1)} %reshape.10), channel_id=1, source_target_pairs={{64,0},{17,1},{66,2},{19,3},{68,4},{21,5},{70,6},{23,7},{72,8},{25... | collective-permute-start | bytes 884744 | tf_op jit(solution)/shard_map/ppermute | solution.py:433
  34.0 8.5 %collective-permute-start.4 = (bf16[1,48,3072]{2,1,0:T(8,128)(2,1)S(1)}, bf16[1,48,3072]{2,1,0:T(8,128)(2,1)S(1)}, u32[]{:S(2)}, u32[]{:S(2)}) collective-permute-start(bf16[1,48,3072]{2,1,0:T(8,128)(2,1)S(1)} %reshape.10), channel_id=1, source_target_pairs={{32,0},{9,1},{34,2},{11,3},{36,4},{13,5},{38,6},{15,7},{40,8},{17,... | collective-permute-start | bytes 884744 | tf_op jit(solution)/shard_map/ppermute | solution.py:433
  41.3 3.1 %copy-start = (bf16[512,1536]{1,0:T(8,128)(2,1)S(1)}, bf16[512,1536]{1,0:T(8,128)(2,1)}, u32[]{:S(2)}) copy-start(bf16[512,1536]{1,0:T(8,128)(2,1)} %refs_11_.3) | copy-start | bytes 4718596
  41.3 3.1 %copy-start.1 = (bf16[512,1536]{1,0:T(8,128)(2,1)S(1)}, bf16[512,1536]{1,0:T(8,128)(2,1)}, u32[]{:S(2)}) copy-start(bf16[512,1536]{1,0:T(8,128)(2,1)} %refs_12_.3) | copy-start | bytes 4718596
  41.3 3.1 %copy-start.4 = (s32[6]{0:T(128)S(1)}, s32[6]{0:T(128)}, u32[]{:S(2)}) copy-start(s32[6]{0:T(128)} %dynamic-slice_bitcast_fusion.info) | copy-start | bytes 76
  41.3 3.1 %copy-start.5 = (s32[1,8]{1,0:T(1,128)S(1)}, s32[1,8]{1,0:T(1,128)}, u32[]{:S(2)}) copy-start(s32[1,8]{1,0:T(1,128)} %clips.7) | copy-start | bytes 100
  41.4 3.1 %copy-start.6 = (s32[1,8]{1,0:T(1,128)S(1)}, s32[1,8]{1,0:T(1,128)}, u32[]{:S(2)}) copy-start(s32[1,8]{1,0:T(1,128)} %valid_rows.7) | copy-start | bytes 100
  41.4 3.1 %copy-start.7 = (s32[1,8]{1,0:T(1,128)S(1)}, s32[1,8]{1,0:T(1,128)}, u32[]{:S(2)}) copy-start(s32[1,8]{1,0:T(1,128)} %valid_cols.7) | copy-start | bytes 100
  41.4 14.0 %collective-permute-start.9 = (bf16[2,48,3072]{2,1,0:T(8,128)(2,1)S(1)}, bf16[2,48,3072]{2,1,0:T(8,128)(2,1)S(1)}, u32[]{:S(2)}, u32[]{:S(2)}) collective-permute-start(bf16[2,48,3072]{2,1,0:T(8,128)(2,1)S(1)} %pad_maximum_fusion.2), channel_id=1, source_target_pairs={{24,0},{225,1},{26,2},{227,3},{28,4},{229,5},{30,6},{231,7},{0,8},... | collective-permute-start | bytes 1769480 | tf_op jit(solution)/shard_map/ppermute | solution.py:433
  42.6 12.8 %collective-permute-start.8 = (bf16[2,48,3072]{2,1,0:T(8,128)(2,1)S(1)}, bf16[2,48,3072]{2,1,0:T(8,128)(2,1)S(1)}, u32[]{:S(2)}, u32[]{:S(2)}) collective-permute-start(bf16[2,48,3072]{2,1,0:T(8,128)(2,1)S(1)} %pad_maximum_fusion.1), channel_id=1, source_target_pairs={{8,0},{33,1},{10,2},{35,3},{12,4},{37,5},{14,6},{39,7},{16,8},{41,... | collective-permute-start | bytes 1769480 | tf_op jit(solution)/shard_map/ppermute | solution.py:433
  44.5 1.9 %copy-start.3 = (bf16[512,3072]{1,0:T(8,128)(2,1)S(1)}, bf16[512,3072]{1,0:T(8,128)(2,1)}, u32[]{:S(2)}) copy-start(bf16[512,3072]{1,0:T(8,128)(2,1)} %refs_0_.3) | copy-start | bytes 9437188
  53.8 8.8 %collective-permute-start.10 = (bf16[2,48,3072]{2,1,0:T(8,128)(2,1)S(1)}, bf16[2,48,3072]{2,1,0:T(8,128)(2,1)S(1)}, u32[]{:S(2)}, u32[]{:S(2)}) collective-permute-start(bf16[2,48,3072]{2,1,0:T(8,128)(2,1)S(1)} %get-tuple-element.29), channel_id=1, source_target_pairs={{8,0},{33,1},{10,2},{35,3},{12,4},{37,5},{14,6},{39,7},{16,8},{41,... | collective-permute-start | bytes 1769480 | tf_op jit(solution)/shard_map/ppermute | solution.py:433
  53.9 10.2 %copy-start.2 = (bf16[512,1536]{1,0:T(8,128)(2,1)S(1)}, bf16[512,1536]{1,0:T(8,128)(2,1)}, u32[]{:S(2)}) copy-start(bf16[512,1536]{1,0:T(8,128)(2,1)} %refs_13_.1) | copy-start | bytes 4718596
  53.9 10.2 %collective-permute-start.7 = (bf16[2,48,3072]{2,1,0:T(8,128)(2,1)S(1)}, bf16[2,48,3072]{2,1,0:T(8,128)(2,1)S(1)}, u32[]{:S(2)}, u32[]{:S(2)}) collective-permute-start(bf16[2,48,3072]{2,1,0:T(8,128)(2,1)S(1)} %get-tuple-element.30), channel_id=1, source_target_pairs={{24,0},{225,1},{26,2},{227,3},{28,4},{229,5},{30,6},{231,7},{0,8},... | collective-permute-start | bytes 1769480 | tf_op jit(solution)/shard_map/ppermute | solution.py:433
  59.6 29.8 %collective-permute-start.11 = (bf16[2,48,3072]{2,1,0:T(8,128)(2,1)S(1)}, bf16[2,48,3072]{2,1,0:T(8,128)(2,1)S(1)}, u32[]{:S(2)}, u32[]{:S(2)}) collective-permute-start(bf16[2,48,3072]{2,1,0:T(8,128)(2,1)S(1)} %get-tuple-element.18.refs_3_.refs_0_), channel_id=1, source_target_pairs={{8,0},{33,1},{10,2},{35,3},{12,4},{37,5},{14,6},{39,7},{16,8},{41,... | collective-permute-start | bytes 1769480 | tf_op jit(solution)/shard_map/ppermute | solution.py:433
  61.1 28.3 %collective-permute-start.12 = (bf16[2,48,3072]{2,1,0:T(8,128)(2,1)S(1)}, bf16[2,48,3072]{2,1,0:T(8,128)(2,1)S(1)}, u32[]{:S(2)}, u32[]{:S(2)}) collective-permute-start(bf16[2,48,3072]{2,1,0:T(8,128)(2,1)S(1)} %get-tuple-element.17.refs_1_.refs_5_), channel_id=1, source_target_pairs={{24,0},{225,1},{26,2},{227,3},{28,4},{229,5},{30,6},{231,7},{0,8},... | collective-permute-start | bytes 1769480 | tf_op jit(solution)/shard_map/ppermute | solution.py:433
  78.4 18.1 %collective-permute-start.13 = (bf16[3,512,512]{2,1,0:T(8,128)(2,1)S(1)}, bf16[3,512,512]{2,1,0:T(8,128)(2,1)S(1)}, u32[]{:S(2)}, u32[]{:S(2)}) collective-permute-start(bf16[3,512,512]{2,1,0:T(8,128)(2,1)S(1)} %get-tuple-element.24), channel_id=1, source_target_pairs={{0,1},{1,0},{2,3},{3,2},{4,5},{5,4},{6,7},{7,6},{8,9},{9,8},{10,11... | collective-permute-start | bytes 4718600 | tf_op jit(solution)/shard_map/ppermute | solution.py:478
  96.3 2.9 %collective-permute-start.14 = (bf16[3,512,256]{2,1,0:T(8,128)(2,1)S(1)}, bf16[3,512,256]{2,1,0:T(8,128)(2,1)S(1)}, u32[]{:S(2)}, u32[]{:S(2)}) collective-permute-start(bf16[3,512,256]{2,1,0:T(8,128)(2,1)S(1)} %get-tuple-element.28), channel_id=1, source_target_pairs={{0,1},{1,0},{2,3},{3,2},{4,5},{5,4},{6,7},{7,6},{8,9},{9,8},{10,11... | collective-permute-start | bytes 2359304 | tf_op jit(solution)/shard_map/ppermute | solution.py:478

commit v5 on v4

--- a/solution.py
+++ b/solution.py
@@ -224,14 +224,41 @@
             weight[pl.ds(start, CHUNK), :] = ref[index]
 
 
-def grads_kernel(pieces, row_slot, info, clips, valid_rows, valid_cols, *refs):
+def head_copies(info, theirs, begin, heads, part, outs, sems, used):
+    core, first = (1 - info[ME], info[THEIRS]) if theirs else (info[ME], info[MINE])
+    copies = []
+    for step in range(heads):
+        head = core * 6 + lax.rem(first + begin + step, 6)
+        cols = pl.ds(pl.multiple_of(head * HEAD_DIM, HEAD_DIM), HEAD_DIM)
+        for index, out in enumerate(outs):
+            copies.append(
+                pltpu.make_async_copy(
+                    part.at[index, :, step * HEAD_DIM : (step + 1) * HEAD_DIM],
+                    out.at[:, cols],
+                    sems.at[used + len(copies)],
+                )
+            )
+    return copies
+
+
+def grads_kernel(pieces, row_slot, placing, info, clips, valid_rows, valid_cols, *refs):
     weight_refs, refs = refs[: len(pieces)], refs[len(pieces) :]
     grad_out, probs = refs[:2]
     own_heads, other_heads = (refs[2:5], refs[5:8]), (refs[8:11], refs[11:14])
-    kept, sent, weight, grad_all, q_all, k_all, v_all, grad_probs_all, grad_scores_all = refs[14:23]
-    dq_all, dk_all, dv_all = refs[23:]
+    earlier, refs = refs[14 : 14 + placing], refs[14 + placing :]
+    (kept, sent), placed, refs = refs[:2], refs[2 : 2 + 3 * placing], refs[2 + 3 * placing :]
+    weight, grad_all, q_all, k_all, v_all, grad_probs_all, grad_scores_all = refs[:7]
+    dq_all, dk_all, dv_all = refs[7:10]
     me = info[ME]
     step = pl.program_id(0)
+    copies = []
+    for part in earlier:
+        copies = head_copies(info, False, 0, 4, part, placed, refs[10], 0)
+
+    @pl.when(step == 0)
+    def _():
+        for copy in copies:
+            copy.start()
     probs_heads = [probs.at[2 * step + head] for head in range(2)]
 
     @pl.when(step == 0)
@@ -311,8 +338,13 @@
     add_grads(7)
     hand_over(1)
 
-
-def grads_call(tables, pieces, begin, heads, row_slot, tokens, probs):
+    @pl.when(step == pl.num_programs(0) - 1)
+    def _():
+        for copy in copies:
+            copy.wait()
+
+
+def grads_call(tables, pieces, begin, heads, row_slot, tokens, probs, earlier=()):
     def head_at(parity, step, info):
         return lax.rem(info[MINE] + begin + 2 * step + parity, 6)
 
@@ -330,19 +362,22 @@
 
     whole = pl.BlockSpec(memory_space=pltpu.VMEM)
     result = jax.ShapeDtypeStruct((3, LOCAL, heads * HEAD_DIM), jnp.bfloat16)
+    full = jax.ShapeDtypeStruct((LOCAL, WIDTH), jnp.bfloat16)
     arrays = [piece for _, _, piece in pieces]
     layout = tuple((slab, slots) for slab, slots, _ in pieces)
     grad_out, *own, other = tokens
     return pl.pallas_call(
-        functools.partial(grads_kernel, layout, row_slot),
-        out_shape=[result] * 2,
+        functools.partial(grads_kernel, layout, row_slot, len(earlier)),
+        out_shape=[result] * 2 + [full] * (3 * len(earlier)),
         grid_spec=pltpu.PrefetchScalarGridSpec(
             num_scalar_prefetch=4,
             grid=(heads // 2,),
             in_specs=[whole] * (len(arrays) + 2)
             + [own_block(parity) for parity in range(2) for _ in range(3)]
-            + [other_block(parity, which) for parity in range(2) for which in range(3)],
-            out_specs=[pl.BlockSpec((3, LOCAL, PAIR), lambda step, *_: (0, 0, step))] * 2,
+            + [other_block(parity, which) for parity in range(2) for which in range(3)]
+            + [whole] * len(earlier),
+            out_specs=[pl.BlockSpec((3, LOCAL, PAIR), lambda step, *_: (0, 0, step))] * 2
+            + [pl.BlockSpec(memory_space=pl.ANY)] * (3 * len(earlier)),
             scratch_shapes=[
                 pltpu.VMEM((3 * SLAB, DIM), jnp.bfloat16),
                 pltpu.VMEM((2, GROUP, HEAD_DIM), jnp.bfloat16),
@@ -354,7 +389,8 @@
                 pltpu.VMEM((2, GROUP, HEAD_DIM), jnp.float32),
                 pltpu.VMEM((2, GROUP, HEAD_DIM), jnp.float32),
                 pltpu.VMEM((2, GROUP, HEAD_DIM), jnp.float32),
-            ],
+            ]
+            + [pltpu.SemaphoreType.DMA((12,))] * len(earlier),
         ),
         compiler_params=pltpu.CompilerParams(vmem_limit_bytes=VMEM),
         cost_estimate=pl.CostEstimate(
@@ -363,25 +399,14 @@
             transcendentals=0,
         ),
         name="grads",
-    )(*tables, *arrays, grad_out, probs, *own, *own, *[other] * 6)
+    )(*tables, *arrays, grad_out, probs, *own, *own, *[other] * 6, *earlier)
 
 
 def merge_kernel(plan, count, info, *refs):
     parts, outs, sems = refs[count : count + len(plan)], refs[-4:-1], refs[-1]
     copies = []
     for part, (theirs, begin, heads) in zip(parts, plan):
-        core, first = (1 - info[ME], info[THEIRS]) if theirs else (info[ME], info[MINE])
-        for step in range(heads):
-            head = core * 6 + lax.rem(first + begin + step, 6)
-            cols = pl.ds(pl.multiple_of(head * HEAD_DIM, HEAD_DIM), HEAD_DIM)
-            for index, out in enumerate(outs):
-                copies.append(
-                    pltpu.make_async_copy(
-                        part.at[index, :, step * HEAD_DIM : (step + 1) * HEAD_DIM],
-                        out.at[:, cols],
-                        sems.at[len(copies)],
-                    )
-                )
+        copies += head_copies(info, theirs, begin, heads, part, outs, sems, len(copies))
     for copy in copies:
         copy.start()
     for copy in copies:
@@ -541,10 +566,12 @@
         (2, low, before_low),
         (2, high, before_high),
     )
-    kept_late, sent_late = grads_call(tables, pieces, 4, 2, ROWS_LATE, tokens, probs_late)
+    kept_late, sent_late, *outs = grads_call(
+        tables, pieces, 4, 2, ROWS_LATE, tokens, probs_late, (kept,)
+    )
     arrived_late = swap(sent_late)
-    parts = ((False, 0, 4, kept), (False, 4, 2, kept_late), (True, 0, 4, arrived))
-    outs = merge_call(info, (), parts)
+    parts = ((False, 4, 2, kept_late), (True, 0, 4, arrived))
+    outs = merge_call(info, tuple(outs), parts)
     return tuple(merge_call(info, tuple(outs), ((True, 4, 2, arrived_late),)))
 
 

time: 101 us -> 100 us (0.990)
  waiting for transfers between devices: 8.91 us -> 7.56 us
    ppermute x11, waiting for transfers between devices: 8.9 us -> 7.44 us  [move(): return lax.ppermute(value, ('dp', 'frame'), pairs)]
    ppermute x11, starting transfers between devices: 21.9 us -> 23.1 us  [move(): return lax.ppermute(value, ('dp', 'frame'), pairs)]
    pallas_call x2, Pallas kernels: 21.2 us -> 22.3 us  [grads_call(): pl.pallas_call(functools.partial(grads_kernel, layout, row_slot, len(earl...]
    ppermute x4, starting transfers between devices: 14.6 us -> 13.5 us  [swap(): return lax.ppermute(value, 'frame', [(0, 1), (1, 0)])]
  transfers between devices with their start and end apart: 15 -> 15, of which waited for: 4 -> 4; matrix products, arithmetic and copies ran while one was open for 2% -> 2% of each run, Pallas kernels for 39% -> 40%
where the time goes in v5:
time: 100 us
  Pallas kernels  41.1 us (41%)
  starting transfers between devices  36.6 us (37%)
  blocking collectives  9.87 us (10%)
  waiting for transfers between devices  7.56 us (8%)
  local copies, waits for them, and re-layouts  3.62 us (4%)
  between operations  1.12 us (1%)
    ppermute x11, starting transfers between devices, move(): return lax.ppermute(value, ('dp', 'frame'), pairs)  23.1 us
    pallas_call x2, Pallas kernels, grads_call(): pl.pallas_call(functools.partial(grads_kernel, layout, row_slot, len(earl...  22.3 us
    ppermute x4, starting transfers between devices, swap(): return lax.ppermute(value, 'frame', [(0, 1), (1, 0)])  13.5 us
    pallas_call x2, Pallas kernels, probs_call(): pl.pallas_call(functools.partial(probs_kernel, len(passing), len(loads)),...  11.5 us
    all_to_all x1, blocking collectives, line_rows(): lax.all_to_all(jnp.broadcast_to(rows[None], (NX,) + rows.shape), 'dp', 0,...  9.87 us
    ppermute x11, waiting for transfers between devices, move(): return lax.ppermute(value, ('dp', 'frame'), pairs)  7.44 us
    pallas_call x1, Pallas kernels, other_halves(): pl.pallas_call(halves_kernel, out_shape=jax.ShapeDtypeStruct((3, LOCAL, H...  3.71 us
    pallas_call x2, Pallas kernels, merge_call(): pl.pallas_call(functools.partial(merge_kernel, plan, len(earlier)), out_s...  3.57 us
  transfers between devices with their start and end apart: 15, of which 4 were waited for; matrix products, arithmetic and copies ran while one was open for 2% of the time, Pallas kernels for 40%

profile of v5, /device:TPU:1, one launch (start us, length us, event | category | flops | bytes accessed | tf_op | source)
XLA Modules:
  0.0 100.2 jit_solution(5729478846835645933)
XLA Ops:
  0.6 3.3 %collective-permute-start.8 = (bf16[512,3072]{1,0:T(8,128)(2,1)}, bf16[512,3072]{1,0:T(8,128)(2,1)}, u32[]{:S(2)}, u32[]{:S(2)}) collective-permute-start(bf16[512,3072]{1,0:T(8,128)(2,1)} %refs_0_.3), channel_id=1, source_target_pairs={{0,1},{1,0},{2,3},{3,2},{4,5},{5,4},{6,7},{7,6},{8,9},{9,8},{10,11... | collective-permute-start | bytes 9437192 | tf_op jit(solution)/shard_map/ppermute | solution.py:503
  4.0 0.1 collective-permute-start.1
  4.1 7.4 %collective-permute-start.2 = (bf16[6,3072]{1,0:T(8,128)(2,1)}, bf16[6,3072]{1,0:T(8,128)(2,1)S(1)}, u32[]{:S(2)}, u32[]{:S(2)}) collective-permute-start(bf16[6,3072]{1,0:T(8,128)(2,1)} %param.13), channel_id=1, source_target_pairs={{0,0},{128,1},{2,2},{130,3},{4,4},{132,5},{6,6},{134,7},{32,8},{13... | collective-permute-start | bytes 110600 | tf_op jit(solution)/shard_map/ppermute | solution.py:458
  11.4 1.2 %dynamic-slice_bitcast_fusion.info = s32[6]{0:T(128)} fusion(s32[256,6]{1,0:T(8,128)} %constant.34.clone, s32[]{:T(128)S(6)} %select_n.21), kind=kLoop, calls=%fused_computation.6 | loop fusion | bytes 52 | tf_op jit(solution)/shard_map/jit(dynamic_index_in_dim)/squeeze | solution.py:538
  12.6 3.7 %halves.1 = bf16[3,512,768]{2,1,0:T(8,128)(2,1)} custom-call(s32[6]{0:T(128)} %dynamic-slice_bitcast_fusion.info, bf16[512,1536]{1,0:T(8,128)(2,1)} %refs_11_.3, bf16[512,1536]{1,0:T(8,128)(2,1)} %refs_12_.3, bf16[512,1536]{1,0:T(8,128)(2,1)} %refs_13_.1), custom_call_target="tpu_custom_call" | custom-call | tf_op jit(solution)/shard_map/halves/pallas_call | solution.py:520
  16.4 0.1 collective-permute-start
  16.5 0.0 collective-permute-done.1
  16.5 0.0 collective-permute-done.2
  16.6 0.1 copy.21
  16.6 0.2 broadcast_in_dim.2
  16.8 9.9 %all_to_all.5 = bf16[4,2,6,3072]{3,1,2,0:T(2,128)(2,1)S(1)} all-to-all(bf16[4,2,6,3072]{3,1,2,0:T(2,128)(2,1)S(1)} %broadcast_in_dim.2), channel_id=1, replica_groups={{0,2,4,6},{8,10,12,14},{16,18,20,22},{24,26,28,30},{32,34,36,38},{40,42..., dimensions={0} | all-to-all | bytes 589824 | tf_op jit(solution)/shard_map/all_to_all | solution.py:484
  26.7 0.1 copy.22
  26.7 0.1 reshape.10
  26.9 3.3 %collective-permute-start.5 = (bf16[1,48,3072]{2,1,0:T(8,128)(2,1)S(1)}, bf16[1,48,3072]{2,1,0:T(8,128)(2,1)S(1)}, u32[]{:S(2)}, u32[]{:S(2)}) collective-permute-start(bf16[1,48,3072]{2,1,0:T(8,128)(2,1)S(1)} %reshape.10), channel_id=1, source_target_pairs={{224,0},{25,1},{226,2},{27,3},{228,4},{29,5},{230,6},{31,7},{232,8... | collective-permute-start | bytes 884744 | tf_op jit(solution)/shard_map/ppermute | solution.py:458
  30.1 3.8 %collective-permute-start.6 = (bf16[1,48,3072]{2,1,0:T(8,128)(2,1)S(1)}, bf16[1,48,3072]{2,1,0:T(8,128)(2,1)S(1)}, u32[]{:S(2)}, u32[]{:S(2)}) collective-permute-start(bf16[1,48,3072]{2,1,0:T(8,128)(2,1)S(1)} %reshape.10), channel_id=1, source_target_pairs={{64,0},{17,1},{66,2},{19,3},{68,4},{21,5},{70,6},{23,7},{72,8},{25... | collective-permute-start | bytes 884744 | tf_op jit(solution)/shard_map/ppermute | solution.py:458
  34.0 1.4 %collective-permute-start.3 = (bf16[1,48,3072]{2,1,0:T(8,128)(2,1)S(1)}, bf16[1,48,3072]{2,1,0:T(8,128)(2,1)S(1)}, u32[]{:S(2)}, u32[]{:S(2)}) collective-permute-start(bf16[1,48,3072]{2,1,0:T(8,128)(2,1)S(1)} %reshape.10), channel_id=1, source_target_pairs={{32,0},{9,1},{34,2},{11,3},{36,4},{13,5},{38,6},{15,7},{40,8},{17,... | collective-permute-start | bytes 884744 | tf_op jit(solution)/shard_map/ppermute | solution.py:458
  35.3 1.7 %collective-permute-done.5 = bf16[1,48,3072]{2,1,0:T(8,128)(2,1)S(1)} collective-permute-done((bf16[1,48,3072]{2,1,0:T(8,128)(2,1)S(1)}, bf16[1,48,3072]{2,1,0:T(8,128)(2,1)S(1)}, u32[]{:S(2)}, u32[]{:S(2)}) %collective-permute-start.5) | collective-permute-done | bytes 294944 | tf_op jit(solution)/shard_map/ppermute | solution.py:458
  37.0 4.2 %collective-permute-done.6 = bf16[1,48,3072]{2,1,0:T(8,128)(2,1)S(1)} collective-permute-done((bf16[1,48,3072]{2,1,0:T(8,128)(2,1)S(1)}, bf16[1,48,3072]{2,1,0:T(8,128)(2,1)S(1)}, u32[]{:S(2)}, u32[]{:S(2)}) %collective-permute-start.6) | collective-permute-done | bytes 294944 | tf_op jit(solution)/shard_map/ppermute | solution.py:458
  41.2 0.1 pad_maximum_fusion.2
  41.3 0.0 copy-start
  41.3 0.0 copy-start.1
  41.3 0.0 copy-start.4
  41.3 0.0 copy-start.5
  41.4 0.0 copy-start.6
  41.4 0.0 copy-start.7
  41.4 1.1 %collective-permute-start.7 = (bf16[2,48,3072]{2,1,0:T(8,128)(2,1)S(1)}, bf16[2,48,3072]{2,1,0:T(8,128)(2,1)S(1)}, u32[]{:S(2)}, u32[]{:S(2)}) collective-permute-start(bf16[2,48,3072]{2,1,0:T(8,128)(2,1)S(1)} %pad_maximum_fusion.2), channel_id=1, source_target_pairs={{24,0},{225,1},{26,2},{227,3},{28,4},{229,5},{30,6},{231,7},{0,8},... | collective-permute-start | bytes 1769480 | tf_op jit(solution)/shard_map/ppermute | solution.py:458
  42.5 0.1 pad_maximum_fusion.1
  42.6 1.7 %collective-permute-start.4 = (bf16[2,48,3072]{2,1,0:T(8,128)(2,1)S(1)}, bf16[2,48,3072]{2,1,0:T(8,128)(2,1)S(1)}, u32[]{:S(2)}, u32[]{:S(2)}) collective-permute-start(bf16[2,48,3072]{2,1,0:T(8,128)(2,1)S(1)} %pad_maximum_fusion.1), channel_id=1, source_target_pairs={{8,0},{33,1},{10,2},{35,3},{12,4},{37,5},{14,6},{39,7},{16,8},{41,... | collective-permute-start | bytes 1769480 | tf_op jit(solution)/shard_map/ppermute | solution.py:458
  44.3 0.1 pad_maximum_fusion.refs_2_
  44.5 0.0 copy-start.3
  44.5 1.9 %copy-done.3 = bf16[512,3072]{1,0:T(8,128)(2,1)S(1)} copy-done((bf16[512,3072]{1,0:T(8,128)(2,1)S(1)}, bf16[512,3072]{1,0:T(8,128)(2,1)}, u32[]{:S(2)}) %copy-start.3) | copy-done | bytes 3145752
  46.4 7.3 %probs.3 = (bf16[4,3072,256]{2,1,0:T(8,128)(2,1)S(1)}, bf16[1024,3072]{1,0:T(8,128)(2,1)S(1)}, bf16[4,48,3072]{2,1,0:T(8,128)(2,1)S(1)}) custom-call(s32[6]{0:T(128)S(1)} %copy-done.4, s32[1,8]{1,0:T(1,128)S(1)} %copy-done.5, s32[1,8]{1,0:T(1,128)S(1)} %copy-done.6, s32[1,8]{1,0:T(1,128)S(1)} %copy-done.7, ...), custom_call_target="tpu_custom_call", output_to_operand_aliasing={{2}: (10, {})} | custom-call | flops 805306368 | bytes 8000000 | tf_op jit(solution)/shard_map/probs/pallas_call | solution.py:170
  53.7 0.1 fusion
  53.8 0.1 collective-permute-start.12
  53.9 0.0 copy-start.2
  53.9 2.7 %collective-permute-start.9 = (bf16[2,48,3072]{2,1,0:T(8,128)(2,1)S(1)}, bf16[2,48,3072]{2,1,0:T(8,128)(2,1)S(1)}, u32[]{:S(2)}, u32[]{:S(2)}) collective-permute-start(bf16[2,48,3072]{2,1,0:T(8,128)(2,1)S(1)} %get-tuple-element.36), channel_id=1, source_target_pairs={{8,0},{33,1},{10,2},{35,3},{12,4},{37,5},{14,6},{39,7},{16,8},{41,... | collective-permute-start | bytes 1769480 | tf_op jit(solution)/shard_map/ppermute | solution.py:458
  56.6 0.0 collective-permute-done.7.refs_1_
  56.6 4.2 %probs.2 = (bf16[2,3072,256]{2,1,0:T(8,128)(2,1)S(1)}, bf16[2,48,3072]{2,1,0:T(8,128)(2,1)S(1)}, bf16[2,48,3072]{2,1,0:T(8,128)(2,1)S(1)}) custom-call(s32[6]{0:T(128)S(1)} %copy-done.4, s32[1,8]{1,0:T(1,128)S(1)} %copy-done.5, s32[1,8]{1,0:T(1,128)S(1)} %copy-done.6, s32[1,8]{1,0:T(1,128)S(1)} %copy-done.7, ...), custom_call_target="tpu_custom_call", output_to_operand_aliasing={{1}: (8, {}), {2}: (9, {})} | custom-call | flops 402653184 | bytes 4000000 | tf_op jit(solution)/shard_map/probs/pallas_call | solution.py:170
  60.8 0.1 collective-permute-start.10
  60.9 1.4 %collective-permute-start.11 = (bf16[2,48,3072]{2,1,0:T(8,128)(2,1)S(1)}, bf16[2,48,3072]{2,1,0:T(8,128)(2,1)S(1)}, u32[]{:S(2)}, u32[]{:S(2)}) collective-permute-start(bf16[2,48,3072]{2,1,0:T(8,128)(2,1)S(1)} %get-tuple-element.21.refs_1_.refs_5_), channel_id=1, source_target_pairs={{24,0},{225,1},{26,2},{227,3},{28,4},{229,5},{30,6},{231,7},{0,8},... | collective-permute-start | bytes 1769480 | tf_op jit(solution)/shard_map/ppermute | solution.py:458
  62.3 1.5 %collective-permute-done.12.refs_0_.refs_4_ = bf16[2,48,3072]{2,1,0:T(8,128)(2,1)S(1)} collective-permute-done((bf16[2,48,3072]{2,1,0:T(8,128)(2,1)S(1)}, bf16[2,48,3072]{2,1,0:T(8,128)(2,1)S(1)}, u32[]{:S(2)}, u32[]{:S(2)}) %collective-permute-start.12) | collective-permute-done | bytes 589856 | tf_op jit(solution)/shard_map/ppermute | solution.py:458
  63.8 14.3 %grads.2 = (bf16[3,512,512]{2,1,0:T(8,128)(2,1)S(1)}, bf16[3,512,512]{2,1,0:T(8,128)(2,1)S(1)}) custom-call(s32[6]{0:T(128)S(1)} %copy-done.4, s32[1,8]{1,0:T(1,128)S(1)} %copy-done.5, s32[1,8]{1,0:T(1,128)S(1)} %copy-done.6, s32[1,8]{1,0:T(1,128)S(1)} %copy-done.7, bf16[2,48,3072]{2,1,0:T(8,128)(2,1)S(1)} %collective-permute-done.12.refs_0_.refs_4_, ...), custom_call_target="tpu_custom_call" | custom-call | flops 6442450944 | bytes 20000000 | tf_op jit(solution)/shard_map/grads/pallas_call | solution.py:369
  78.1 9.9 %collective-permute-start.13 = (bf16[3,512,512]{2,1,0:T(8,128)(2,1)S(1)}, bf16[3,512,512]{2,1,0:T(8,128)(2,1)S(1)}, u32[]{:S(2)}, u32[]{:S(2)}) collective-permute-start(bf16[3,512,512]{2,1,0:T(8,128)(2,1)S(1)} %get-tuple-element.30), channel_id=1, source_target_pairs={{0,1},{1,0},{2,3},{3,2},{4,5},{5,4},{6,7},{7,6},{8,9},{9,8},{10,11... | collective-permute-start | bytes 4718600 | tf_op jit(solution)/shard_map/ppermute | solution.py:503
  88.0 8.1 %grads.3 = (bf16[3,512,256]{2,1,0:T(8,128)(2,1)S(1)}, bf16[3,512,256]{2,1,0:T(8,128)(2,1)S(1)}, bf16[512,1536]{1,0:T(8,128)(2,1)}, bf16[512,1536]{1,0:T(8,128)(2,1)}, bf16[512,1536]{1,0:T(8,128)(2,1)}) custom-call(s32[6]{0:T(128)S(1)} %copy-done.4, s32[1,8]{1,0:T(1,128)S(1)} %copy-done.5, s32[1,8]{1,0:T(1,128)S(1)} %copy-done.6, s32[1,8]{1,0:T(1,128)S(1)} %copy-done.7, ...), custom_call_target="tpu_custom_call" | custom-call | flops 3221225472 | bytes 10000000 | tf_op jit(solution)/shard_map/grads/pallas_call | solution.py:369
  96.1 0.2 collective-permute-start.14
  96.3 2.1 %merge.2 = (bf16[512,1536]{1,0:T(8,128)(2,1)}, bf16[512,1536]{1,0:T(8,128)(2,1)}, bf16[512,1536]{1,0:T(8,128)(2,1)}) custom-call(s32[6]{0:T(128)S(1)} %copy-done.4, bf16[512,1536]{1,0:T(8,128)(2,1)} %get-tuple-element.26.refs_0_, bf16[512,1536]{1,0:T(8,128)(2,1)} %get-tuple-element.27.refs_1_, ...), custom_call_target="tpu_custom_call", output_to_operand_aliasing={{0}: (1, {}), {1}: (2, {}), {2}: (3, {})} | custom-call | tf_op jit(solution)/shard_map/merge/pallas_call | solution.py:420
  98.4 0.1 collective-permute-done.14.refs_3_
  98.5 1.5 %merge.3 = (bf16[512,1536]{1,0:T(8,128)(2,1)}, bf16[512,1536]{1,0:T(8,128)(2,1)}, bf16[512,1536]{1,0:T(8,128)(2,1)}) custom-call(s32[6]{0:T(128)S(1)} %copy-done.4, bf16[512,1536]{1,0:T(8,128)(2,1)} %get-tuple-element.31.refs_0_, bf16[512,1536]{1,0:T(8,128)(2,1)} %get-tuple-element.32.refs_1_, ...), custom_call_target="tpu_custom_call", output_to_operand_aliasing={{0}: (1, {}), {1}: (2, {}), {2}: (3, {})} | custom-call | tf_op jit(solution)/shard_map/merge/pallas_call | solution.py:420
  (17 shorter events, 0.1 us)
Async XLA Ops:
  0.6 43.8 %collective-permute-start.8 = (bf16[512,3072]{1,0:T(8,128)(2,1)}, bf16[512,3072]{1,0:T(8,128)(2,1)}, u32[]{:S(2)}, u32[]{:S(2)}) collective-permute-start(bf16[512,3072]{1,0:T(8,128)(2,1)} %refs_0_.3), channel_id=1, source_target_pairs={{0,1},{1,0},{2,3},{3,2},{4,5},{5,4},{6,7},{7,6},{8,9},{9,8},{10,11... | collective-permute-start | bytes 9437192 | tf_op jit(solution)/shard_map/ppermute | solution.py:503
  4.0 12.5 %collective-permute-start.1 = (bf16[6,3072]{1,0:T(8,128)(2,1)}, bf16[6,3072]{1,0:T(8,128)(2,1)S(1)}, u32[]{:S(2)}, u32[]{:S(2)}) collective-permute-start(bf16[6,3072]{1,0:T(8,128)(2,1)} %param.13), channel_id=1, source_target_pairs={{1,0},{129,1},{3,2},{131,3},{5,4},{133,5},{7,6},{135,7},{33,8},{13... | collective-permute-start | bytes 110600 | tf_op jit(solution)/shard_map/ppermute | solution.py:458
  4.1 12.4 %collective-permute-start.2 = (bf16[6,3072]{1,0:T(8,128)(2,1)}, bf16[6,3072]{1,0:T(8,128)(2,1)S(1)}, u32[]{:S(2)}, u32[]{:S(2)}) collective-permute-start(bf16[6,3072]{1,0:T(8,128)(2,1)} %param.13), channel_id=1, source_target_pairs={{0,0},{128,1},{2,2},{130,3},{4,4},{132,5},{6,6},{134,7},{32,8},{13... | collective-permute-start | bytes 110600 | tf_op jit(solution)/shard_map/ppermute | solution.py:458
  16.4 28.1 %collective-permute-start = (bf16[3,512,768]{2,1,0:T(8,128)(2,1)}, bf16[3,512,768]{2,1,0:T(8,128)(2,1)S(1)}, u32[]{:S(2)}, u32[]{:S(2)}) collective-permute-start(bf16[3,512,768]{2,1,0:T(8,128)(2,1)} %halves.1), channel_id=1, source_target_pairs={{0,1},{1,0},{2,3},{3,2},{4,5},{5,4},{6,7},{7,6},{8,9},{9,8},{10,11... | collective-permute-start | bytes 7077896 | tf_op jit(solution)/shard_map/ppermute | solution.py:503
  26.9 10.2 %collective-permute-start.5 = (bf16[1,48,3072]{2,1,0:T(8,128)(2,1)S(1)}, bf16[1,48,3072]{2,1,0:T(8,128)(2,1)S(1)}, u32[]{:S(2)}, u32[]{:S(2)}) collective-permute-start(bf16[1,48,3072]{2,1,0:T(8,128)(2,1)S(1)} %reshape.10), channel_id=1, source_target_pairs={{224,0},{25,1},{226,2},{27,3},{228,4},{29,5},{230,6},{31,7},{232,8... | collective-permute-start | bytes 884744 | tf_op jit(solution)/shard_map/ppermute | solution.py:458
  30.1 11.1 %collective-permute-start.6 = (bf16[1,48,3072]{2,1,0:T(8,128)(2,1)S(1)}, bf16[1,48,3072]{2,1,0:T(8,128)(2,1)S(1)}, u32[]{:S(2)}, u32[]{:S(2)}) collective-permute-start(bf16[1,48,3072]{2,1,0:T(8,128)(2,1)S(1)} %reshape.10), channel_id=1, source_target_pairs={{64,0},{17,1},{66,2},{19,3},{68,4},{21,5},{70,6},{23,7},{72,8},{25... | collective-permute-start | bytes 884744 | tf_op jit(solution)/shard_map/ppermute | solution.py:458
  34.0 8.5 %collective-permute-start.3 = (bf16[1,48,3072]{2,1,0:T(8,128)(2,1)S(1)}, bf16[1,48,3072]{2,1,0:T(8,128)(2,1)S(1)}, u32[]{:S(2)}, u32[]{:S(2)}) collective-permute-start(bf16[1,48,3072]{2,1,0:T(8,128)(2,1)S(1)} %reshape.10), channel_id=1, source_target_pairs={{32,0},{9,1},{34,2},{11,3},{36,4},{13,5},{38,6},{15,7},{40,8},{17,... | collective-permute-start | bytes 884744 | tf_op jit(solution)/shard_map/ppermute | solution.py:458
  41.3 3.1 %copy-start = (bf16[512,1536]{1,0:T(8,128)(2,1)S(1)}, bf16[512,1536]{1,0:T(8,128)(2,1)}, u32[]{:S(2)}) copy-start(bf16[512,1536]{1,0:T(8,128)(2,1)} %refs_11_.3) | copy-start | bytes 4718596
  41.3 3.1 %copy-start.1 = (bf16[512,1536]{1,0:T(8,128)(2,1)S(1)}, bf16[512,1536]{1,0:T(8,128)(2,1)}, u32[]{:S(2)}) copy-start(bf16[512,1536]{1,0:T(8,128)(2,1)} %refs_12_.3) | copy-start | bytes 4718596
  41.3 3.1 %copy-start.4 = (s32[6]{0:T(128)S(1)}, s32[6]{0:T(128)}, u32[]{:S(2)}) copy-start(s32[6]{0:T(128)} %dynamic-slice_bitcast_fusion.info) | copy-start | bytes 76
  41.3 3.1 %copy-start.5 = (s32[1,8]{1,0:T(1,128)S(1)}, s32[1,8]{1,0:T(1,128)}, u32[]{:S(2)}) copy-start(s32[1,8]{1,0:T(1,128)} %clips.7) | copy-start | bytes 100
  41.4 3.1 %copy-start.6 = (s32[1,8]{1,0:T(1,128)S(1)}, s32[1,8]{1,0:T(1,128)}, u32[]{:S(2)}) copy-start(s32[1,8]{1,0:T(1,128)} %valid_rows.7) | copy-start | bytes 100
  41.4 3.1 %copy-start.7 = (s32[1,8]{1,0:T(1,128)S(1)}, s32[1,8]{1,0:T(1,128)}, u32[]{:S(2)}) copy-start(s32[1,8]{1,0:T(1,128)} %valid_cols.7) | copy-start | bytes 100
  41.4 15.2 %collective-permute-start.7 = (bf16[2,48,3072]{2,1,0:T(8,128)(2,1)S(1)}, bf16[2,48,3072]{2,1,0:T(8,128)(2,1)S(1)}, u32[]{:S(2)}, u32[]{:S(2)}) collective-permute-start(bf16[2,48,3072]{2,1,0:T(8,128)(2,1)S(1)} %pad_maximum_fusion.2), channel_id=1, source_target_pairs={{24,0},{225,1},{26,2},{227,3},{28,4},{229,5},{30,6},{231,7},{0,8},... | collective-permute-start | bytes 1769480 | tf_op jit(solution)/shard_map/ppermute | solution.py:458
  42.6 14.0 %collective-permute-start.4 = (bf16[2,48,3072]{2,1,0:T(8,128)(2,1)S(1)}, bf16[2,48,3072]{2,1,0:T(8,128)(2,1)S(1)}, u32[]{:S(2)}, u32[]{:S(2)}) collective-permute-start(bf16[2,48,3072]{2,1,0:T(8,128)(2,1)S(1)} %pad_maximum_fusion.1), channel_id=1, source_target_pairs={{8,0},{33,1},{10,2},{35,3},{12,4},{37,5},{14,6},{39,7},{16,8},{41,... | collective-permute-start | bytes 1769480 | tf_op jit(solution)/shard_map/ppermute | solution.py:458
  44.5 1.9 %copy-start.3 = (bf16[512,3072]{1,0:T(8,128)(2,1)S(1)}, bf16[512,3072]{1,0:T(8,128)(2,1)}, u32[]{:S(2)}) copy-start(bf16[512,3072]{1,0:T(8,128)(2,1)} %refs_0_.3) | copy-start | bytes 9437188
  53.8 10.0 %collective-permute-start.12 = (bf16[2,48,3072]{2,1,0:T(8,128)(2,1)S(1)}, bf16[2,48,3072]{2,1,0:T(8,128)(2,1)S(1)}, u32[]{:S(2)}, u32[]{:S(2)}) collective-permute-start(bf16[2,48,3072]{2,1,0:T(8,128)(2,1)S(1)} %get-tuple-element.35), channel_id=1, source_target_pairs={{24,0},{225,1},{26,2},{227,3},{28,4},{229,5},{30,6},{231,7},{0,8},... | collective-permute-start | bytes 1769480 | tf_op jit(solution)/shard_map/ppermute | solution.py:458
  53.9 9.9 %copy-start.2 = (bf16[512,1536]{1,0:T(8,128)(2,1)S(1)}, bf16[512,1536]{1,0:T(8,128)(2,1)}, u32[]{:S(2)}) copy-start(bf16[512,1536]{1,0:T(8,128)(2,1)} %refs_13_.1) | copy-start | bytes 4718596
  53.9 9.9 %collective-permute-start.9 = (bf16[2,48,3072]{2,1,0:T(8,128)(2,1)S(1)}, bf16[2,48,3072]{2,1,0:T(8,128)(2,1)S(1)}, u32[]{:S(2)}, u32[]{:S(2)}) collective-permute-start(bf16[2,48,3072]{2,1,0:T(8,128)(2,1)S(1)} %get-tuple-element.36), channel_id=1, source_target_pairs={{8,0},{33,1},{10,2},{35,3},{12,4},{37,5},{14,6},{39,7},{16,8},{41,... | collective-permute-start | bytes 1769480 | tf_op jit(solution)/shard_map/ppermute | solution.py:458
  60.8 27.3 %collective-permute-start.10 = (bf16[2,48,3072]{2,1,0:T(8,128)(2,1)S(1)}, bf16[2,48,3072]{2,1,0:T(8,128)(2,1)S(1)}, u32[]{:S(2)}, u32[]{:S(2)}) collective-permute-start(bf16[2,48,3072]{2,1,0:T(8,128)(2,1)S(1)} %get-tuple-element.19.refs_3_.refs_0_), channel_id=1, source_target_pairs={{8,0},{33,1},{10,2},{35,3},{12,4},{37,5},{14,6},{39,7},{16,8},{41,... | collective-permute-start | bytes 1769480 | tf_op jit(solution)/shard_map/ppermute | solution.py:458
  60.9 27.2 %collective-permute-start.11 = (bf16[2,48,3072]{2,1,0:T(8,128)(2,1)S(1)}, bf16[2,48,3072]{2,1,0:T(8,128)(2,1)S(1)}, u32[]{:S(2)}, u32[]{:S(2)}) collective-permute-start(bf16[2,48,3072]{2,1,0:T(8,128)(2,1)S(1)} %get-tuple-element.21.refs_1_.refs_5_), channel_id=1, source_target_pairs={{24,0},{225,1},{26,2},{227,3},{28,4},{229,5},{30,6},{231,7},{0,8},... | collective-permute-start | bytes 1769480 | tf_op jit(solution)/shard_map/ppermute | solution.py:458
  78.1 18.2 %collective-permute-start.13 = (bf16[3,512,512]{2,1,0:T(8,128)(2,1)S(1)}, bf16[3,512,512]{2,1,0:T(8,128)(2,1)S(1)}, u32[]{:S(2)}, u32[]{:S(2)}) collective-permute-start(bf16[3,512,512]{2,1,0:T(8,128)(2,1)S(1)} %get-tuple-element.30), channel_id=1, source_target_pairs={{0,1},{1,0},{2,3},{3,2},{4,5},{5,4},{6,7},{7,6},{8,9},{9,8},{10,11... | collective-permute-start | bytes 4718600 | tf_op jit(solution)/shard_map/ppermute | solution.py:503
  96.1 2.4 %collective-permute-start.14 = (bf16[3,512,256]{2,1,0:T(8,128)(2,1)S(1)}, bf16[3,512,256]{2,1,0:T(8,128)(2,1)S(1)}, u32[]{:S(2)}, u32[]{:S(2)}) collective-permute-start(bf16[3,512,256]{2,1,0:T(8,128)(2,1)S(1)} %get-tuple-element.34), channel_id=1, source_target_pairs={{0,1},{1,0},{2,3},{3,2},{4,5},{5,4},{6,7},{7,6},{8,9},{9,8},{10,11... | collective-permute-start | bytes 2359304 | tf_op jit(solution)/shard_map/ppermute | solution.py:503

commit v6 on v5

--- a/solution.py
+++ b/solution.py
@@ -503,9 +503,9 @@
     return lax.ppermute(value, "frame", [(0, 1), (1, 0)])
 
 
-def halves_kernel(info, *refs):
+def halves_kernel(*refs):
     values, out, sems = refs[:3], refs[3], refs[4]
-    cols = pl.ds(pl.multiple_of((1 - info[ME]) * HALF, HALF), HALF)
+    cols = pl.ds(pl.multiple_of((1 - lax.axis_index("frame")) * HALF, HALF), HALF)
     copies = [
         pltpu.make_async_copy(value.at[:, cols], out.at[index], sems.at[index])
         for index, value in enumerate(values)
@@ -516,20 +516,16 @@
         copy.wait()
 
 
-def other_halves(info, values):
+def other_halves(values):
     return pl.pallas_call(
         halves_kernel,
         out_shape=jax.ShapeDtypeStruct((3, LOCAL, HALF), jnp.bfloat16),
-        grid_spec=pltpu.PrefetchScalarGridSpec(
-            num_scalar_prefetch=1,
-            grid=(1,),
-            in_specs=[pl.BlockSpec(memory_space=pl.ANY)] * 3,
-            out_specs=pl.BlockSpec(memory_space=pltpu.VMEM),
-            scratch_shapes=[pltpu.SemaphoreType.DMA((3,))],
-        ),
+        in_specs=[pl.BlockSpec(memory_space=pl.ANY)] * 3,
+        out_specs=pl.BlockSpec(memory_space=pltpu.VMEM),
+        scratch_shapes=[pltpu.SemaphoreType.DMA((3,))],
         compiler_params=pltpu.CompilerParams(vmem_limit_bytes=60 * 1024 * 1024),
         name="halves",
-    )(info, *values)
+    )(*values)
 
 
 def on_device(queries, keys, values, grad_out, out_weight, frame_clip, frame_rows, frame_cols):
@@ -538,7 +534,7 @@
     info = lax.dynamic_index_in_dim(jnp.asarray(place_table()), dp * 2 + me, 0, keepdims=False)
     tables = (info, frame_clip, frame_rows, frame_cols)
     g_other = swap(grad_out)
-    others = swap(other_halves(info, (queries, keys, values)))
+    others = swap(other_halves((queries, keys, values)))
     rows = line_rows(out_weight, dp // (NY * NX))
     slab = jnp.concatenate([rows] + beside_rows(rows))
     after_low, before_high = move(slab[:2], along(True, 1)), move(slab[2:], along(True, -1))

time: 100 us -> 99.7 us (level)
  starting transfers between devices: 36.6 us -> 37.7 us
    ppermute x4, starting transfers between devices: 13.5 us -> 15.5 us  [swap(): return lax.ppermute(value, 'frame', [(0, 1), (1, 0)])]
  transfers between devices with their start and end apart: 15 -> 15, of which waited for: 4 -> 4; matrix products, arithmetic and copies ran while one was open for 2% -> 1% of each run, Pallas kernels for 40% -> 39%
where the time goes in v6:
time: 99.7 us; the launch traced here: 99.4 us
  Pallas kernels  40.5 us (41%)
  starting transfers between devices  37.7 us (38%)
  blocking collectives  9.87 us (10%)
  waiting for transfers between devices  6.87 us (7%)
  local copies, waits for them, and re-layouts  3.1 us (3%)
  between operations  1.1 us (1%)
    pallas_call x2, Pallas kernels, grads_call(): pl.pallas_call(functools.partial(grads_kernel, layout, row_slot, len(earl...  22.3 us
    ppermute x11, starting transfers between devices, move(): return lax.ppermute(value, ('dp', 'frame'), pairs)  22.2 us
    ppermute x4, starting transfers between devices, swap(): return lax.ppermute(value, 'frame', [(0, 1), (1, 0)])  15.5 us
    pallas_call x2, Pallas kernels, probs_call(): pl.pallas_call(functools.partial(probs_kernel, len(passing), len(loads)),...  11.5 us
    all_to_all x1, blocking collectives, line_rows(): lax.all_to_all(jnp.broadcast_to(rows[None], (NX,) + rows.shape), 'dp', 0,...  9.87 us
    ppermute x11, waiting for transfers between devices, move(): return lax.ppermute(value, ('dp', 'frame'), pairs)  6.74 us
    pallas_call x2, Pallas kernels, merge_call(): pl.pallas_call(functools.partial(merge_kernel, plan, len(earlier)), out_s...  3.57 us
    pallas_call x1, Pallas kernels, other_halves(): pl.pallas_call(halves_kernel, out_shape=jax.ShapeDtypeStruct((3, LOCAL, H...  3.05 us
  transfers between devices with their start and end apart: 15, of which 4 were waited for; matrix products, arithmetic and copies ran while one was open for 1% of the time, Pallas kernels for 39%

profile of v6, /device:TPU:1, one launch (start us, length us, event | category | flops | bytes accessed | tf_op | source)
XLA Modules:
  0.0 99.4 jit_solution(575033106708256756)
XLA Ops:
  0.6 3.3 %collective-permute-start.8 = (bf16[512,3072]{1,0:T(8,128)(2,1)}, bf16[512,3072]{1,0:T(8,128)(2,1)}, u32[]{:S(2)}, u32[]{:S(2)}) collective-permute-start(bf16[512,3072]{1,0:T(8,128)(2,1)} %refs_0_.3), channel_id=1, source_target_pairs={{0,1},{1,0},{2,3},{3,2},{4,5},{5,4},{6,7},{7,6},{8,9},{9,8},{10,11... | collective-permute-start | bytes 9437192 | tf_op jit(solution)/shard_map/ppermute | solution.py:503
  4.0 0.1 collective-permute-start.1
  4.1 7.4 %collective-permute-start.2 = (bf16[6,3072]{1,0:T(8,128)(2,1)}, bf16[6,3072]{1,0:T(8,128)(2,1)S(1)}, u32[]{:S(2)}, u32[]{:S(2)}) collective-permute-start(bf16[6,3072]{1,0:T(8,128)(2,1)} %param.13), channel_id=1, source_target_pairs={{0,0},{128,1},{2,2},{130,3},{4,4},{132,5},{6,6},{134,7},{32,8},{13... | collective-permute-start | bytes 110600 | tf_op jit(solution)/shard_map/ppermute | solution.py:458
  11.4 3.0 %halves.1 = bf16[3,512,768]{2,1,0:T(8,128)(2,1)} custom-call(bf16[512,1536]{1,0:T(8,128)(2,1)} %refs_11_.3, bf16[512,1536]{1,0:T(8,128)(2,1)} %refs_12_.3, bf16[512,1536]{1,0:T(8,128)(2,1)} %refs_13_.1), custom_call_target="tpu_custom_call" | custom-call | tf_op jit(solution)/shard_map/halves/pallas_call | solution.py:520
  14.5 0.1 collective-permute-start
  14.6 0.0 collective-permute-done.1
  14.6 0.0 collective-permute-done.2
  14.7 0.1 copy.21
  14.8 0.2 broadcast_in_dim.2
  14.9 9.9 %all_to_all.5 = bf16[4,2,6,3072]{3,1,2,0:T(2,128)(2,1)S(1)} all-to-all(bf16[4,2,6,3072]{3,1,2,0:T(2,128)(2,1)S(1)} %broadcast_in_dim.2), channel_id=1, replica_groups={{0,2,4,6},{8,10,12,14},{16,18,20,22},{24,26,28,30},{32,34,36,38},{40,42..., dimensions={0} | all-to-all | bytes 589824 | tf_op jit(solution)/shard_map/all_to_all | solution.py:484
  24.8 0.1 copy.22
  24.9 0.1 reshape.10
  25.0 3.3 %collective-permute-start.5 = (bf16[1,48,3072]{2,1,0:T(8,128)(2,1)S(1)}, bf16[1,48,3072]{2,1,0:T(8,128)(2,1)S(1)}, u32[]{:S(2)}, u32[]{:S(2)}) collective-permute-start(bf16[1,48,3072]{2,1,0:T(8,128)(2,1)S(1)} %reshape.10), channel_id=1, source_target_pairs={{224,0},{25,1},{226,2},{27,3},{228,4},{29,5},{230,6},{31,7},{232,8... | collective-permute-start | bytes 884744 | tf_op jit(solution)/shard_map/ppermute | solution.py:458
  28.3 3.0 %collective-permute-start.6 = (bf16[1,48,3072]{2,1,0:T(8,128)(2,1)S(1)}, bf16[1,48,3072]{2,1,0:T(8,128)(2,1)S(1)}, u32[]{:S(2)}, u32[]{:S(2)}) collective-permute-start(bf16[1,48,3072]{2,1,0:T(8,128)(2,1)S(1)} %reshape.10), channel_id=1, source_target_pairs={{64,0},{17,1},{66,2},{19,3},{68,4},{21,5},{70,6},{23,7},{72,8},{25... | collective-permute-start | bytes 884744 | tf_op jit(solution)/shard_map/ppermute | solution.py:458
  31.2 0.7 dynamic-slice_bitcast_fusion.info
  31.9 1.4 %collective-permute-start.3 = (bf16[1,48,3072]{2,1,0:T(8,128)(2,1)S(1)}, bf16[1,48,3072]{2,1,0:T(8,128)(2,1)S(1)}, u32[]{:S(2)}, u32[]{:S(2)}) collective-permute-start(bf16[1,48,3072]{2,1,0:T(8,128)(2,1)S(1)} %reshape.10), channel_id=1, source_target_pairs={{32,0},{9,1},{34,2},{11,3},{36,4},{13,5},{38,6},{15,7},{40,8},{17,... | collective-permute-start | bytes 884744 | tf_op jit(solution)/shard_map/ppermute | solution.py:458
  33.3 1.2 %collective-permute-done.5 = bf16[1,48,3072]{2,1,0:T(8,128)(2,1)S(1)} collective-permute-done((bf16[1,48,3072]{2,1,0:T(8,128)(2,1)S(1)}, bf16[1,48,3072]{2,1,0:T(8,128)(2,1)S(1)}, u32[]{:S(2)}, u32[]{:S(2)}) %collective-permute-start.5) | collective-permute-done | bytes 294944 | tf_op jit(solution)/shard_map/ppermute | solution.py:458
  34.5 4.0 %collective-permute-done.6 = bf16[1,48,3072]{2,1,0:T(8,128)(2,1)S(1)} collective-permute-done((bf16[1,48,3072]{2,1,0:T(8,128)(2,1)S(1)}, bf16[1,48,3072]{2,1,0:T(8,128)(2,1)S(1)}, u32[]{:S(2)}, u32[]{:S(2)}) %collective-permute-start.6) | collective-permute-done | bytes 294944 | tf_op jit(solution)/shard_map/ppermute | solution.py:458
  38.5 0.1 pad_maximum_fusion.2
  38.6 0.0 copy-start
  38.6 0.0 copy-start.1
  38.6 0.0 copy-start.4
  38.6 0.0 copy-start.5
  38.6 0.0 copy-start.6
  38.6 1.1 %collective-permute-start.7 = (bf16[2,48,3072]{2,1,0:T(8,128)(2,1)S(1)}, bf16[2,48,3072]{2,1,0:T(8,128)(2,1)S(1)}, u32[]{:S(2)}, u32[]{:S(2)}) collective-permute-start(bf16[2,48,3072]{2,1,0:T(8,128)(2,1)S(1)} %pad_maximum_fusion.2), channel_id=1, source_target_pairs={{24,0},{225,1},{26,2},{227,3},{28,4},{229,5},{30,6},{231,7},{0,8},... | collective-permute-start | bytes 1769480 | tf_op jit(solution)/shard_map/ppermute | solution.py:458
  39.7 0.0 collective-permute-done.3
  39.7 0.1 pad_maximum_fusion.1
  39.8 1.7 %collective-permute-start.4 = (bf16[2,48,3072]{2,1,0:T(8,128)(2,1)S(1)}, bf16[2,48,3072]{2,1,0:T(8,128)(2,1)S(1)}, u32[]{:S(2)}, u32[]{:S(2)}) collective-permute-start(bf16[2,48,3072]{2,1,0:T(8,128)(2,1)S(1)} %pad_maximum_fusion.1), channel_id=1, source_target_pairs={{8,0},{33,1},{10,2},{35,3},{12,4},{37,5},{14,6},{39,7},{16,8},{41,... | collective-permute-start | bytes 1769480 | tf_op jit(solution)/shard_map/ppermute | solution.py:458
  41.5 0.1 pad_maximum_fusion.refs_2_
  41.7 0.0 collective-permute-done.q_other.k_other.refs_13_.refs_14_.refs_15_.refs_16_.refs_17_.refs_18_.refs_19_
  41.7 0.0 copy-start.3
  41.8 1.9 %copy-done.3 = bf16[512,3072]{1,0:T(8,128)(2,1)S(1)} copy-done((bf16[512,3072]{1,0:T(8,128)(2,1)S(1)}, bf16[512,3072]{1,0:T(8,128)(2,1)}, u32[]{:S(2)}) %copy-start.3) | copy-done | bytes 3145752
  43.6 7.3 %probs.3 = (bf16[4,3072,256]{2,1,0:T(8,128)(2,1)S(1)}, bf16[1024,3072]{1,0:T(8,128)(2,1)S(1)}, bf16[4,48,3072]{2,1,0:T(8,128)(2,1)S(1)}) custom-call(s32[6]{0:T(128)S(1)} %dynamic-slice_bitcast_fusion.info, s32[1,8]{1,0:T(1,128)S(1)} %copy-done.4, s32[1,8]{1,0:T(1,128)S(1)} %copy-done.5, s32[1,8]{1,0:T(1,128)S(1)} %copy-done.6, ...), custom_call_target="tpu_custom_call", output_to_operand_aliasing={{2}: (10, {})} | custom-call | flops 805306368 | bytes 8000000 | tf_op jit(solution)/shard_map/probs/pallas_call | solution.py:170
  51.0 0.1 fusion
  51.1 0.1 collective-permute-start.12
  51.1 0.0 copy-start.2
  51.2 2.7 %collective-permute-start.9 = (bf16[2,48,3072]{2,1,0:T(8,128)(2,1)S(1)}, bf16[2,48,3072]{2,1,0:T(8,128)(2,1)S(1)}, u32[]{:S(2)}, u32[]{:S(2)}) collective-permute-start(bf16[2,48,3072]{2,1,0:T(8,128)(2,1)S(1)} %get-tuple-element.36), channel_id=1, source_target_pairs={{8,0},{33,1},{10,2},{35,3},{12,4},{37,5},{14,6},{39,7},{16,8},{41,... | collective-permute-start | bytes 1769480 | tf_op jit(solution)/shard_map/ppermute | solution.py:458
  53.8 4.2 %probs.2 = (bf16[2,3072,256]{2,1,0:T(8,128)(2,1)S(1)}, bf16[2,48,3072]{2,1,0:T(8,128)(2,1)S(1)}, bf16[2,48,3072]{2,1,0:T(8,128)(2,1)S(1)}) custom-call(s32[6]{0:T(128)S(1)} %dynamic-slice_bitcast_fusion.info, s32[1,8]{1,0:T(1,128)S(1)} %copy-done.4, s32[1,8]{1,0:T(1,128)S(1)} %copy-done.5, ...), custom_call_target="tpu_custom_call", output_to_operand_aliasing={{1}: (8, {}), {2}: (9, {})} | custom-call | flops 402653184 | bytes 4000000 | tf_op jit(solution)/shard_map/probs/pallas_call | solution.py:170
  58.0 0.1 collective-permute-start.10
  58.1 1.4 %collective-permute-start.11 = (bf16[2,48,3072]{2,1,0:T(8,128)(2,1)S(1)}, bf16[2,48,3072]{2,1,0:T(8,128)(2,1)S(1)}, u32[]{:S(2)}, u32[]{:S(2)}) collective-permute-start(bf16[2,48,3072]{2,1,0:T(8,128)(2,1)S(1)} %get-tuple-element.21.refs_1_.refs_5_), channel_id=1, source_target_pairs={{24,0},{225,1},{26,2},{227,3},{28,4},{229,5},{30,6},{231,7},{0,8},... | collective-permute-start | bytes 1769480 | tf_op jit(solution)/shard_map/ppermute | solution.py:458
  59.6 1.5 %collective-permute-done.12.refs_0_.refs_4_ = bf16[2,48,3072]{2,1,0:T(8,128)(2,1)S(1)} collective-permute-done((bf16[2,48,3072]{2,1,0:T(8,128)(2,1)S(1)}, bf16[2,48,3072]{2,1,0:T(8,128)(2,1)S(1)}, u32[]{:S(2)}, u32[]{:S(2)}) %collective-permute-start.12) | collective-permute-done | bytes 589856 | tf_op jit(solution)/shard_map/ppermute | solution.py:458
  61.1 14.3 %grads.2 = (bf16[3,512,512]{2,1,0:T(8,128)(2,1)S(1)}, bf16[3,512,512]{2,1,0:T(8,128)(2,1)S(1)}) custom-call(s32[6]{0:T(128)S(1)} %dynamic-slice_bitcast_fusion.info, s32[1,8]{1,0:T(1,128)S(1)} %copy-done.4, s32[1,8]{1,0:T(1,128)S(1)} %copy-done.5, s32[1,8]{1,0:T(1,128)S(1)} %copy-done.6, bf16[2,48,3072]{2,1,0:T(8,128)(2,1)S(1)} %collective-permute-done.12.refs_0_.refs_4_, ...), custom_call_target="tpu_custom_call" | custom-call | flops 6442450944 | bytes 20000000 | tf_op jit(solution)/shard_map/grads/pallas_call | solution.py:369
  75.4 11.9 %collective-permute-start.13 = (bf16[3,512,512]{2,1,0:T(8,128)(2,1)S(1)}, bf16[3,512,512]{2,1,0:T(8,128)(2,1)S(1)}, u32[]{:S(2)}, u32[]{:S(2)}) collective-permute-start(bf16[3,512,512]{2,1,0:T(8,128)(2,1)S(1)} %get-tuple-element.30), channel_id=1, source_target_pairs={{0,1},{1,0},{2,3},{3,2},{4,5},{5,4},{6,7},{7,6},{8,9},{9,8},{10,11... | collective-permute-start | bytes 4718600 | tf_op jit(solution)/shard_map/ppermute | solution.py:503
  87.2 8.1 %grads.3 = (bf16[3,512,256]{2,1,0:T(8,128)(2,1)S(1)}, bf16[3,512,256]{2,1,0:T(8,128)(2,1)S(1)}, bf16[512,1536]{1,0:T(8,128)(2,1)}, bf16[512,1536]{1,0:T(8,128)(2,1)}, bf16[512,1536]{1,0:T(8,128)(2,1)}) custom-call(s32[6]{0:T(128)S(1)} %dynamic-slice_bitcast_fusion.info, s32[1,8]{1,0:T(1,128)S(1)} %copy-done.4, s32[1,8]{1,0:T(1,128)S(1)} %copy-done.5, ...), custom_call_target="tpu_custom_call" | custom-call | flops 3221225472 | bytes 10000000 | tf_op jit(solution)/shard_map/grads/pallas_call | solution.py:369
  95.3 0.2 collective-permute-start.14
  95.5 2.1 %merge.2 = (bf16[512,1536]{1,0:T(8,128)(2,1)}, bf16[512,1536]{1,0:T(8,128)(2,1)}, bf16[512,1536]{1,0:T(8,128)(2,1)}) custom-call(s32[6]{0:T(128)S(1)} %dynamic-slice_bitcast_fusion.info, bf16[512,1536]{1,0:T(8,128)(2,1)} %get-tuple-element.26.refs_0_, ...), custom_call_target="tpu_custom_call", output_to_operand_aliasing={{0}: (1, {}), {1}: (2, {}), {2}: (3, {})} | custom-call | tf_op jit(solution)/shard_map/merge/pallas_call | solution.py:420
  97.6 0.1 collective-permute-done.14.refs_3_
  97.7 1.5 %merge.3 = (bf16[512,1536]{1,0:T(8,128)(2,1)}, bf16[512,1536]{1,0:T(8,128)(2,1)}, bf16[512,1536]{1,0:T(8,128)(2,1)}) custom-call(s32[6]{0:T(128)S(1)} %dynamic-slice_bitcast_fusion.info, bf16[512,1536]{1,0:T(8,128)(2,1)} %get-tuple-element.31.refs_0_, ...), custom_call_target="tpu_custom_call", output_to_operand_aliasing={{0}: (1, {}), {1}: (2, {}), {2}: (3, {})} | custom-call | tf_op jit(solution)/shard_map/merge/pallas_call | solution.py:420
  (15 shorter events, 0.1 us)
Async XLA Ops:
  0.6 41.1 %collective-permute-start.8 = (bf16[512,3072]{1,0:T(8,128)(2,1)}, bf16[512,3072]{1,0:T(8,128)(2,1)}, u32[]{:S(2)}, u32[]{:S(2)}) collective-permute-start(bf16[512,3072]{1,0:T(8,128)(2,1)} %refs_0_.3), channel_id=1, source_target_pairs={{0,1},{1,0},{2,3},{3,2},{4,5},{5,4},{6,7},{7,6},{8,9},{9,8},{10,11... | collective-permute-start | bytes 9437192 | tf_op jit(solution)/shard_map/ppermute | solution.py:503
  4.0 10.6 %collective-permute-start.1 = (bf16[6,3072]{1,0:T(8,128)(2,1)}, bf16[6,3072]{1,0:T(8,128)(2,1)S(1)}, u32[]{:S(2)}, u32[]{:S(2)}) collective-permute-start(bf16[6,3072]{1,0:T(8,128)(2,1)} %param.13), channel_id=1, source_target_pairs={{1,0},{129,1},{3,2},{131,3},{5,4},{133,5},{7,6},{135,7},{33,8},{13... | collective-permute-start | bytes 110600 | tf_op jit(solution)/shard_map/ppermute | solution.py:458
  4.1 10.6 %collective-permute-start.2 = (bf16[6,3072]{1,0:T(8,128)(2,1)}, bf16[6,3072]{1,0:T(8,128)(2,1)S(1)}, u32[]{:S(2)}, u32[]{:S(2)}) collective-permute-start(bf16[6,3072]{1,0:T(8,128)(2,1)} %param.13), channel_id=1, source_target_pairs={{0,0},{128,1},{2,2},{130,3},{4,4},{132,5},{6,6},{134,7},{32,8},{13... | collective-permute-start | bytes 110600 | tf_op jit(solution)/shard_map/ppermute | solution.py:458
  14.5 27.2 %collective-permute-start = (bf16[3,512,768]{2,1,0:T(8,128)(2,1)}, bf16[3,512,768]{2,1,0:T(8,128)(2,1)S(1)}, u32[]{:S(2)}, u32[]{:S(2)}) collective-permute-start(bf16[3,512,768]{2,1,0:T(8,128)(2,1)} %halves.1), channel_id=1, source_target_pairs={{0,1},{1,0},{2,3},{3,2},{4,5},{5,4},{6,7},{7,6},{8,9},{9,8},{10,11... | collective-permute-start | bytes 7077896 | tf_op jit(solution)/shard_map/ppermute | solution.py:503
  25.0 9.5 %collective-permute-start.5 = (bf16[1,48,3072]{2,1,0:T(8,128)(2,1)S(1)}, bf16[1,48,3072]{2,1,0:T(8,128)(2,1)S(1)}, u32[]{:S(2)}, u32[]{:S(2)}) collective-permute-start(bf16[1,48,3072]{2,1,0:T(8,128)(2,1)S(1)} %reshape.10), channel_id=1, source_target_pairs={{224,0},{25,1},{226,2},{27,3},{228,4},{29,5},{230,6},{31,7},{232,8... | collective-permute-start | bytes 884744 | tf_op jit(solution)/shard_map/ppermute | solution.py:458
  28.3 10.2 %collective-permute-start.6 = (bf16[1,48,3072]{2,1,0:T(8,128)(2,1)S(1)}, bf16[1,48,3072]{2,1,0:T(8,128)(2,1)S(1)}, u32[]{:S(2)}, u32[]{:S(2)}) collective-permute-start(bf16[1,48,3072]{2,1,0:T(8,128)(2,1)S(1)} %reshape.10), channel_id=1, source_target_pairs={{64,0},{17,1},{66,2},{19,3},{68,4},{21,5},{70,6},{23,7},{72,8},{25... | collective-permute-start | bytes 884744 | tf_op jit(solution)/shard_map/ppermute | solution.py:458
  31.9 7.8 %collective-permute-start.3 = (bf16[1,48,3072]{2,1,0:T(8,128)(2,1)S(1)}, bf16[1,48,3072]{2,1,0:T(8,128)(2,1)S(1)}, u32[]{:S(2)}, u32[]{:S(2)}) collective-permute-start(bf16[1,48,3072]{2,1,0:T(8,128)(2,1)S(1)} %reshape.10), channel_id=1, source_target_pairs={{32,0},{9,1},{34,2},{11,3},{36,4},{13,5},{38,6},{15,7},{40,8},{17,... | collective-permute-start | bytes 884744 | tf_op jit(solution)/shard_map/ppermute | solution.py:458
  38.6 3.1 %copy-start = (bf16[512,1536]{1,0:T(8,128)(2,1)S(1)}, bf16[512,1536]{1,0:T(8,128)(2,1)}, u32[]{:S(2)}) copy-start(bf16[512,1536]{1,0:T(8,128)(2,1)} %refs_11_.3) | copy-start | bytes 4718596
  38.6 3.1 %copy-start.1 = (bf16[512,1536]{1,0:T(8,128)(2,1)S(1)}, bf16[512,1536]{1,0:T(8,128)(2,1)}, u32[]{:S(2)}) copy-start(bf16[512,1536]{1,0:T(8,128)(2,1)} %refs_12_.3) | copy-start | bytes 4718596
  38.6 3.1 %copy-start.4 = (s32[1,8]{1,0:T(1,128)S(1)}, s32[1,8]{1,0:T(1,128)}, u32[]{:S(2)}) copy-start(s32[1,8]{1,0:T(1,128)} %clips.7) | copy-start | bytes 100
  38.6 3.1 %copy-start.5 = (s32[1,8]{1,0:T(1,128)S(1)}, s32[1,8]{1,0:T(1,128)}, u32[]{:S(2)}) copy-start(s32[1,8]{1,0:T(1,128)} %valid_rows.7) | copy-start | bytes 100
  38.6 3.1 %copy-start.6 = (s32[1,8]{1,0:T(1,128)S(1)}, s32[1,8]{1,0:T(1,128)}, u32[]{:S(2)}) copy-start(s32[1,8]{1,0:T(1,128)} %valid_cols.7) | copy-start | bytes 100
  38.6 15.2 %collective-permute-start.7 = (bf16[2,48,3072]{2,1,0:T(8,128)(2,1)S(1)}, bf16[2,48,3072]{2,1,0:T(8,128)(2,1)S(1)}, u32[]{:S(2)}, u32[]{:S(2)}) collective-permute-start(bf16[2,48,3072]{2,1,0:T(8,128)(2,1)S(1)} %pad_maximum_fusion.2), channel_id=1, source_target_pairs={{24,0},{225,1},{26,2},{227,3},{28,4},{229,5},{30,6},{231,7},{0,8},... | collective-permute-start | bytes 1769480 | tf_op jit(solution)/shard_map/ppermute | solution.py:458
  39.8 14.0 %collective-permute-start.4 = (bf16[2,48,3072]{2,1,0:T(8,128)(2,1)S(1)}, bf16[2,48,3072]{2,1,0:T(8,128)(2,1)S(1)}, u32[]{:S(2)}, u32[]{:S(2)}) collective-permute-start(bf16[2,48,3072]{2,1,0:T(8,128)(2,1)S(1)} %pad_maximum_fusion.1), channel_id=1, source_target_pairs={{8,0},{33,1},{10,2},{35,3},{12,4},{37,5},{14,6},{39,7},{16,8},{41,... | collective-permute-start | bytes 1769480 | tf_op jit(solution)/shard_map/ppermute | solution.py:458
  41.7 1.9 %copy-start.3 = (bf16[512,3072]{1,0:T(8,128)(2,1)S(1)}, bf16[512,3072]{1,0:T(8,128)(2,1)}, u32[]{:S(2)}) copy-start(bf16[512,3072]{1,0:T(8,128)(2,1)} %refs_0_.3) | copy-start | bytes 9437188
  51.1 10.0 %collective-permute-start.12 = (bf16[2,48,3072]{2,1,0:T(8,128)(2,1)S(1)}, bf16[2,48,3072]{2,1,0:T(8,128)(2,1)S(1)}, u32[]{:S(2)}, u32[]{:S(2)}) collective-permute-start(bf16[2,48,3072]{2,1,0:T(8,128)(2,1)S(1)} %get-tuple-element.35), channel_id=1, source_target_pairs={{24,0},{225,1},{26,2},{227,3},{28,4},{229,5},{30,6},{231,7},{0,8},... | collective-permute-start | bytes 1769480 | tf_op jit(solution)/shard_map/ppermute | solution.py:458
  51.1 9.9 %copy-start.2 = (bf16[512,1536]{1,0:T(8,128)(2,1)S(1)}, bf16[512,1536]{1,0:T(8,128)(2,1)}, u32[]{:S(2)}) copy-start(bf16[512,1536]{1,0:T(8,128)(2,1)} %refs_13_.1) | copy-start | bytes 4718596
  51.2 9.9 %collective-permute-start.9 = (bf16[2,48,3072]{2,1,0:T(8,128)(2,1)S(1)}, bf16[2,48,3072]{2,1,0:T(8,128)(2,1)S(1)}, u32[]{:S(2)}, u32[]{:S(2)}) collective-permute-start(bf16[2,48,3072]{2,1,0:T(8,128)(2,1)S(1)} %get-tuple-element.36), channel_id=1, source_target_pairs={{8,0},{33,1},{10,2},{35,3},{12,4},{37,5},{14,6},{39,7},{16,8},{41,... | collective-permute-start | bytes 1769480 | tf_op jit(solution)/shard_map/ppermute | solution.py:458
  58.0 29.2 %collective-permute-start.10 = (bf16[2,48,3072]{2,1,0:T(8,128)(2,1)S(1)}, bf16[2,48,3072]{2,1,0:T(8,128)(2,1)S(1)}, u32[]{:S(2)}, u32[]{:S(2)}) collective-permute-start(bf16[2,48,3072]{2,1,0:T(8,128)(2,1)S(1)} %get-tuple-element.19.refs_3_.refs_0_), channel_id=1, source_target_pairs={{8,0},{33,1},{10,2},{35,3},{12,4},{37,5},{14,6},{39,7},{16,8},{41,... | collective-permute-start | bytes 1769480 | tf_op jit(solution)/shard_map/ppermute | solution.py:458
  58.1 29.1 %collective-permute-start.11 = (bf16[2,48,3072]{2,1,0:T(8,128)(2,1)S(1)}, bf16[2,48,3072]{2,1,0:T(8,128)(2,1)S(1)}, u32[]{:S(2)}, u32[]{:S(2)}) collective-permute-start(bf16[2,48,3072]{2,1,0:T(8,128)(2,1)S(1)} %get-tuple-element.21.refs_1_.refs_5_), channel_id=1, source_target_pairs={{24,0},{225,1},{26,2},{227,3},{28,4},{229,5},{30,6},{231,7},{0,8},... | collective-permute-start | bytes 1769480 | tf_op jit(solution)/shard_map/ppermute | solution.py:458
  75.4 20.1 %collective-permute-start.13 = (bf16[3,512,512]{2,1,0:T(8,128)(2,1)S(1)}, bf16[3,512,512]{2,1,0:T(8,128)(2,1)S(1)}, u32[]{:S(2)}, u32[]{:S(2)}) collective-permute-start(bf16[3,512,512]{2,1,0:T(8,128)(2,1)S(1)} %get-tuple-element.30), channel_id=1, source_target_pairs={{0,1},{1,0},{2,3},{3,2},{4,5},{5,4},{6,7},{7,6},{8,9},{9,8},{10,11... | collective-permute-start | bytes 4718600 | tf_op jit(solution)/shard_map/ppermute | solution.py:503
  95.3 2.4 %collective-permute-start.14 = (bf16[3,512,256]{2,1,0:T(8,128)(2,1)S(1)}, bf16[3,512,256]{2,1,0:T(8,128)(2,1)S(1)}, u32[]{:S(2)}, u32[]{:S(2)}) collective-permute-start(bf16[3,512,256]{2,1,0:T(8,128)(2,1)S(1)} %get-tuple-element.34), channel_id=1, source_target_pairs={{0,1},{1,0},{2,3},{3,2},{4,5},{5,4},{6,7},{7,6},{8,9},{9,8},{10,11... | collective-permute-start | bytes 2359304 | tf_op jit(solution)/shard_map/ppermute | solution.py:503
